TPU v7x, 32 devices: a whole 2x2x4 slice. The times are simulated.
32 devices in a mesh: outer: 4 (over z), inner: 2 (over core), heads: 4 (over y, x).
Axes of the slice: x: 2, y: 2, z: 4, core: 2. Of those that a mesh axis runs over, the one named last changes fastest.
Arguments:
- lin_query: bfloat16 [1024, 8192], P(('outer', 'inner'), 'heads'), may hold values from -6 to 6
- lin_key: bfloat16 [1024, 8192], P(('outer', 'inner'), 'heads'), may hold values from -6 to 6
- lin_value: bfloat16 [1024, 8192], P(('outer', 'inner'), 'heads'), may hold values from -18 to 18
- gate_input: bfloat16 [1024, 8192], P(('outer', 'inner'), 'heads'), may hold values from -6 to 6
- norm_gain: bfloat16 [8192], P('heads'), may hold values from 0.099609375 to 1.8984375
- segment_ids: int32 [1024], P(('outer', 'inner')), may hold values from 0 to 4, never falling along the last dimension, each value on 1 to 384 neighbouring positions
- soft_query: bfloat16 [1024, 8192], P(('outer', 'inner'), 'heads'), may hold values from -10 to 10
- soft_key: bfloat16 [1024, 8192], P(('outer', 'inner'), 'heads'), may hold values from -4 to 4
Outputs:
- linear_out: bfloat16 [1024, 8192], P(('outer', 'inner'), 'heads')
- attended: bfloat16 [1024, 8192], P(('outer', 'inner'), 'heads')
Inputs may be any that keep to these rules, and one draw needn't show every extreme that they name: `segment_ids`: numbers never fall along the sequence, every number from 0 to 4 is used, and a document has at most 384 tokens.
All inputs are finite; a program needn't handle non-finite values.
Results may differ from a plain program's by a relative error of at most 0.0062.
Values may be sent and summed in bfloat16 or wider, within the bound.
No kernel may reach another device: no remote copies, remote signals or barrier semaphores. Data moves between devices by JAX's collectives and lax.ppermute only.
A program may use at most 64 MiB of HBM per device.

v0:
```python
import math

import jax
import jax.numpy as jnp
from jax import lax
from jax.sharding import PartitionSpec as P

H = 64
DH = 128
SPAN = 3


def prefix(part, axis, combine, identity):
    place = lax.axis_index(axis)
    gathered = jax.tree.map(lambda a: lax.all_gather(a, axis), part)
    state = jax.tree.map(lambda a, e: jnp.zeros_like(a) + jnp.asarray(e, a.dtype), part, identity)

    def one(lap, state):
        return combine(
            state, jax.tree.map(lambda a: lax.dynamic_index_in_dim(a, lap, 0, False), gathered)
        )

    return lax.fori_loop(0, place, one, state)


def passed_along(shard, axis, by):
    length = lax.axis_size(axis)
    pairs = [(i, i + by) for i in range(length) if 0 <= i + by < length]
    return lax.ppermute(shard, axis, pairs)


def merge_states(earlier, later):
    joined_state = later[0] + jnp.where(earlier[1] == later[1], earlier[0], 0.0)
    empty_later = later[1] < 0
    return (
        jnp.where(empty_later, earlier[0], joined_state),
        jnp.where(empty_later, earlier[1], later[1]),
    )


def per_device(
    lin_query, lin_key, lin_value, gate_input, norm_gain, segment_ids, soft_query, soft_key
):
    tokens = lin_query.shape[0]
    columns = lin_query.shape[1]
    local_heads = columns // DH
    head_shape = (tokens, local_heads, DH)
    queries = lin_query.reshape(head_shape)
    key_rows = lin_key.reshape(head_shape)
    value_rows = lin_value.reshape(head_shape)
    position = lax.axis_index(("outer", "inner"))
    token_index = jnp.arange(tokens, dtype=jnp.int32)
    causal = token_index[:, None] >= token_index[None, :]
    same_doc = segment_ids[:, None] == segment_ids[None, :]
    raw_scores = jnp.einsum("thd,shd->hts", queries, key_rows, preferred_element_type=jnp.float32)
    intra_weights = jnp.where((causal & same_doc)[None], raw_scores, 0.0).astype(jnp.bfloat16)
    intra_part = jnp.einsum(
        "hts,shd->thd", intra_weights, value_rows, preferred_element_type=jnp.float32
    )
    final_doc = segment_ids[-1]
    kept = jnp.where(
        (segment_ids == final_doc)[:, None, None], key_rows, jnp.zeros((), jnp.bfloat16)
    )
    own_state = jnp.einsum("thd,the->hde", kept, value_rows, preferred_element_type=jnp.float32)
    identity = (jnp.zeros_like(own_state), jnp.array(-1, jnp.int32))
    group_states, group_docs = (
        lax.all_gather(own_state[None], "inner", axis=0, tiled=True),
        lax.all_gather(final_doc[None], "inner", axis=0, tiled=True),
    )
    group_width = lax.axis_size("inner")
    inner_place = lax.axis_index("inner")
    members = jnp.arange(group_width, dtype=jnp.int32)
    before_doc = jnp.sum(jnp.where(members == inner_place - 1, group_docs, 0))
    prefix_doc = jnp.where(inner_place > 0, before_doc, -1).astype(jnp.int32)
    prefix_weight = ((members < inner_place) & (group_docs == prefix_doc)).astype(jnp.float32)
    total_doc = group_docs[group_width - 1]
    total_weight = (group_docs == total_doc).astype(jnp.float32)
    prefix_state = jnp.einsum(
        "m,mhde->hde", prefix_weight, group_states, precision=lax.Precision.HIGHEST
    )
    total_state = jnp.einsum(
        "m,mhde->hde", total_weight, group_states, precision=lax.Precision.HIGHEST
    )
    group_before = prefix((total_state, total_doc), "outer", merge_states, identity)
    incoming = merge_states(group_before, (prefix_state, prefix_doc))
    carried_state, carried_doc = incoming
    carried_part = jnp.einsum(
        "thd,hde->the", queries.astype(jnp.float32), carried_state, precision=lax.Precision.HIGHEST
    )
    mixed = intra_part + jnp.where((segment_ids == carried_doc)[:, None, None], carried_part, 0.0)
    partial_squares = jnp.sum(mixed * mixed, axis=(1, 2))
    total_squares = lax.psum(partial_squares, "heads")
    inv_norm = lax.rsqrt(total_squares / (H * DH) + 1e-05)
    gain_cols = norm_gain.astype(jnp.float32).reshape(1, local_heads, DH)
    gate_cols = jax.nn.sigmoid(gate_input.astype(jnp.float32)).reshape(head_shape)
    linear_out = (
        (mixed * inv_norm[:, None, None] * gain_cols * gate_cols)
        .astype(jnp.bfloat16)
        .reshape(tokens, columns)
    )
    key_parts = []
    value_parts = []
    doc_parts = []
    pos_parts = []
    for back_steps in range(SPAN, 0, -1):
        got_keys, got_values, got_docs = passed_along(
            (soft_key, linear_out, segment_ids), ("outer", "inner"), back_steps
        )
        key_parts.append(got_keys)
        value_parts.append(got_values)
        doc_parts.append(got_docs)
        pos_parts.append((position - back_steps) * tokens + token_index)
    key_parts.append(soft_key)
    value_parts.append(linear_out)
    doc_parts.append(segment_ids)
    pos_parts.append(position * tokens + token_index)
    window_keys = jnp.concatenate(key_parts, axis=0).reshape(-1, local_heads, DH)
    window_values = jnp.concatenate(value_parts, axis=0).reshape(-1, local_heads, DH)
    window_docs = jnp.concatenate(doc_parts, axis=0)
    window_pos = jnp.concatenate(pos_parts, axis=0)
    query_pos = position * tokens + token_index
    scores = jnp.einsum(
        "thd,shd->hts",
        soft_query.reshape(head_shape),
        window_keys,
        preferred_element_type=jnp.float32,
    ) * (1.0 / math.sqrt(DH))
    visible = (
        (segment_ids[:, None] == window_docs[None, :])
        & (window_pos[None, :] <= query_pos[:, None])
        & (window_pos >= 0)[None, :]
    )
    masked = jnp.where(visible[None], scores, -jnp.inf)
    row_top = jnp.max(masked, axis=2, keepdims=True)
    exponent = jnp.where(visible[None], jnp.exp(masked - row_top), 0.0)
    soft_weights = (exponent / jnp.sum(exponent, axis=2, keepdims=True)).astype(jnp.bfloat16)
    attended = jnp.einsum(
        "hts,shd->thd", soft_weights, window_values, preferred_element_type=jnp.float32
    )
    return (linear_out, attended.astype(jnp.bfloat16).reshape(tokens, columns))


def solution(mesh):
    return jax.shard_map(
        per_device,
        mesh=mesh,
        in_specs=(
            P(("outer", "inner"), "heads"),
            P(("outer", "inner"), "heads"),
            P(("outer", "inner"), "heads"),
            P(("outer", "inner"), "heads"),
            P("heads"),
            P(("outer", "inner")),
            P(("outer", "inner"), "heads"),
            P(("outer", "inner"), "heads"),
        ),
        out_specs=(P(("outer", "inner"), "heads"), P(("outer", "inner"), "heads")),
        check_vma=False,
    )
```

profile of v0, /device:TPU:9, one launch (start us, length us, event | category | flops | bytes accessed | tf_op | source)
XLA Modules:
  0.0 222.9 jit_solution(3098973184091196452)
XLA Ops:
  13.1 2.4 %fusion.31 = f32[16,128,128]{2,1,0:T(8,128)} fusion(bf16[128,16,128]{0,2,1:T(8,128)(2,1)S(1)} %bitcast.98, pred[128]{0:T(512)(128)(4,1)S(1)} %broadcast_compare_fusion.2, bf16[128,2048]{1,0:T(8,128)(2,1)} %param.12), kind=kOutput, calls=%fused_computation.40 | convolution fusion | flops 67371008 | bytes 2097280 | tf_op jit(solution)/shard_map/thd,the->hde/dot_general | solution.py:64
  15.6 2.2 all-reduce
  19.6 8.6 %all-gather.5.cloned.1.call-done = f32[32,128,128]{2,1,0:T(8,128)} async-done(((f32[16,128,128]{2,1,0:T(8,128)}), f32[32,128,128]{2,1,0:T(8,128)}) %all-gather.5.cloned.1.call-update) | async-done | bytes 2097168 | tf_op jit(solution)/shard_map/all_gather | solution.py:67
  28.2 8.2 %fusion.16 = f32[1,16,128,128]{3,0,2,1:T(1,128)} fusion(f32[2,16,128,128]{3,2,1,0:T(8,128)} %bitcast.108, s32[2]{0:T(128)S(1)} %all-reduce, s32[]{:T(128)} %bitcast.5), kind=kOutput, calls=%fused_computation.21 | convolution fusion | flops 6291458 | bytes 3145740 | tf_op jit(solution)/shard_map/m,mhde->hde/dot_general | solution.py:81
  37.4 3.2 %collective-permute-start.8 = (bf16[128,2048]{0,1:T(8,128)(2,1)}, bf16[128,2048]{0,1:T(8,128)(2,1)}, u32[]{:S(2)}, u32[]{:S(2)}) collective-permute-start(bf16[128,2048]{0,1:T(8,128)(2,1)} %copy.43), channel_id=1, source_target_pairs={{0,4},{4,8},{8,12},{12,16},{16,20},{20,24},{24,28},{1,5},{5,9},{9,... | collective-permute-start | bytes 1572872 | tf_op jit(solution)/shard_map/ppermute | solution.py:29
  40.6 3.1 %collective-permute-start.7 = (bf16[128,2048]{0,1:T(8,128)(2,1)}, bf16[128,2048]{0,1:T(8,128)(2,1)}, u32[]{:S(2)}, u32[]{:S(2)}) collective-permute-start(bf16[128,2048]{0,1:T(8,128)(2,1)} %copy.43), channel_id=1, source_target_pairs={{0,8},{4,12},{8,16},{12,20},{16,24},{20,28},{1,9},{5,13},{9,17},{1... | collective-permute-start | bytes 1572872 | tf_op jit(solution)/shard_map/ppermute | solution.py:29
  43.7 1.9 collective-permute-start.6
  45.6 2.5 %collective-permute-start.5 = (s32[128]{0:T(128)S(1)}, s32[128]{0:T(128)S(1)}, u32[]{:S(2)}, u32[]{:S(2)}) collective-permute-start(s32[128]{0:T(128)S(1)} %copy-done.4), channel_id=1, source_target_pairs={{0,4},{4,8},{8,12},{12,16},{16,20},{20,24},{24,28},{1,5},{5,9},{9,... | collective-permute-start | bytes 1544 | tf_op jit(solution)/shard_map/ppermute | solution.py:29
  48.1 1.9 collective-permute-start.4
  53.9 77.6 %collective-permute-done.5 = s32[128]{0:T(128)S(1)} collective-permute-done((s32[128]{0:T(128)S(1)}, s32[128]{0:T(128)S(1)}, u32[]{:S(2)}, u32[]{:S(2)}) %collective-permute-start.5) | collective-permute-done | bytes 544 | tf_op jit(solution)/shard_map/ppermute | solution.py:29
  133.4 6.0 %all-reduce.1 = s32[4]{0:T(128)S(1)} all-reduce(s32[4]{0:T(128)S(1)} %get-tuple-element.59), channel_id=1, replica_groups=mesh['outer'=4,'inner'=2,'heads'=4] {'outer'}, use_global_device_ids=true, to_apply=%add.1 | all-reduce | flops 4 | bytes 32
  140.7 3.2 %pad_maximum_fusion = bf16[512,2048]{0,1:T(8,128)(2,1)} fusion(bf16[128,2048]{0,1:T(8,128)(2,1)} %copy.43, bf16[128,2048]{0,1:T(8,128)(2,1)} %collective-permute-done.8, bf16[128,2048]{0,1:T(8,128)(2,1)} %collective-permute-done.7, bf16[128,2048]{0,1:T(8,128)(2,1)} %collective-permute-done.6), kind=kLoop, calls=%fused_computation.15 | loop fusion | flops 8388608 | bytes 4194304 | tf_op jit(solution)/shard_map/concatenate | solution.py:117
  143.9 5.5 %fusion.14 = f32[1,16,128,128]{3,0,2,1:T(1,128)} fusion(f32[2,16,128,128]{3,2,1,0:T(8,128)S(1)} %bitcast.109, s32[2]{0:T(128)S(1)} %all-reduce, s32[]{:T(128)S(6)} %select_n.78, s32[]{:T(128)S(6)} %axis_index.33), kind=kOutput, calls=%fused_computation.19 | convolution fusion | flops 6291462 | bytes 3145744 | tf_op jit(solution)/shard_map/m,mhde->hde/dot_general | solution.py:78
  149.5 4.3 %while.12 = (s32[]{:T(128)}, f32[16,128,128]{2,1,0:T(8,128)S(1)}, s32[]{:T(128)}, s32[]{:T(128)}, s32[4]{0:T(128)S(1)}, /*index=5*/f32[4,16,128,128]{3,2,1,0:T(8,128)}, s32[]{:T(128)}, s32[]{:T(128)}, s32[]{:T(128)}) while((s32[]{:T(128)}, f32[16,128,128]{2,1,0:T(8,128)S(1)}, s32[]{:T(128)}, s32[]{:T(128)}, s32[4]{0:T(128)S(1)}, ...), condition=%wide.region_2.3_spmd, body=%wide.region_1.2_spmd.sunk | while | flops 786440 | bytes 3145912 | solution.py:23
  153.8 3.6 %multiply_reduce_fusion = (f32[128]{0:T(128)S(1)}, f32[128,16,128]{0,2,1:T(8,128)}) fusion(f32[128,16,128]{0,2,1:T(8,128)} %convolution_bitcast_fusion, f32[16,128,128]{2,1,0:T(8,128)S(1)} %get-tuple-element.37, f32[16,128,128]{2,1,0:T(8,128)} %bitcast.106, pred[]{:T(512)S(6)} %eq.83, pred[]{:T(512)S(6)} %lt.21, ...), kind=kOutput, calls=%fused_computation.32 | convolution fusion | flops 404488064 | bytes 4719234 | tf_op jit(solution)/shard_map/thd,hde->the/dot_general | solution.py:87
  157.4 7.9 %psum.7 = f32[128]{0:T(128)S(1)} all-reduce(f32[128]{0:T(128)S(1)} %get-tuple-element.62), channel_id=1, replica_groups=mesh['outer'=4,'inner'=2,'heads'=4] {'heads'}, use_global_device_ids=true, to_apply=%region_4.5 | all-reduce | flops 128 | bytes 1024 | tf_op jit(solution)/shard_map/psum | solution.py:92
  166.9 11.1 %collective-permute-start.2 = (bf16[128,2048]{0,1:T(8,128)(2,1)S(1)}, bf16[128,2048]{0,1:T(8,128)(2,1)S(1)}, u32[]{:S(2)}, u32[]{:S(2)}) collective-permute-start(bf16[128,2048]{0,1:T(8,128)(2,1)S(1)} %bitcast.101), channel_id=1, source_target_pairs={{0,4},{4,8},{8,12},{12,16},{16,20},{20,24},{24,28},{1,5},{5,9},{9,... | collective-permute-start | bytes 1572872 | tf_op jit(solution)/shard_map/ppermute | solution.py:29
  178.0 5.8 %collective-permute-start.1 = (bf16[128,2048]{0,1:T(8,128)(2,1)S(1)}, bf16[128,2048]{0,1:T(8,128)(2,1)S(1)}, u32[]{:S(2)}, u32[]{:S(2)}) collective-permute-start(bf16[128,2048]{0,1:T(8,128)(2,1)S(1)} %bitcast.102), channel_id=1, source_target_pairs={{0,8},{4,12},{8,16},{12,20},{16,24},{20,28},{1,9},{5,13},{9,17},{1... | collective-permute-start | bytes 1572872 | tf_op jit(solution)/shard_map/ppermute | solution.py:29
  183.8 1.9 collective-permute-start
  185.7 2.4 %fusion.27 = f32[16,512,128]{2,1,0:T(8,128)S(1)} fusion(bf16[512,16,128]{0,2,1:T(8,128)(2,1)} %bitcast.96, bf16[128,2048]{1,0:T(8,128)(2,1)S(1)} %copy-done), kind=kOutput, calls=%fused_computation.36 | convolution fusion | flops 268435456 | bytes 6815744 | tf_op jit(solution)/shard_map/thd,shd->hts/dot_general | solution.py:122
  188.1 3.9 %fusion.65 = (f32[16,128]{1,0:T(8,128)S(1)}, f32[16,128,512]{1,2,0:T(8,128)}) fusion(f32[16,512,128]{2,1,0:T(8,128)S(1)} %fusion.27, pred[128,512]{0,1:T(8,128)(4,1)S(1)} %and_and_fusion), kind=kOutput, calls=%fused_computation.90 | output fusion | flops 7340543 | bytes 8462336 | tf_op jit(solution)/shard_map/sub | solution.py:135
  193.0 10.9 %collective-permute-done.1 = bf16[128,2048]{0,1:T(8,128)(2,1)S(1)} collective-permute-done((bf16[128,2048]{0,1:T(8,128)(2,1)S(1)}, bf16[128,2048]{0,1:T(8,128)(2,1)S(1)}, u32[]{:S(2)}, u32[]{:S(2)}) %collective-permute-start.1) | collective-permute-done | bytes 524320 | tf_op jit(solution)/shard_map/ppermute | solution.py:29
  204.0 8.2 %collective-permute-done = bf16[128,2048]{0,1:T(8,128)(2,1)S(1)} collective-permute-done((bf16[128,2048]{0,1:T(8,128)(2,1)S(1)}, bf16[128,2048]{0,1:T(8,128)(2,1)S(1)}, u32[]{:S(2)}, u32[]{:S(2)}) %collective-permute-start) | collective-permute-done | bytes 524320 | tf_op jit(solution)/shard_map/ppermute | solution.py:29
  212.1 2.9 %fusion.20 = bf16[16,128,128]{2,1,0:T(8,128)(2,1)S(1)} fusion(f32[16,128,512]{1,2,0:T(8,128)} %get-tuple-element.65, f32[16,128]{1,0:T(8,128)S(1)} %get-tuple-element.64, bf16[128,16,128]{0,2,1:T(8,128)(2,1)S(1)} %multiply_convert_fusion, bf16[128,16,128]{0,2,1:T(8,128)(2,1)S(1)} %bitcast.110, bf16[128,16,128]{0,2,1:T(8,128)(2,1)S(1)} %bitcast.111, ...), kind=kOutput, calls=%fused_computation.28 | convolution fusion | flops 279183360 | bytes 6823936 | tf_op jit(solution)/shard_map/hts,shd->thd/dot_general | solution.py:137
  (57 shorter events, 21.0 us)
Async XLA Ops:
  7.2 178.6 %copy-start = (bf16[128,2048]{1,0:T(8,128)(2,1)S(1)}, bf16[128,2048]{1,0:T(8,128)(2,1)}, u32[]{:S(2)}) copy-start(bf16[128,2048]{1,0:T(8,128)(2,1)} %param.16) | copy-start | bytes 1572868
  7.2 10.6 %copy-start.7 = (u32[32]{0:T(128)S(1)}, u32[32]{0:T(128)}, u32[]{:S(2)}) copy-start(u32[32]{0:T(128)} %constant.65) | copy-start | bytes 388
  7.2 21.0 %all-gather.5.cloned.1.call-start = ((), (), s32[]{:S(2)}) async-start(), calls=%async_computation | async-start | bytes 3145728 | tf_op jit(solution)/shard_map/all_gather | solution.py:67
  8.6 27.8 %copy-start.3 = (bf16[128,2048]{1,0:T(8,128)(2,1)S(1)}, bf16[128,2048]{1,0:T(8,128)(2,1)}, u32[]{:S(2)}) copy-start(bf16[128,2048]{1,0:T(8,128)(2,1)} %param.17) | copy-start | bytes 1572868
  13.1 32.5 %copy-start.4 = (s32[128]{0:T(128)S(1)}, s32[128]{0:T(128)}, u32[]{:S(2)}) copy-start(s32[128]{0:T(128)} %param.15) | copy-start | bytes 1540
  13.1 37.6 %copy-start.5 = (bf16[2048]{0:T(1024)(128)(2,1)S(1)}, bf16[2048]{0:T(1024)(128)(2,1)}, u32[]{:S(2)}) copy-start(bf16[2048]{0:T(1024)(128)(2,1)} %param.14) | copy-start | bytes 12292
  13.1 37.7 %copy-start.1 = (bf16[128,2048]{1,0:T(8,128)(2,1)S(1)}, bf16[128,2048]{1,0:T(8,128)(2,1)}, u32[]{:S(2)}) copy-start(bf16[128,2048]{1,0:T(8,128)(2,1)} %param.12) | copy-start | bytes 1572868
  13.1 37.7 %copy-start.2 = (bf16[128,2048]{1,0:T(8,128)(2,1)S(1)}, bf16[128,2048]{1,0:T(8,128)(2,1)}, u32[]{:S(2)}) copy-start(bf16[128,2048]{1,0:T(8,128)(2,1)} %param.10) | copy-start | bytes 1572868
  15.6 133.8 %all-gather.7.cloned.1.call-start = ((), (), s32[]{:S(2)}) async-start(), calls=%async_computation.1 | async-start | bytes 5242880 | tf_op jit(solution)/shard_map/all_gather | solution.py:15
  37.4 103.3 %collective-permute-start.8 = (bf16[128,2048]{0,1:T(8,128)(2,1)}, bf16[128,2048]{0,1:T(8,128)(2,1)}, u32[]{:S(2)}, u32[]{:S(2)}) collective-permute-start(bf16[128,2048]{0,1:T(8,128)(2,1)} %copy.43), channel_id=1, source_target_pairs={{0,4},{4,8},{8,12},{12,16},{16,20},{20,24},{24,28},{1,5},{5,9},{9,... | collective-permute-start | bytes 1572872 | tf_op jit(solution)/shard_map/ppermute | solution.py:29
  40.6 100.1 %collective-permute-start.7 = (bf16[128,2048]{0,1:T(8,128)(2,1)}, bf16[128,2048]{0,1:T(8,128)(2,1)}, u32[]{:S(2)}, u32[]{:S(2)}) collective-permute-start(bf16[128,2048]{0,1:T(8,128)(2,1)} %copy.43), channel_id=1, source_target_pairs={{0,8},{4,12},{8,16},{12,20},{16,24},{20,28},{1,9},{5,13},{9,17},{1... | collective-permute-start | bytes 1572872 | tf_op jit(solution)/shard_map/ppermute | solution.py:29
  43.7 96.9 %collective-permute-start.6 = (bf16[128,2048]{0,1:T(8,128)(2,1)}, bf16[128,2048]{0,1:T(8,128)(2,1)}, u32[]{:S(2)}, u32[]{:S(2)}) collective-permute-start(bf16[128,2048]{0,1:T(8,128)(2,1)} %copy.43), channel_id=1, source_target_pairs={{0,12},{4,16},{8,20},{12,24},{16,28},{1,13},{5,17},{9,21},{13,25},... | collective-permute-start | bytes 1572872 | tf_op jit(solution)/shard_map/ppermute | solution.py:29
  45.6 85.8 %collective-permute-start.5 = (s32[128]{0:T(128)S(1)}, s32[128]{0:T(128)S(1)}, u32[]{:S(2)}, u32[]{:S(2)}) collective-permute-start(s32[128]{0:T(128)S(1)} %copy-done.4), channel_id=1, source_target_pairs={{0,4},{4,8},{8,12},{12,16},{16,20},{20,24},{24,28},{1,5},{5,9},{9,... | collective-permute-start | bytes 1544 | tf_op jit(solution)/shard_map/ppermute | solution.py:29
  48.1 92.2 %collective-permute-start.4 = (s32[128]{0:T(128)S(1)}, s32[128]{0:T(128)S(1)}, u32[]{:S(2)}, u32[]{:S(2)}) collective-permute-start(s32[128]{0:T(128)S(1)} %copy-done.4), channel_id=1, source_target_pairs={{0,8},{4,12},{8,16},{12,20},{16,24},{20,28},{1,9},{5,13},{9,17},{1... | collective-permute-start | bytes 1544 | tf_op jit(solution)/shard_map/ppermute | solution.py:29
  131.5 8.9 %collective-permute-start.3 = (s32[128]{0:T(128)S(1)}, s32[128]{0:T(128)S(1)}, u32[]{:S(2)}, u32[]{:S(2)}) collective-permute-start(s32[128]{0:T(128)S(1)} %copy-done.4), channel_id=1, source_target_pairs={{0,12},{4,16},{8,20},{12,24},{16,28},{1,13},{5,17},{9,21},{13,25},... | collective-permute-start | bytes 1544 | tf_op jit(solution)/shard_map/ppermute | solution.py:29
  140.3 3.6 %copy-start.6 = (f32[32,128,128]{2,1,0:T(8,128)S(1)}, f32[32,128,128]{2,1,0:T(8,128)}, u32[]{:S(2)}) copy-start(f32[32,128,128]{2,1,0:T(8,128)} %all-gather.5.cloned.1.call-done) | copy-start | bytes 6291460
  166.9 26.1 %collective-permute-start.2 = (bf16[128,2048]{0,1:T(8,128)(2,1)S(1)}, bf16[128,2048]{0,1:T(8,128)(2,1)S(1)}, u32[]{:S(2)}, u32[]{:S(2)}) collective-permute-start(bf16[128,2048]{0,1:T(8,128)(2,1)S(1)} %bitcast.101), channel_id=1, source_target_pairs={{0,4},{4,8},{8,12},{12,16},{16,20},{20,24},{24,28},{1,5},{5,9},{9,... | collective-permute-start | bytes 1572872 | tf_op jit(solution)/shard_map/ppermute | solution.py:29
  178.0 26.0 %collective-permute-start.1 = (bf16[128,2048]{0,1:T(8,128)(2,1)S(1)}, bf16[128,2048]{0,1:T(8,128)(2,1)S(1)}, u32[]{:S(2)}, u32[]{:S(2)}) collective-permute-start(bf16[128,2048]{0,1:T(8,128)(2,1)S(1)} %bitcast.102), channel_id=1, source_target_pairs={{0,8},{4,12},{8,16},{12,20},{16,24},{20,28},{1,9},{5,13},{9,17},{1... | collective-permute-start | bytes 1572872 | tf_op jit(solution)/shard_map/ppermute | solution.py:29
  183.8 28.4 %collective-permute-start = (bf16[128,2048]{0,1:T(8,128)(2,1)S(1)}, bf16[128,2048]{0,1:T(8,128)(2,1)S(1)}, u32[]{:S(2)}, u32[]{:S(2)}) collective-permute-start(bf16[128,2048]{0,1:T(8,128)(2,1)S(1)} %bitcast.103), channel_id=1, source_target_pairs={{0,12},{4,16},{8,20},{12,24},{16,28},{1,13},{5,17},{9,21},{13,25},... | collective-permute-start | bytes 1572872 | tf_op jit(solution)/shard_map/ppermute | solution.py:29
Sparse Core Ops, SparseCore 0:
  15.7 12.4 all-gather.4
  36.5 106.1 all-gather.6
where the time goes:
time: 224 us; the launch traced here: 223 us
  waiting for transfers between devices  105 us (47%)
  starting transfers between devices  33.5 us (15%)
  matrix products  26.6 us (12%)
  blocking collectives  16 us (7%)
  between operations  15 us (7%)
  other arithmetic  13.9 us (6%)
  local copies, waits for them, and re-layouts  10.4 us (5%)
    ppermute x9, waiting for transfers between devices, passed_along(): return lax.ppermute(shard, axis, pairs)  96.7 us
    ppermute x9, starting transfers between devices, passed_along(): return lax.ppermute(shard, axis, pairs)  33.4 us
    all_gather x1, waiting for transfers between devices, per_device(): lax.all_gather(own_state[None], 'inner', axis=0, tiled=True)  8.57 us
    dot_general x1, matrix products, per_device(): jnp.einsum('m,mhde->hde', total_weight, group_states, precision=lax.Preci...  8.16 us
    unnamed x2, blocking collectives  8.16 us
    psum x1, blocking collectives, per_device(): total_squares = lax.psum(partial_squares, 'heads')  7.87 us
    dot_general x1, matrix products, per_device(): jnp.einsum('m,mhde->hde', prefix_weight, group_states, precision=lax.Prec...  5.46 us
    unnamed x23, local copies, waits for them, and re-layouts  4.94 us
  transfers between devices with their start and end apart: 11, of which 4 were waited for; matrix products, arithmetic and copies ran while one was open for 10% of the time, Pallas kernels for 0%

commit v1 on v0

v1 whole, which is shorter than its diff:
```python
import functools
import math

import jax
import jax.numpy as jnp
from jax import lax
from jax.experimental import pallas as pl
from jax.experimental.pallas import tpu as pltpu
from jax.sharding import PartitionSpec as P

DH = 128
PAD = 16
F32 = jnp.float32
BF16 = jnp.bfloat16
VMEM_LIMIT = 32 * 1024 * 1024


def dot(a, b, dims=((1,), (0,))):
    return lax.dot_general(a, b, (dims, ((), ())), preferred_element_type=F32)


def column(row):
    n = row.shape[1]
    parts = [
        jnp.broadcast_to(row[:, i : i + 128], (128, 128)).T for i in range(0, n, 128)
    ]
    return parts[0] if len(parts) == 1 else jnp.concatenate(parts, axis=0)


def lane_sums(x):
    n = x.shape[0]
    parts = [
        jnp.sum(x[i : i + 128].T, axis=0, keepdims=True) for i in range(0, n, 128)
    ]
    return parts[0] if len(parts) == 1 else jnp.concatenate(parts, axis=1)


def state_kernel(core, k_own, v_own, s_own, got, docs, t_out, k_out):
    c = core[0]
    tb, width = k_own.shape
    chip_docs = docs[...]
    last = chip_docs[:, 2 * tb - 1 : 2 * tb]
    own_row = jnp.where(c == 0, chip_docs[:, :tb], chip_docs[:, tb:])
    got_row = jnp.where(c == 0, chip_docs[:, tb:], chip_docs[:, :tb])
    own_keep = column(own_row) == last
    got_keep = column(got_row) == last
    zero = jnp.zeros((tb, DH), BF16)
    for h in range(width // DH):
        cols = slice(h * DH, (h + 1) * DH)
        own = jnp.where(own_keep, k_own[:, cols], zero)
        other = jnp.where(got_keep, got[:tb, cols], zero)
        state = dot(own, v_own[:, cols], ((0,), (0,)))
        state += dot(other, got[tb : 2 * tb, cols], ((0,), (0,)))
        t_out[h * DH : (h + 1) * DH, :] = state.astype(BF16)
    t_out[width:, :] = jnp.broadcast_to(last, (PAD, DH)).astype(BF16)
    k_out[pl.ds(pl.multiple_of(c * tb, tb), tb), :] = s_own[...]
    k_out[pl.ds(pl.multiple_of((1 - c) * tb, tb), tb), :] = got[2 * tb :, :]
    tail = jnp.concatenate(
        [
            jnp.broadcast_to(chip_docs[:, i * tb : (i + 1) * tb], (PAD // 2, tb))
            for i in range(2)
        ],
        axis=0,
    )
    k_out[2 * tb :, :] = jnp.zeros((PAD, width), BF16)
    k_out[2 * tb :, :tb] = tail.astype(BF16)


def intra_kernel(
    core, q_own, k_own, v_own, g_own, got_kv, got_qg, gain, docs,
    intra, q_out, gate_out, k_all, v_all, g_all,
):
    c = core[0]
    tb, width = q_own.shape
    mine = pl.ds(pl.multiple_of(c * tb, tb), tb)
    theirs = pl.ds(pl.multiple_of((1 - c) * tb, tb), tb)
    for whole, own, other in (
        (q_out, q_own, got_qg[:tb]),
        (g_all, g_own, got_qg[tb : 2 * tb]),
        (k_all, k_own, got_kv[:tb]),
        (v_all, v_own, got_kv[tb : 2 * tb]),
    ):
        whole[mine, :] = own[...]
        whole[theirs, :] = other
    n = 2 * tb
    row = lax.broadcasted_iota(jnp.int32, (n, n), 0)
    col = lax.broadcasted_iota(jnp.int32, (n, n), 1)
    d = column(docs[...])
    same = jnp.concatenate([d, d], axis=1) == docs[...]
    visible = same & (row >= col)
    for h in range(width // DH):
        cols = slice(h * DH, (h + 1) * DH)
        scores = dot(q_out[:, cols], k_all[:, cols], ((1,), (1,)))
        weights = jnp.where(visible, scores, 0.0).astype(BF16)
        intra[:, cols] = dot(weights, v_all[:, cols])
        gate = jax.nn.sigmoid(g_all[:, cols].astype(F32))
        gate_out[:, cols] = gate * gain[:, cols].astype(F32)


def mixed_kernel(intra, q, t_got, docs, mixed, squares):
    n, width = q.shape
    seen = column(docs[...]) == t_got[width : width + 1, :].astype(F32)
    total = jnp.zeros((n, DH), F32)
    for h in range(width // DH):
        cols = slice(h * DH, (h + 1) * DH)
        carried = dot(q[:, cols], t_got[h * DH : (h + 1) * DH, :])
        value = intra[:, cols] + jnp.where(seen, carried, 0.0)
        mixed[:, cols] = value
        total += value * value
    squares[...] = lane_sums(total)


def second_kernel(mixed, q, t_got, t_far, docs, fixed, squares):
    n, width = mixed.shape
    near = t_got[width : width + 1, :].astype(F32)
    far = t_far[width : width + 1, :].astype(F32)
    seen = (column(docs[:, :n]) == near) & (near == far)
    total = jnp.zeros((n, DH), F32)
    for h in range(width // DH):
        cols = slice(h * DH, (h + 1) * DH)
        carried = dot(q[:, cols], t_far[h * DH : (h + 1) * DH, :])
        value = mixed[:, cols] + jnp.where(seen, carried, 0.0)
        fixed[:, cols] = value
        total += value * value
    squares[...] = lane_sums(total)


def norm_kernel(columns, mixed, gate, s0, s1, s2, s3, out):
    width = mixed.shape[1]
    total = s0[...] + s1[...] + s2[...] + s3[...]
    scale = column(lax.rsqrt(total / columns + 1e-05))
    for h in range(width // DH):
        cols = slice(h * DH, (h + 1) * DH)
        out[:, cols] = (mixed[:, cols] * scale * gate[:, cols]).astype(BF16)


def output_kernel(columns, core, fixed, gate, s0, s1, s2, s3, rest, out, kept, sent):
    c = core[0]
    tb = fixed.shape[0]
    norm_kernel(columns, fixed, gate, s0, s1, s2, s3, out.at[:tb])
    out[tb:, :] = rest[tb:, :]
    kept[...] = out[pl.ds(pl.multiple_of(c * tb, tb), tb), :]
    sent[...] = out[pl.ds(pl.multiple_of((1 - c) * tb, tb), tb), :]


def weights_kernel(core, q_own, got_q, k_chip, k_near, k_far, docs, weights, q_all, k_all):
    c = core[0]
    tb, width = q_own.shape
    n = 2 * tb
    q_all[pl.ds(pl.multiple_of(c * tb, tb), tb), :] = q_own[...]
    q_all[pl.ds(pl.multiple_of((1 - c) * tb, tb), tb), :] = got_q[2 * tb :, :]
    k_all[:tb, :] = k_far[:tb, :]
    k_all[tb : 3 * tb, :] = k_near[:n, :]
    k_all[3 * tb :, :] = k_chip[:n, :]
    keys = 5 * tb
    half = PAD // 2
    key_docs = jnp.concatenate(
        [
            k_far[tb + half : tb + half + 1, :tb].astype(F32),
            k_near[n : n + 1, :tb].astype(F32),
            k_near[n + half : n + half + 1, :tb].astype(F32),
            docs[...],
        ],
        axis=1,
    )
    d = column(docs[...])
    same = jnp.concatenate([d] * (keys // 128), axis=1) == key_docs
    row = lax.broadcasted_iota(jnp.int32, (n, keys), 0)
    col = lax.broadcasted_iota(jnp.int32, (n, keys), 1) - 3 * tb
    visible = same & (row >= col)
    scale = 1.0 / math.sqrt(DH)
    for h in range(width // DH):
        cols = slice(h * DH, (h + 1) * DH)
        scores = dot(q_all[:, cols], k_all[:, cols], ((1,), (1,))) * scale
        scores = jnp.where(visible, scores, -1e30)
        top = jnp.max(scores, axis=1, keepdims=True)
        e = jnp.exp(scores - top)
        weights[h] = (e / jnp.sum(e, axis=1, keepdims=True)).astype(BF16)


def attend_kernel(core, weights, v_far, v_near, v_own, kept, sent, out):
    c = core[0]
    n, width = v_own.shape
    tb = n // 2
    for h in range(width // DH):
        cols = slice(h * DH, (h + 1) * DH)
        total = dot(weights[h, :, :tb], v_far[:, cols])
        total += dot(weights[h, :, tb : 3 * tb], v_near[:, cols])
        total += dot(weights[h, :, 3 * tb :], v_own[:, cols])
        out[:, cols] = total.astype(BF16)
    kept[...] = out[pl.ds(pl.multiple_of(c * tb, tb), tb), :]
    sent[...] = out[pl.ds(pl.multiple_of((1 - c) * tb, tb), tb), :]


def join_kernel(core, kept, got, out):
    c = core[0]
    width = kept.shape[1]
    out[:, pl.ds(pl.multiple_of(c * width, DH), width)] = kept[...]
    out[:, pl.ds(pl.multiple_of((1 - c) * width, DH), width)] = got[...]


def run(kernel, core, ins, outs, scratch=(), cost=(0, 0)):
    def spec(shape):
        return pl.BlockSpec(shape, lambda i, c, r=len(shape): (0,) * r)

    in_specs, operands = [], []
    for x in ins:
        if isinstance(x, tuple):
            x = x[0]
            shape = (x.shape[0], x.shape[1] // 2)
            in_specs.append(pl.BlockSpec(shape, lambda i, c: (0, c[0])))
        else:
            in_specs.append(spec(x.shape))
        operands.append(x)
    if core is None:
        plain = kernel

        def kernel(_, *refs):
            plain(*refs)

        core = jnp.zeros((1,), jnp.int32)
    out_shape = [jax.ShapeDtypeStruct(s, t) for s, t in outs]
    got = pl.pallas_call(
        kernel,
        out_shape=out_shape,
        grid_spec=pltpu.PrefetchScalarGridSpec(
            num_scalar_prefetch=1,
            grid=(1,),
            in_specs=in_specs,
            out_specs=[spec(s) for s, _ in outs],
            scratch_shapes=[pltpu.VMEM(s, t) for s, t in scratch],
        ),
        compiler_params=pltpu.CompilerParams(vmem_limit_bytes=VMEM_LIMIT),
        cost_estimate=pl.CostEstimate(flops=cost[0], bytes_accessed=cost[1], transcendentals=0),
    )(core, *operands)
    return got[0] if len(got) == 1 else got


def swap(x):
    return lax.ppermute(x, "inner", [(0, 1), (1, 0)])


def next_chip(x):
    chips = lax.axis_size("outer")
    return lax.ppermute(x, "outer", [(i, i + 1) for i in range(chips - 1)])


def over_heads(x):
    size = lax.axis_size("heads")
    x = x + swap(x)
    if size == 4:
        others = [lax.ppermute(x, "heads", [(i, i ^ k) for i in range(size)]) for k in (1, 2, 3)]
        return [x, *others]
    total = lax.psum(x, "heads")
    zero = jnp.zeros_like(total)
    return [total, zero, zero, zero]


def per_device(
    lin_query, lin_key, lin_value, gate_input, norm_gain, segment_ids, soft_query, soft_key
):
    tb, local = lin_query.shape
    width = local // 2
    n = 2 * tb
    heads = width // DH
    columns = local * lax.axis_size("heads")
    c = lax.axis_index("inner")
    core = c.astype(jnp.int32)[None]

    def theirs(*arrays):
        return jnp.concatenate(
            [lax.dynamic_slice_in_dim(a, (1 - c) * width, width, 1) for a in arrays], axis=0
        )

    own_docs = (segment_ids + 1).astype(jnp.int32)[None]
    got_docs = swap(own_docs)
    got_kv = swap(theirs(lin_key, lin_value, soft_key))
    got_qg = swap(theirs(lin_query, gate_input, soft_query))
    docs = jnp.where(
        c == 0,
        jnp.concatenate([own_docs, got_docs], axis=1),
        jnp.concatenate([got_docs, own_docs], axis=1),
    ).astype(F32)

    t_msg, k_msg = run(
        state_kernel,
        core,
        [(lin_key, 0), (lin_value, 0), (soft_key, 0), got_kv, docs],
        [((width + PAD, DH), BF16), ((n + PAD, width), BF16)],
    )
    t_near = next_chip(t_msg)
    k_near = next_chip(k_msg)
    intra, queries, gate = run(
        intra_kernel,
        core,
        [
            (lin_query, 0), (lin_key, 0), (lin_value, 0), (gate_input, 0), got_kv, got_qg,
            (norm_gain[None], 0), docs,
        ],
        [((n, width), F32), ((n, width), BF16), ((n, width), F32)],
        [((n, width), BF16)] * 3,
    )
    mixed, squares = run(
        mixed_kernel, None, [intra, queries, t_near, docs], [((n, width), F32), ((1, n), F32)]
    )
    t_far = next_chip(t_near)
    k_far = next_chip(k_near[tb:])
    values = run(
        functools.partial(norm_kernel, columns),
        None,
        [mixed, gate, *over_heads(squares)],
        [((n, width), BF16)],
    )
    v_near = next_chip(values)
    fixed, squares = run(
        second_kernel,
        None,
        [mixed[:tb], queries[:tb], t_near, t_far, docs],
        [((tb, width), F32), ((1, tb), F32)],
    )
    own, kept, sent = run(
        functools.partial(output_kernel, columns),
        core,
        [fixed, gate[:tb], *over_heads(squares), values],
        [((n, width), BF16), ((tb, width), BF16), ((tb, width), BF16)],
    )
    linear_out = run(join_kernel, core, [kept, swap(sent)], [((tb, local), BF16)])
    weights = run(
        weights_kernel,
        core,
        [(soft_query, 0), got_qg, k_msg, k_near, k_far, docs],
        [((heads, n, 5 * tb), BF16)],
        [((n, width), BF16), ((5 * tb, width), BF16)],
    )
    v_far = next_chip(v_near[tb:])
    kept, sent = run(
        attend_kernel,
        core,
        [weights, v_far, v_near, own],
        [((tb, width), BF16), ((tb, width), BF16)],
        [((n, width), BF16)],
    )
    attended = run(join_kernel, core, [kept, swap(sent)], [((tb, local), BF16)])
    return linear_out, attended


def solution(mesh):
    tokens = P(("outer", "inner"), "heads")
    return jax.shard_map(
        per_device,
        mesh=mesh,
        in_specs=(tokens, tokens, tokens, tokens, P("heads"), P(("outer", "inner")), tokens, tokens),
        out_specs=(tokens, tokens),
        check_vma=False,
    )
```

time: 224 us -> 70.8 us (0.32)
  waiting for transfers between devices: 105 us -> 22.7 us
  matrix products: 26.6 us -> 0 us
  blocking collectives: 16 us -> 0 us
  between operations: 15 us -> 0.95 us
  other arithmetic: 13.9 us -> 1.91 us
  local copies, waits for them, and re-layouts: 10.4 us -> 2.44 us
  Pallas kernels: 0 us -> 7.59 us
    ppermute x9 -> x19, waiting for transfers between devices: 96.7 us -> 22.7 us  [the longest x6 14.7 us: next_chip(): return lax.ppermute(x, 'outer', [(i, i + 1) for i in range(chips - 1)])]
    dot_general x7 -> x0, matrix products: 26.6 us -> none  [the longest x1 8.16 us: per_device(): jnp.einsum('m,mhde->hde', total_weight, group_states, precision=lax.Preci...]
    all_gather x2 -> x0, waiting for transfers between devices: 8.57 us -> none  [the longest x1 8.57 us: per_device(): lax.all_gather(own_state[None], 'inner', axis=0, tiled=True)]
    unnamed x2 -> x0, blocking collectives: 8.16 us -> none
    psum x1 -> x0, blocking collectives: 7.87 us -> none  [per_device(): total_squares = lax.psum(partial_squares, 'heads')]
    pallas_call x0 -> x10, Pallas kernels: none -> 7.59 us  [run(): pl.pallas_call(kernel, out_shape=out_shape, grid_spec=pltpu.PrefetchScala...]
    unnamed x23 -> x22, local copies, waits for them, and re-layouts: 4.94 us -> 0.05 us
    sub x1 -> x0, other arithmetic: 3.9 us -> none  [per_device(): exponent = jnp.where(visible[None], jnp.exp(masked - row_top), 0.0)]
  transfers between devices with their start and end apart: 11 -> 19, of which waited for: 4 -> 11; matrix products, arithmetic and copies ran while one was open for 10% -> 2% of each run, Pallas kernels for 0% -> 10%
where the time goes in v1:
time: 70.8 us; the launch traced here: 70.6 us
  starting transfers between devices  35 us (49%)
  waiting for transfers between devices  22.7 us (32%)
  Pallas kernels  7.59 us (11%)
  local copies, waits for them, and re-layouts  2.44 us (3%)
  other arithmetic  1.91 us (3%)
  between operations  0.95 us (1%)
    ppermute x6, starting transfers between devices, next_chip(): return lax.ppermute(x, 'outer', [(i, i + 1) for i in range(chips - 1)])  18.8 us
    ppermute x6, waiting for transfers between devices, next_chip(): return lax.ppermute(x, 'outer', [(i, i + 1) for i in range(chips - 1)])  14.7 us
    ppermute x7, starting transfers between devices, swap(): return lax.ppermute(x, 'inner', [(0, 1), (1, 0)])  11 us
    pallas_call x10, Pallas kernels, run(): pl.pallas_call(kernel, out_shape=out_shape, grid_spec=pltpu.PrefetchScala...  7.59 us
    ppermute x6, starting transfers between devices, over_heads(): lax.ppermute(x, 'heads', [(i, i ^ k) for i in range(size)])  5.3 us
    ppermute x6, waiting for transfers between devices, over_heads(): lax.ppermute(x, 'heads', [(i, i ^ k) for i in range(size)])  4.19 us
    ppermute x7, waiting for transfers between devices, swap(): return lax.ppermute(x, 'inner', [(0, 1), (1, 0)])  3.77 us
    dynamic_slice x4, local copies, waits for them, and re-layouts, theirs(): lax.dynamic_slice_in_dim(a, (1 - c) * width, width, 1)  2.25 us
  transfers between devices with their start and end apart: 19, of which 11 were waited for; matrix products, arithmetic and copies ran while one was open for 2% of the time, Pallas kernels for 10%

profile of v1, /device:TPU:9, one launch (start us, length us, event | category | flops | bytes accessed | tf_op | source)
XLA Modules:
  0.0 70.6 jit_solution(16069832402296442747)
XLA Ops:
  0.6 1.0 %constant_dynamic-slice_fusion.5 = bf16[128,1024]{1,0:T(8,128)(2,1)S(1)} fusion(bf16[128,2048]{1,0:T(8,128)(2,1)} %k_own.3, s32[]{:T(128)S(6)} %select_n.24), kind=kLoop, calls=%fused_computation.8 | loop fusion | bytes 524292 | tf_op jit(solution)/shard_map/dynamic_slice | solution.py:272
  1.7 1.2 %constant_dynamic-slice_fusion.3 = (bf16[128,1024]{1,0:T(8,128)(2,1)S(1)}, bf16[128,1024]{1,0:T(8,128)(2,1)S(1)}) fusion(bf16[128,2048]{1,0:T(8,128)(2,1)} %s_own.1, s32[]{:T(128)S(6)} %select_n.24, bf16[128,2048]{1,0:T(8,128)(2,1)} %v_own.3), kind=kLoop, calls=%fused_computation.6 | loop fusion | bytes 1048580 | tf_op jit(solution)/shard_map/dynamic_slice | solution.py:272
  4.7 1.0 %pad_maximum_fusion.1 = bf16[384,1024]{1,0:T(8,128)(2,1)} fusion(bf16[128,1024]{1,0:T(8,128)(2,1)S(1)} %get-tuple-element.30, bf16[128,1024]{1,0:T(8,128)(2,1)S(1)} %get-tuple-element.31, bf16[128,1024]{1,0:T(8,128)(2,1)S(1)} %constant_dynamic-slice_fusion.2), kind=kLoop, calls=%fused_computation.1 | loop fusion | flops 2359296 | bytes 1572864 | tf_op jit(solution)/shard_map/concatenate | solution.py:271
  6.1 1.5 %collective-permute-done.2 = s32[1,128]{1,0:T(1,128)S(1)} collective-permute-done((s32[1,128]{1,0:T(1,128)S(1)}, s32[1,128]{1,0:T(1,128)S(1)}, u32[]{:S(2)}, u32[]{:S(2)}) %collective-permute-start.2) | collective-permute-done | bytes 544 | tf_op jit(solution)/shard_map/ppermute | solution.py:240
  8.1 3.2 %collective-permute-start.3 = (bf16[1040,128]{1,0:T(8,128)(2,1)S(1)}, bf16[1040,128]{1,0:T(8,128)(2,1)S(1)}, u32[]{:S(2)}, u32[]{:S(2)}) collective-permute-start(bf16[1040,128]{1,0:T(8,128)(2,1)S(1)} %get-tuple-element.18), channel_id=1, source_target_pairs={{0,8},{8,16},{16,24},{1,9},{9,17},{17,25},{2,10},{10,18},{18,26},{... | collective-permute-start | bytes 798728 | tf_op jit(solution)/shard_map/ppermute | solution.py:245
  11.3 3.2 %collective-permute-start.14 = (bf16[272,1024]{1,0:T(8,128)(2,1)S(1)}, bf16[272,1024]{1,0:T(8,128)(2,1)S(1)}, u32[]{:S(2)}, u32[]{:S(2)}) collective-permute-start(bf16[272,1024]{1,0:T(8,128)(2,1)S(1)} %get-tuple-element.26.k_chip), channel_id=1, source_target_pairs={{0,8},{8,16},{16,24},{1,9},{9,17},{17,25},{2,10},{10,18},{18,26},{... | collective-permute-start | bytes 1671176 | tf_op jit(solution)/shard_map/ppermute | solution.py:245
  14.5 1.2 %shard_map.95 = (f32[256,1024]{1,0:T(8,128)S(1)}, bf16[256,1024]{1,0:T(8,128)(2,1)S(1)}, f32[256,1024]{1,0:T(8,128)S(1)}) custom-call(s32[1]{0:T(128)} %bitcast.core, bf16[128,2048]{1,0:T(8,128)(2,1)S(1)} %copy-done.6, bf16[128,2048]{1,0:T(8,128)(2,1)S(1)} %copy-done, bf16[128,2048]{1,0:T(8,128)(2,1)S(1)} %copy-done.1, bf16[128,2048]{1,0:T(8,128)(2,1)S(1)} %copy-done.8, ...), custom_call_target="tpu_custom_call" | custom-call | tf_op jit(solution)/shard_map/pallas_call | solution.py:223
  15.7 1.9 %collective-permute-done.3.refs_2_ = bf16[1040,128]{1,0:T(8,128)(2,1)S(1)} collective-permute-done((bf16[1040,128]{1,0:T(8,128)(2,1)S(1)}, bf16[1040,128]{1,0:T(8,128)(2,1)S(1)}, u32[]{:S(2)}, u32[]{:S(2)}) %collective-permute-start.3) | collective-permute-done | bytes 266272 | tf_op jit(solution)/shard_map/ppermute | solution.py:245
  18.0 2.0 %collective-permute-start.9 = (f32[1,256]{1,0:T(1,128)S(1)}, f32[1,256]{1,0:T(1,128)S(1)}, u32[]{:S(2)}, u32[]{:S(2)}) collective-permute-start(f32[1,256]{1,0:T(1,128)S(1)} %get-tuple-element.23), channel_id=1, source_target_pairs={{0,4},{4,0},{1,5},{5,1},{2,6},{6,2},{3,7},{7,3},{8,12},{12,8},{9,1... | collective-permute-start | bytes 3080 | tf_op jit(solution)/shard_map/ppermute | solution.py:240
  20.8 1.2 %collective-permute-start.10 = (f32[1,256]{1,0:T(1,128)S(1)}, f32[1,256]{1,0:T(1,128)S(1)}, u32[]{:S(2)}, u32[]{:S(2)}) collective-permute-start(f32[1,256]{1,0:T(1,128)S(1)} %add.24.refs_2_), channel_id=1, source_target_pairs={{0,1},{1,0},{2,3},{3,2},{4,5},{5,4},{6,7},{7,6},{8,9},{9,8},{10,11... | collective-permute-start | bytes 3080 | tf_op jit(solution)/shard_map/ppermute | solution.py:252
  22.0 1.2 %collective-permute-start.11 = (f32[1,256]{1,0:T(1,128)S(1)}, f32[1,256]{1,0:T(1,128)S(1)}, u32[]{:S(2)}, u32[]{:S(2)}) collective-permute-start(f32[1,256]{1,0:T(1,128)S(1)} %add.24.refs_2_), channel_id=1, source_target_pairs={{0,2},{1,3},{2,0},{3,1},{4,6},{5,7},{6,4},{7,5},{8,10},{9,11},{10,... | collective-permute-start | bytes 3080 | tf_op jit(solution)/shard_map/ppermute | solution.py:252
  23.5 1.2 %collective-permute-done.11.refs_4_ = f32[1,256]{1,0:T(1,128)S(1)} collective-permute-done((f32[1,256]{1,0:T(1,128)S(1)}, f32[1,256]{1,0:T(1,128)S(1)}, u32[]{:S(2)}, u32[]{:S(2)}) %collective-permute-start.11) | collective-permute-done | bytes 1056 | tf_op jit(solution)/shard_map/ppermute | solution.py:252
  24.7 1.8 %collective-permute-done.12.refs_5_ = f32[1,256]{1,0:T(1,128)S(1)} collective-permute-done((f32[1,256]{1,0:T(1,128)S(1)}, f32[1,256]{1,0:T(1,128)S(1)}, u32[]{:S(2)}, u32[]{:S(2)}) %collective-permute-start.12) | collective-permute-done | bytes 1056 | tf_op jit(solution)/shard_map/ppermute | solution.py:252
  26.8 3.2 %collective-permute-start.16 = (bf16[256,1024]{1,0:T(8,128)(2,1)S(1)}, bf16[256,1024]{1,0:T(8,128)(2,1)S(1)}, u32[]{:S(2)}, u32[]{:S(2)}) collective-permute-start(bf16[256,1024]{1,0:T(8,128)(2,1)S(1)} %shard_map.99.rest), channel_id=1, source_target_pairs={{0,8},{8,16},{16,24},{1,9},{9,17},{17,25},{2,10},{10,18},{18,26},{... | collective-permute-start | bytes 1572872 | tf_op jit(solution)/shard_map/ppermute | solution.py:245
  30.0 3.2 %collective-permute-start.15 = (bf16[144,1024]{1,0:T(8,128)(2,1)S(1)}, bf16[144,1024]{1,0:T(8,128)(2,1)S(1)}, u32[]{:S(2)}, u32[]{:S(2)}) collective-permute-start(bf16[144,1024]{1,0:T(8,128)(2,1)S(1)} %slice.20), channel_id=1, source_target_pairs={{0,8},{8,16},{16,24},{1,9},{9,17},{17,25},{2,10},{10,18},{18,26},{... | collective-permute-start | bytes 884744 | tf_op jit(solution)/shard_map/ppermute | solution.py:245
  33.3 2.7 %collective-permute-start.4 = (bf16[1040,128]{1,0:T(8,128)(2,1)S(1)}, bf16[1040,128]{1,0:T(8,128)(2,1)S(1)}, u32[]{:S(2)}, u32[]{:S(2)}) collective-permute-start(bf16[1040,128]{1,0:T(8,128)(2,1)S(1)} %collective-permute-done.3.refs_2_), channel_id=1, source_target_pairs={{0,8},{8,16},{16,24},{1,9},{9,17},{17,25},{2,10},{10,18},{18,26},{... | collective-permute-start | bytes 798728 | tf_op jit(solution)/shard_map/ppermute | solution.py:245
  36.0 4.1 %collective-permute-done.16.v_near = bf16[256,1024]{1,0:T(8,128)(2,1)S(1)} collective-permute-done((bf16[256,1024]{1,0:T(8,128)(2,1)S(1)}, bf16[256,1024]{1,0:T(8,128)(2,1)S(1)}, u32[]{:S(2)}, u32[]{:S(2)}) %collective-permute-start.16) | collective-permute-done | bytes 524320 | tf_op jit(solution)/shard_map/ppermute | solution.py:245
  40.1 3.2 %collective-permute-start.17 = (bf16[128,1024]{1,0:T(8,128)(2,1)S(1)}, bf16[128,1024]{1,0:T(8,128)(2,1)S(1)}, u32[]{:S(2)}, u32[]{:S(2)}) collective-permute-start(bf16[128,1024]{1,0:T(8,128)(2,1)S(1)} %slice.21), channel_id=1, source_target_pairs={{0,8},{8,16},{16,24},{1,9},{9,17},{17,25},{2,10},{10,18},{18,26},{... | collective-permute-start | bytes 786440 | tf_op jit(solution)/shard_map/ppermute | solution.py:245
  43.4 8.7 %collective-permute-done.4.refs_3_ = bf16[1040,128]{1,0:T(8,128)(2,1)S(1)} collective-permute-done((bf16[1040,128]{1,0:T(8,128)(2,1)S(1)}, bf16[1040,128]{1,0:T(8,128)(2,1)S(1)}, u32[]{:S(2)}, u32[]{:S(2)}) %collective-permute-start.4) | collective-permute-done | bytes 266272 | tf_op jit(solution)/shard_map/ppermute | solution.py:245
  52.4 5.6 %collective-permute-start.5 = (f32[1,128]{1,0:T(1,128)S(1)}, f32[1,128]{1,0:T(1,128)S(1)}, u32[]{:S(2)}, u32[]{:S(2)}) collective-permute-start(f32[1,128]{1,0:T(1,128)S(1)} %get-tuple-element.22), channel_id=1, source_target_pairs={{0,4},{4,0},{1,5},{5,1},{2,6},{6,2},{3,7},{7,3},{8,12},{12,8},{9,1... | collective-permute-start | bytes 1544 | tf_op jit(solution)/shard_map/ppermute | solution.py:240
  59.3 2.2 %collective-permute-start.8 = (f32[1,128]{1,0:T(1,128)S(1)}, f32[1,128]{1,0:T(1,128)S(1)}, u32[]{:S(2)}, u32[]{:S(2)}) collective-permute-start(f32[1,128]{1,0:T(1,128)S(1)} %add.23.s0), channel_id=1, source_target_pairs={{0,3},{1,2},{2,1},{3,0},{4,7},{5,6},{6,5},{7,4},{8,11},{9,10},{10,... | collective-permute-start | bytes 1544 | tf_op jit(solution)/shard_map/ppermute | solution.py:252
  61.5 1.1 %collective-permute-done.8.s3 = f32[1,128]{1,0:T(1,128)S(1)} collective-permute-done((f32[1,128]{1,0:T(1,128)S(1)}, f32[1,128]{1,0:T(1,128)S(1)}, u32[]{:S(2)}, u32[]{:S(2)}) %collective-permute-start.8) | collective-permute-done | bytes 544 | tf_op jit(solution)/shard_map/ppermute | solution.py:252
  62.8 2.1 %collective-permute-start.13 = (bf16[128,1024]{1,0:T(8,128)(2,1)S(1)}, bf16[128,1024]{1,0:T(8,128)(2,1)S(1)}, u32[]{:S(2)}, u32[]{:S(2)}) collective-permute-start(bf16[128,1024]{1,0:T(8,128)(2,1)S(1)} %get-tuple-element.25), channel_id=1, source_target_pairs={{0,4},{4,0},{1,5},{5,1},{2,6},{6,2},{3,7},{7,3},{8,12},{12,8},{9,1... | collective-permute-start | bytes 786440 | tf_op jit(solution)/shard_map/ppermute | solution.py:240
  64.9 2.4 %shard_map.102.weights = bf16[8,256,640]{2,1,0:T(8,128)(2,1)S(1)} custom-call(s32[1]{0:T(128)} %bitcast.core, bf16[128,2048]{1,0:T(8,128)(2,1)S(1)} %copy-done.4, bf16[384,1024]{1,0:T(8,128)(2,1)S(1)} %collective-permute-done.1.got_qg.got_q, bf16[272,1024]{1,0:T(8,128)(2,1)S(1)} %get-tuple-element.26.k_chip, ...), custom_call_target="tpu_custom_call" | custom-call | tf_op jit(solution)/shard_map/pallas_call | solution.py:223
  (62 shorter events, 9.7 us)
Async XLA Ops:
  0.6 3.9 %copy-start.5 = (bf16[128,2048]{1,0:T(8,128)(2,1)S(1)}, bf16[128,2048]{1,0:T(8,128)(2,1)}, u32[]{:S(2)}) copy-start(bf16[128,2048]{1,0:T(8,128)(2,1)} %q_own.2) | copy-start | bytes 1572868
  3.8 3.8 %collective-permute-start = (bf16[384,1024]{1,0:T(8,128)(2,1)}, bf16[384,1024]{1,0:T(8,128)(2,1)S(1)}, u32[]{:S(2)}, u32[]{:S(2)}) collective-permute-start(bf16[384,1024]{1,0:T(8,128)(2,1)} %pad_maximum_fusion), channel_id=1, source_target_pairs={{0,4},{4,0},{1,5},{5,1},{2,6},{6,2},{3,7},{7,3},{8,12},{12,8},{9,1... | collective-permute-start | bytes 2359304 | tf_op jit(solution)/shard_map/ppermute | solution.py:240
  5.6 8.9 %copy-start.9 = (bf16[2048]{0:T(1024)(128)(2,1)S(1)}, bf16[2048]{0:T(1024)(128)(2,1)}, u32[]{:S(2)}) copy-start(bf16[2048]{0:T(1024)(128)(2,1)} %param.12) | copy-start | bytes 12292
  5.6 8.9 %collective-permute-start.1 = (bf16[384,1024]{1,0:T(8,128)(2,1)}, bf16[384,1024]{1,0:T(8,128)(2,1)S(1)}, u32[]{:S(2)}, u32[]{:S(2)}) collective-permute-start(bf16[384,1024]{1,0:T(8,128)(2,1)} %pad_maximum_fusion.1), channel_id=1, source_target_pairs={{0,4},{4,0},{1,5},{5,1},{2,6},{6,2},{3,7},{7,3},{8,12},{12,8},{9,1... | collective-permute-start | bytes 2359304 | tf_op jit(solution)/shard_map/ppermute | solution.py:240
  5.7 1.9 %collective-permute-start.2 = (s32[1,128]{1,0:T(1,128)S(1)}, s32[1,128]{1,0:T(1,128)S(1)}, u32[]{:S(2)}, u32[]{:S(2)}) collective-permute-start(s32[1,128]{1,0:T(1,128)S(1)} %add_bitcast_fusion), channel_id=1, source_target_pairs={{0,4},{4,0},{1,5},{5,1},{2,6},{6,2},{3,7},{7,3},{8,12},{12,8},{9,1... | collective-permute-start | bytes 1544 | tf_op jit(solution)/shard_map/ppermute | solution.py:240
  6.1 8.4 %copy-start.6 = (bf16[128,2048]{1,0:T(8,128)(2,1)S(1)}, bf16[128,2048]{1,0:T(8,128)(2,1)}, u32[]{:S(2)}) copy-start(bf16[128,2048]{1,0:T(8,128)(2,1)} %q_own.2) | copy-start | bytes 1572868
  6.1 8.4 %copy-start.8 = (bf16[128,2048]{1,0:T(8,128)(2,1)S(1)}, bf16[128,2048]{1,0:T(8,128)(2,1)}, u32[]{:S(2)}) copy-start(bf16[128,2048]{1,0:T(8,128)(2,1)} %g_own.1) | copy-start | bytes 1572868
  8.1 9.5 %collective-permute-start.3 = (bf16[1040,128]{1,0:T(8,128)(2,1)S(1)}, bf16[1040,128]{1,0:T(8,128)(2,1)S(1)}, u32[]{:S(2)}, u32[]{:S(2)}) collective-permute-start(bf16[1040,128]{1,0:T(8,128)(2,1)S(1)} %get-tuple-element.18), channel_id=1, source_target_pairs={{0,8},{8,16},{16,24},{1,9},{9,17},{17,25},{2,10},{10,18},{18,26},{... | collective-permute-start | bytes 798728 | tf_op jit(solution)/shard_map/ppermute | solution.py:245
  11.3 18.7 %collective-permute-start.14 = (bf16[272,1024]{1,0:T(8,128)(2,1)S(1)}, bf16[272,1024]{1,0:T(8,128)(2,1)S(1)}, u32[]{:S(2)}, u32[]{:S(2)}) collective-permute-start(bf16[272,1024]{1,0:T(8,128)(2,1)S(1)} %get-tuple-element.26.k_chip), channel_id=1, source_target_pairs={{0,8},{8,16},{16,24},{1,9},{9,17},{17,25},{2,10},{10,18},{18,26},{... | collective-permute-start | bytes 1671176 | tf_op jit(solution)/shard_map/ppermute | solution.py:245
  18.0 2.8 %collective-permute-start.9 = (f32[1,256]{1,0:T(1,128)S(1)}, f32[1,256]{1,0:T(1,128)S(1)}, u32[]{:S(2)}, u32[]{:S(2)}) collective-permute-start(f32[1,256]{1,0:T(1,128)S(1)} %get-tuple-element.23), channel_id=1, source_target_pairs={{0,4},{4,0},{1,5},{5,1},{2,6},{6,2},{3,7},{7,3},{8,12},{12,8},{9,1... | collective-permute-start | bytes 3080 | tf_op jit(solution)/shard_map/ppermute | solution.py:240
  20.8 2.7 %collective-permute-start.10 = (f32[1,256]{1,0:T(1,128)S(1)}, f32[1,256]{1,0:T(1,128)S(1)}, u32[]{:S(2)}, u32[]{:S(2)}) collective-permute-start(f32[1,256]{1,0:T(1,128)S(1)} %add.24.refs_2_), channel_id=1, source_target_pairs={{0,1},{1,0},{2,3},{3,2},{4,5},{5,4},{6,7},{7,6},{8,9},{9,8},{10,11... | collective-permute-start | bytes 3080 | tf_op jit(solution)/shard_map/ppermute | solution.py:252
  22.0 2.7 %collective-permute-start.11 = (f32[1,256]{1,0:T(1,128)S(1)}, f32[1,256]{1,0:T(1,128)S(1)}, u32[]{:S(2)}, u32[]{:S(2)}) collective-permute-start(f32[1,256]{1,0:T(1,128)S(1)} %add.24.refs_2_), channel_id=1, source_target_pairs={{0,2},{1,3},{2,0},{3,1},{4,6},{5,7},{6,4},{7,5},{8,10},{9,11},{10,... | collective-permute-start | bytes 3080 | tf_op jit(solution)/shard_map/ppermute | solution.py:252
  23.3 3.3 %collective-permute-start.12 = (f32[1,256]{1,0:T(1,128)S(1)}, f32[1,256]{1,0:T(1,128)S(1)}, u32[]{:S(2)}, u32[]{:S(2)}) collective-permute-start(f32[1,256]{1,0:T(1,128)S(1)} %add.24.refs_2_), channel_id=1, source_target_pairs={{0,3},{1,2},{2,1},{3,0},{4,7},{5,6},{6,5},{7,4},{8,11},{9,10},{10,... | collective-permute-start | bytes 3080 | tf_op jit(solution)/shard_map/ppermute | solution.py:252
  26.8 13.3 %collective-permute-start.16 = (bf16[256,1024]{1,0:T(8,128)(2,1)S(1)}, bf16[256,1024]{1,0:T(8,128)(2,1)S(1)}, u32[]{:S(2)}, u32[]{:S(2)}) collective-permute-start(bf16[256,1024]{1,0:T(8,128)(2,1)S(1)} %shard_map.99.rest), channel_id=1, source_target_pairs={{0,8},{8,16},{16,24},{1,9},{9,17},{17,25},{2,10},{10,18},{18,26},{... | collective-permute-start | bytes 1572872 | tf_op jit(solution)/shard_map/ppermute | solution.py:245
  30.0 34.8 %collective-permute-start.15 = (bf16[144,1024]{1,0:T(8,128)(2,1)S(1)}, bf16[144,1024]{1,0:T(8,128)(2,1)S(1)}, u32[]{:S(2)}, u32[]{:S(2)}) collective-permute-start(bf16[144,1024]{1,0:T(8,128)(2,1)S(1)} %slice.20), channel_id=1, source_target_pairs={{0,8},{8,16},{16,24},{1,9},{9,17},{17,25},{2,10},{10,18},{18,26},{... | collective-permute-start | bytes 884744 | tf_op jit(solution)/shard_map/ppermute | solution.py:245
  33.3 18.8 %collective-permute-start.4 = (bf16[1040,128]{1,0:T(8,128)(2,1)S(1)}, bf16[1040,128]{1,0:T(8,128)(2,1)S(1)}, u32[]{:S(2)}, u32[]{:S(2)}) collective-permute-start(bf16[1040,128]{1,0:T(8,128)(2,1)S(1)} %collective-permute-done.3.refs_2_), channel_id=1, source_target_pairs={{0,8},{8,16},{16,24},{1,9},{9,17},{17,25},{2,10},{10,18},{18,26},{... | collective-permute-start | bytes 798728 | tf_op jit(solution)/shard_map/ppermute | solution.py:245
  40.1 27.1 %collective-permute-start.17 = (bf16[128,1024]{1,0:T(8,128)(2,1)S(1)}, bf16[128,1024]{1,0:T(8,128)(2,1)S(1)}, u32[]{:S(2)}, u32[]{:S(2)}) collective-permute-start(bf16[128,1024]{1,0:T(8,128)(2,1)S(1)} %slice.21), channel_id=1, source_target_pairs={{0,8},{8,16},{16,24},{1,9},{9,17},{17,25},{2,10},{10,18},{18,26},{... | collective-permute-start | bytes 786440 | tf_op jit(solution)/shard_map/ppermute | solution.py:245
  52.4 12.5 %copy-start.4 = (bf16[128,2048]{1,0:T(8,128)(2,1)S(1)}, bf16[128,2048]{1,0:T(8,128)(2,1)}, u32[]{:S(2)}) copy-start(bf16[128,2048]{1,0:T(8,128)(2,1)} %q_own.3) | copy-start | bytes 1572868
  52.4 6.4 %collective-permute-start.5 = (f32[1,128]{1,0:T(1,128)S(1)}, f32[1,128]{1,0:T(1,128)S(1)}, u32[]{:S(2)}, u32[]{:S(2)}) collective-permute-start(f32[1,128]{1,0:T(1,128)S(1)} %get-tuple-element.22), channel_id=1, source_target_pairs={{0,4},{4,0},{1,5},{5,1},{2,6},{6,2},{3,7},{7,3},{8,12},{12,8},{9,1... | collective-permute-start | bytes 1544 | tf_op jit(solution)/shard_map/ppermute | solution.py:240
  58.8 2.7 %collective-permute-start.6 = (f32[1,128]{1,0:T(1,128)S(1)}, f32[1,128]{1,0:T(1,128)S(1)}, u32[]{:S(2)}, u32[]{:S(2)}) collective-permute-start(f32[1,128]{1,0:T(1,128)S(1)} %add.23.s0), channel_id=1, source_target_pairs={{0,1},{1,0},{2,3},{3,2},{4,5},{5,4},{6,7},{7,6},{8,9},{9,8},{10,11... | collective-permute-start | bytes 1544 | tf_op jit(solution)/shard_map/ppermute | solution.py:252
  59.1 2.4 %collective-permute-start.7 = (f32[1,128]{1,0:T(1,128)S(1)}, f32[1,128]{1,0:T(1,128)S(1)}, u32[]{:S(2)}, u32[]{:S(2)}) collective-permute-start(f32[1,128]{1,0:T(1,128)S(1)} %add.23.s0), channel_id=1, source_target_pairs={{0,2},{1,3},{2,0},{3,1},{4,6},{5,7},{6,4},{7,5},{8,10},{9,11},{10,... | collective-permute-start | bytes 1544 | tf_op jit(solution)/shard_map/ppermute | solution.py:252
  59.3 3.3 %collective-permute-start.8 = (f32[1,128]{1,0:T(1,128)S(1)}, f32[1,128]{1,0:T(1,128)S(1)}, u32[]{:S(2)}, u32[]{:S(2)}) collective-permute-start(f32[1,128]{1,0:T(1,128)S(1)} %add.23.s0), channel_id=1, source_target_pairs={{0,3},{1,2},{2,1},{3,0},{4,7},{5,6},{6,5},{7,4},{8,11},{9,10},{10,... | collective-permute-start | bytes 1544 | tf_op jit(solution)/shard_map/ppermute | solution.py:252
  62.8 5.4 %collective-permute-start.13 = (bf16[128,1024]{1,0:T(8,128)(2,1)S(1)}, bf16[128,1024]{1,0:T(8,128)(2,1)S(1)}, u32[]{:S(2)}, u32[]{:S(2)}) collective-permute-start(bf16[128,1024]{1,0:T(8,128)(2,1)S(1)} %get-tuple-element.25), channel_id=1, source_target_pairs={{0,4},{4,0},{1,5},{5,1},{2,6},{6,2},{3,7},{7,3},{8,12},{12,8},{9,1... | collective-permute-start | bytes 786440 | tf_op jit(solution)/shard_map/ppermute | solution.py:240
  68.1 1.6 %collective-permute-start.18 = (bf16[128,1024]{1,0:T(8,128)(2,1)S(1)}, bf16[128,1024]{1,0:T(8,128)(2,1)S(1)}, u32[]{:S(2)}, u32[]{:S(2)}) collective-permute-start(bf16[128,1024]{1,0:T(8,128)(2,1)S(1)} %get-tuple-element.29), channel_id=1, source_target_pairs={{0,4},{4,0},{1,5},{5,1},{2,6},{6,2},{3,7},{7,3},{8,12},{12,8},{9,1... | collective-permute-start | bytes 786440 | tf_op jit(solution)/shard_map/ppermute | solution.py:240
  (6 other events, 19.1 us)

commit v2 on v1

v2 whole, which is shorter than its diff:
```python
import functools
import math

import jax
import jax.numpy as jnp
from jax import lax
from jax.experimental import pallas as pl
from jax.experimental.pallas import tpu as pltpu
from jax.sharding import PartitionSpec as P

DH = 128
PAD = 16
F32 = jnp.float32
BF16 = jnp.bfloat16
NONE = -1e30
VMEM_LIMIT = 20 * 1024 * 1024
BYTES_PER_US = 3.0e6


def dot(a, b, dims=((1,), (0,))):
    return lax.dot_general(a, b, (dims, ((), ())), preferred_element_type=F32)


def column(row):
    n = row.shape[1]
    parts = [jnp.broadcast_to(row[:, i : i + 128], (128, 128)).T for i in range(0, n, 128)]
    return parts[0] if len(parts) == 1 else jnp.concatenate(parts, axis=0)


def as_row(col):
    return jnp.broadcast_to(col, (128, 128)).T[:1]


def lane_sums(x):
    parts = [
        jnp.sum(x[i : i + 128].T, axis=0, keepdims=True) for i in range(0, x.shape[0], 128)
    ]
    return parts[0] if len(parts) == 1 else jnp.concatenate(parts, axis=1)


def split(x):
    high = x.astype(BF16)
    rest = x - high.astype(F32)
    middle = rest.astype(BF16)
    return high, middle, (rest - middle.astype(F32)).astype(BF16)


def inner():
    return lax.axis_index("inner")


def chip():
    return lax.axis_index("outer")


def in_order(own, other):
    first = inner() == 0
    return jnp.where(first, own, other), jnp.where(first, other, own)


def mine(width, h=0, heads=None):
    size = width if heads is None else DH
    return pl.ds(pl.multiple_of(inner() * width + h * DH, DH), size)


def head(width, h):
    return mine(width, h, 1)


def place(whole, own, other):
    tb, width = own.shape[0], whole.shape[1]
    cols = mine(width)
    whole[:tb, :], whole[tb:, :] = in_order(own[:, cols], other[:, cols])


def message_docs(message, valid):
    tail = jnp.where(valid, message[message.shape[0] - PAD :, :DH].astype(F32), 0.0)
    half = PAD // 2
    return tail[:1], tail[half : half + 1], tail[PAD - 1 :, DH - 1 :]


def cut_kernel(key, value, segments, keys, values, docs):
    cols = mine(keys.shape[1])
    keys[...] = key[:, cols]
    values[...] = value[:, cols]
    docs[...] = (segments[...] + 1).astype(F32)


def state_kernel(k_own, v_own, k_got, v_got, own_docs, got_docs, t_out, docs):
    tb, width = k_own.shape
    own_row = own_docs[...]
    got_row = (got_docs[...] + 1).astype(F32)
    rows = in_order(own_row, got_row)
    last = rows[1][:, tb - 1 :]
    own_keep = column(own_row) == last
    got_keep = column(got_row) == last
    zero = jnp.zeros((tb, DH), BF16)
    for h in range(width // DH):
        cols, got = slice(h * DH, (h + 1) * DH), head(width, h)
        own = jnp.where(own_keep, k_own[:, cols], zero)
        other = jnp.where(got_keep, k_got[:, got], zero)
        state = dot(own, v_own[:, cols], ((0,), (0,)))
        state += dot(other, v_got[:, got], ((0,), (0,)))
        t_out[:DH, cols] = state.astype(BF16)
    half = PAD // 2
    tail = jnp.concatenate([jnp.broadcast_to(r, (half, tb)) for r in rows], axis=0)
    t_out[DH:, :] = jnp.zeros((PAD, width), BF16)
    t_out[DH:, :tb] = tail.astype(BF16)
    docs[...] = jnp.concatenate(rows, axis=1)


def intra_kernel(
    q_own, k_own, v_own, g_own, q_got, k_got, v_got, g_got, gain, docs,
    intra, q_out, gate_out, k_all, v_all, g_all,
):
    n, width = intra.shape
    tb = n // 2
    place(q_out, q_own, q_got)
    place(g_all, g_own, g_got)
    cols = mine(width)
    k_all[:tb, :], k_all[tb:, :] = in_order(k_own[...], k_got[:, cols])
    v_all[:tb, :], v_all[tb:, :] = in_order(v_own[...], v_got[:, cols])
    row = lax.broadcasted_iota(jnp.int32, (n, n), 0)
    col = lax.broadcasted_iota(jnp.int32, (n, n), 1)
    d = column(docs[...])
    same = jnp.concatenate([d, d], axis=1) == docs[...]
    visible = same & (row >= col)
    gains = gain[:, mine(width)].astype(F32)
    for h in range(width // DH):
        cols = slice(h * DH, (h + 1) * DH)
        scores = dot(q_out[:, cols], k_all[:, cols], ((1,), (1,)))
        weights = jnp.where(visible, scores, 0.0).astype(BF16)
        intra[:, cols] = dot(weights, v_all[:, cols])
        gate = jax.nn.sigmoid(g_all[:, cols].astype(F32))
        gate_out[:, cols] = gate * gains[:, cols]


def mixed_kernel(intra, q, t_near, docs, mixed, squares):
    n, width = q.shape
    seen = column(docs[...]) == message_docs(t_near, chip() >= 1)[2]
    total = jnp.zeros((n, DH), F32)
    for h in range(width // DH):
        cols = slice(h * DH, (h + 1) * DH)
        carried = dot(q[:, cols], t_near[:DH, cols])
        value = intra[:, cols] + jnp.where(seen, carried, 0.0)
        mixed[:, cols] = value
        total += value * value
    squares[...] = lane_sums(total)


def second_kernel(mixed, q, t_near, message, docs, fixed, squares):
    n, width = fixed.shape
    near = message_docs(t_near, chip() >= 1)[2]
    far = message_docs(message, chip() >= 2)[2]
    seen = (column(docs[:, :n]) == near) & (near == far)
    total = jnp.zeros((n, DH), F32)
    for h in range(width // DH):
        cols = slice(h * DH, (h + 1) * DH)
        carried = dot(q[:n, cols], message[2 * n : 2 * n + DH, cols])
        value = mixed[:n, cols] + jnp.where(seen, carried, 0.0)
        fixed[:, cols] = value
        total += value * value
    squares[...] = lane_sums(total)


def normed(columns, mixed, gate, sums, out):
    scale = column(lax.rsqrt(sum(x[...] for x in sums) / columns + 1e-05))
    for h in range(mixed.shape[1] // DH):
        cols = slice(h * DH, (h + 1) * DH)
        out[:, cols] = (mixed[:, cols] * scale * gate[:, cols]).astype(BF16)


def norm_kernel(columns, mixed, gate, s0, s1, s2, s3, t_near, out):
    n = mixed.shape[0]
    normed(columns, mixed, gate, (s0, s1, s2, s3), out.at[pl.ds(0, n)])
    out[n:, :] = t_near[...]


def output_kernel(columns, fixed, gate, s0, s1, s2, s3, values, first, out, sent):
    tb = fixed.shape[0]
    normed(columns, fixed, gate.at[pl.ds(0, tb)], (s0, s1, s2, s3), first)
    top = inner() == 0
    out[...] = jnp.where(top, first[...], values[tb : 2 * tb, :])
    sent[...] = jnp.where(top, values[tb : 2 * tb, :], first[...])


def softmax_part(q, k, visible):
    scores = dot(q, k, ((1,), (1,))) * (1.0 / math.sqrt(DH))
    scores = jnp.where(visible, scores, NONE)
    top = jnp.max(scores, axis=1, keepdims=True)
    e = jnp.where(visible, jnp.exp(scores - top), 0.0)
    total = jnp.sum(e, axis=1, keepdims=True)
    some = jnp.where(total > 0.0, total, 1.0)
    return (e / some).astype(BF16), jnp.where(total > 0.0, top + jnp.log(some), NONE)


def pick_kernel(first, second, out):
    out[...] = jnp.where(inner() == 0, first[...], second[...])


def far_kernel(mixed_own, mixed_got, k_own, k_got, t_near, docs, weights, lse):
    tb, local = k_own.shape
    width = local // 2
    near = message_docs(t_near, chip() >= 1)
    last = docs[:, 2 * tb - 1 :]
    visible = jnp.broadcast_to((near[1] == last) & (near[2] == last), (tb, tb))
    for h in range(width // DH):
        cols = head(width, h)
        queries = in_order(mixed_own[:, cols], mixed_got[:, cols])[1]
        keys = in_order(k_own[:, cols], k_got[:, cols])[0]
        weights[h], top = softmax_part(queries, keys, visible)
        lse[:, h * DH : (h + 1) * DH] = as_row(top)


def answer_kernel(weights, lse, values, out):
    tb = weights.shape[1]
    width = values.shape[1]
    for h in range(width // DH):
        cols = slice(h * DH, (h + 1) * DH)
        out[:tb, cols] = dot(weights[h], values[tb : 2 * tb, cols]).astype(BF16)
    high, middle, low = split(lse[...])
    rows = [high, middle, low, jnp.zeros((PAD - 3, width), BF16)]
    out[tb:, :] = jnp.concatenate([r.astype(F32) for r in rows], axis=0).astype(BF16)


def weights_kernel(
    q_own, k_own, q_got, k_got, near_first, near_first_got, near_last, near_last_got,
    t_near, docs, weights, lse, q_all, k_all,
):
    n, width = q_all.shape
    tb = n // 2
    keys = 2 * n
    place(q_all, q_own, q_got)
    cols = mine(width)
    k_all[:tb, :] = in_order(near_first[:, cols], near_first_got[:, cols])[0]
    k_all[tb:n, :] = in_order(near_last[:, cols], near_last_got[:, cols])[0]
    place(k_all.at[n:], k_own, k_got)
    near_docs = message_docs(t_near, chip() >= 1)
    key_docs = jnp.concatenate([near_docs[0], near_docs[1], docs[...]], axis=1)
    d = column(docs[...])
    same = jnp.concatenate([d] * (keys // 128), axis=1) == key_docs
    row = lax.broadcasted_iota(jnp.int32, (n, keys), 0)
    col = lax.broadcasted_iota(jnp.int32, (n, keys), 1) - n
    visible = same & (row >= col)
    for h in range(width // DH):
        cols = slice(h * DH, (h + 1) * DH)
        weights[h], top = softmax_part(q_all[:, cols], k_all[:, cols], visible)
        lse[:, cols] = as_row(top[:tb])


def attend_kernel(weights, lse, answer, near, first, values, t_near, docs, out, sent):
    tb, width = first.shape
    n = 2 * tb
    near_last = message_docs(t_near, chip() >= 2)[2]
    asked = column(docs[:, :tb]) == near_last
    for h in range(width // DH):
        cols = slice(h * DH, (h + 1) * DH)
        total = dot(weights[h, :, :n], near[:n, cols])
        total += dot(weights[h, :, n : n + tb], first[:, cols])
        total += dot(weights[h, :, n + tb :], values[tb:n, cols])
        far_lse = sum(answer[tb + i : tb + i + 1, cols].astype(F32) for i in range(3))
        far_lse = jnp.where(asked, column(far_lse), NONE)
        here_lse = column(lse[:, cols])
        top = jnp.maximum(far_lse, here_lse)
        far, here = jnp.exp(far_lse - top), jnp.exp(here_lse - top)
        part = jnp.where(asked, far * answer[:tb, cols].astype(F32), 0.0)
        upper = ((here * total[:tb] + part) / (here + far)).astype(BF16)
        lower = total[tb:].astype(BF16)
        is_first = inner() == 0
        out[:, cols] = jnp.where(is_first, upper, lower)
        sent[:, cols] = jnp.where(is_first, lower, upper)


def join_kernel(kept, got, out):
    width = kept.shape[1]
    out[:, pl.ds(pl.multiple_of(inner() * width, DH), width)] = kept[...]
    out[:, pl.ds(pl.multiple_of((1 - inner()) * width, DH), width)] = got[...]


def run(kernel, ins, outs, scratch=(), us=0.5):
    got = pl.pallas_call(
        kernel,
        out_shape=[jax.ShapeDtypeStruct(*o) for o in outs],
        in_specs=[pl.BlockSpec(memory_space=pltpu.VMEM)] * len(ins),
        out_specs=[pl.BlockSpec(memory_space=pltpu.VMEM)] * len(outs),
        scratch_shapes=scratch,
        compiler_params=pltpu.CompilerParams(vmem_limit_bytes=VMEM_LIMIT),
        cost_estimate=pl.CostEstimate(
            flops=0, bytes_accessed=int(us * BYTES_PER_US), transcendentals=0
        ),
    )(*ins)
    return got[0] if len(got) == 1 else got


def swap(x):
    return lax.ppermute(x, "inner", [(0, 1), (1, 0)])


def next_chip(x):
    chips = lax.axis_size("outer")
    return lax.ppermute(x, "outer", [(i, (i + 1) % chips) for i in range(chips)])


def both_ways(x):
    last = lax.axis_size("outer") - 1
    up = [(2 * i, 2 * i + 2) for i in range(last)] + [(2 * last, 2 * last + 1)]
    down = [(2 * i + 1, 2 * i - 1) for i in range(1, last + 1)] + [(1, 0)]
    return lax.ppermute(x, ("outer", "inner"), up + down)


def over_heads(x):
    size = lax.axis_size("heads")
    x = x + swap(x)
    if size == 4:
        others = [lax.ppermute(x, "heads", [(i, i ^ k) for i in range(size)]) for k in (1, 2, 3)]
        return [x, *others]
    total = lax.psum(x, "heads")
    zero = jnp.zeros_like(total)
    return [total, zero, zero, zero]


def per_device(
    lin_query, lin_key, lin_value, gate_input, norm_gain, segment_ids, soft_query, soft_key
):
    tb, local = lin_query.shape
    width = local // 2
    n = 2 * tb
    heads = width // DH
    columns = local * lax.axis_size("heads")
    block, whole = ((tb, width), BF16), ((n, width), BF16)
    scratch = pltpu.VMEM((n, width), BF16)
    tie = lax.optimization_barrier

    def joined(kept, sent):
        return run(join_kernel, [kept, swap(sent)], [((tb, local), BF16)])

    own_docs = segment_ids[None]
    got_docs = swap(own_docs)
    lk_got, lv_got = swap(lin_key), swap(lin_value)
    keys, values, own_docs = run(
        cut_kernel,
        [lin_key, lin_value, own_docs],
        [block, block, ((1, tb), F32)],
        us=2.0,
    )
    t_msg, docs = run(
        state_kernel,
        [keys, values, lk_got, lv_got, own_docs, got_docs],
        [((DH + PAD, width), BF16), ((1, n), F32)],
    )
    t_near = next_chip(t_msg)
    lin_query, gate_input, soft_query, soft_key, _ = tie(
        (lin_query, gate_input, soft_query, soft_key, t_msg)
    )
    lq_got, g_got = swap(lin_query), swap(gate_input)
    sq_got, sk_got = swap(soft_query), swap(soft_key)
    out_first = run(pick_kernel, [soft_key, sq_got], [((tb, local), BF16)], us=0.3)
    intra, queries, gate = run(
        intra_kernel,
        [
            lin_query, keys, values, gate_input, lq_got, lk_got, lv_got, g_got,
            norm_gain[None], docs,
        ],
        [((n, width), F32), whole, ((n, width), F32)],
        [scratch] * 3,
        us=1.2,
    )
    t_near, intra, out_first, out_last = tie((t_near, intra, out_first, sk_got))
    first_own, last_own = both_ways(out_first), both_ways(out_last)
    first_got, last_got = swap(first_own), swap(last_own)
    mixed, squares = run(
        mixed_kernel, [intra, queries, t_near, docs], [((n, width), F32), ((1, n), F32)]
    )
    values = run(
        functools.partial(norm_kernel, columns),
        [mixed, gate, *over_heads(squares), t_near],
        [((n + DH + PAD, width), BF16)],
        us=0.3,
    )
    near_values = next_chip(values)
    far_weights, far_lse = run(
        far_kernel,
        [first_own, first_got, last_own, last_got, t_near, docs],
        [((heads, tb, tb), BF16), ((1, width), F32)],
    )
    weights, lse = run(
        weights_kernel,
        [
            soft_query, soft_key, sq_got, sk_got, first_own, first_got, last_own, last_got,
            t_near, docs,
        ],
        [((heads, n, 2 * n), BF16), ((1, width), F32)],
        [scratch, pltpu.VMEM((2 * n, width), BF16)],
        us=2.5,
    )
    far_weights, weights, near_values = tie((far_weights, weights, near_values))
    answer = next_chip(
        run(
            answer_kernel, [far_weights, far_lse, near_values], [((tb + PAD, width), BF16)], us=0.3
        )
    )
    fixed, squares = run(
        second_kernel,
        [mixed, queries, t_near, near_values, docs],
        [((tb, width), F32), ((1, tb), F32)],
    )
    first, kept, sent = run(
        functools.partial(output_kernel, columns),
        [fixed, gate, *over_heads(squares), values],
        [block] * 3,
        us=0.3,
    )
    linear_out = joined(kept, sent)
    kept, sent = run(
        attend_kernel,
        [weights, lse, answer, near_values, first, values, t_near, docs],
        [block, block],
        us=1.0,
    )
    return linear_out, joined(kept, sent)


def solution(mesh):
    tokens = P(("outer", "inner"), "heads")
    return jax.shard_map(
        per_device,
        mesh=mesh,
        in_specs=(tokens, tokens, tokens, tokens, P("heads"), P(("outer", "inner")), tokens, tokens),
        out_specs=(tokens, tokens),
        check_vma=False,
    )
```

time: 70.8 us -> 64.1 us (0.905)
  starting transfers between devices: 35 us -> 25.3 us
  waiting for transfers between devices: 22.7 us -> 25.9 us
  other arithmetic: 1.91 us -> 0.01 us
  Pallas kernels: 7.59 us -> 8.73 us
    ppermute x6 -> x5, starting transfers between devices: 18.8 us -> 4.63 us  [the longest x2 3.21 us: both_ways(): return lax.ppermute(x, ('outer', 'inner'), up + down)]
    ppermute x7 -> x13, starting transfers between devices: 11 us -> 14.2 us  [swap(): return lax.ppermute(x, 'inner', [(0, 1), (1, 0)])]
    unnamed x22 -> x16, local copies, waits for them, and re-layouts: 0.05 us -> 3.1 us
    dynamic_slice x4 -> x0, local copies, waits for them, and re-layouts: 2.25 us -> none  [theirs(): lax.dynamic_slice_in_dim(a, (1 - c) * width, width, 1)]
    ppermute x6, waiting for transfers between devices: 4.19 us -> 6.41 us  [over_heads(): lax.ppermute(x, 'heads', [(i, i ^ k) for i in range(size)])]
    concatenate x3 -> x0, other arithmetic: 1.9 us -> none  [the longest x2 1.9 us: theirs(): jnp.concatenate([lax.dynamic_slice_in_dim(a, (1 - c) * width, width, 1) f...]
    ppermute x6, starting transfers between devices: 5.3 us -> 6.45 us  [over_heads(): lax.ppermute(x, 'heads', [(i, i ^ k) for i in range(size)])]
    pallas_call x10 -> x14, Pallas kernels: 7.59 us -> 8.73 us  [run(): pl.pallas_call(kernel, out_shape=[jax.ShapeDtypeStruct(*o) for o in outs]...]
  transfers between devices with their start and end apart: 19 -> 24, of which waited for: 11 -> 15; matrix products, arithmetic and copies ran while one was open for 2% -> 0% of each run, Pallas kernels for 10% -> 11%
where the time goes in v2:
time: 64.1 us; the launch traced here: 63.9 us
  waiting for transfers between devices  25.9 us (40%)
  starting transfers between devices  25.3 us (39%)
  Pallas kernels  8.73 us (14%)
  local copies, waits for them, and re-layouts  3.11 us (5%)
  between operations  0.81 us (1%)
    ppermute x3, waiting for transfers between devices, next_chip(): lax.ppermute(x, 'outer', [(i, (i + 1) % chips) for i in range(chips)])  14.4 us
    ppermute x13, starting transfers between devices, swap(): return lax.ppermute(x, 'inner', [(0, 1), (1, 0)])  14.2 us
    pallas_call x14, Pallas kernels, run(): pl.pallas_call(kernel, out_shape=[jax.ShapeDtypeStruct(*o) for o in outs]...  8.73 us
    ppermute x6, starting transfers between devices, over_heads(): lax.ppermute(x, 'heads', [(i, i ^ k) for i in range(size)])  6.45 us
    ppermute x6, waiting for transfers between devices, over_heads(): lax.ppermute(x, 'heads', [(i, i ^ k) for i in range(size)])  6.41 us
    ppermute x13, waiting for transfers between devices, swap(): return lax.ppermute(x, 'inner', [(0, 1), (1, 0)])  4.82 us
    ppermute x2, starting transfers between devices, both_ways(): return lax.ppermute(x, ('outer', 'inner'), up + down)  3.21 us
    unnamed x16, local copies, waits for them, and re-layouts  3.1 us
  transfers between devices with their start and end apart: 24, of which 15 were waited for; matrix products, arithmetic and copies ran while one was open for 0% of the time, Pallas kernels for 11%

profile of v2, /device:TPU:9, one launch (start us, length us, event | category | flops | bytes accessed | tf_op | source)
XLA Modules:
  0.0 63.9 jit_solution(14602008879674531108)
XLA Ops:
  1.9 1.0 %copy-done.2 = bf16[128,2048]{1,0:T(8,128)(2,1)S(1)} copy-done((bf16[128,2048]{1,0:T(8,128)(2,1)S(1)}, bf16[128,2048]{1,0:T(8,128)(2,1)}, u32[]{:S(2)}) %copy-start.2) | copy-done | bytes 524312
  2.9 1.0 %copy-done.3 = bf16[128,2048]{1,0:T(8,128)(2,1)S(1)} copy-done((bf16[128,2048]{1,0:T(8,128)(2,1)S(1)}, bf16[128,2048]{1,0:T(8,128)(2,1)}, u32[]{:S(2)}) %copy-start.3) | copy-done | bytes 524312
  6.4 1.3 %collective-permute-start.3 = (bf16[144,1024]{1,0:T(8,128)(2,1)S(1)}, bf16[144,1024]{1,0:T(8,128)(2,1)S(1)}, u32[]{:S(2)}, u32[]{:S(2)}) collective-permute-start(bf16[144,1024]{1,0:T(8,128)(2,1)S(1)} %get-tuple-element.37), channel_id=1, source_target_pairs={{0,8},{8,16},{16,24},{24,0},{1,9},{9,17},{17,25},{25,1},{2,10},{10... | collective-permute-start | bytes 884744 | tf_op jit(solution)/shard_map/ppermute | solution.py:301
  8.7 1.2 %shard_map.97 = (f32[256,1024]{1,0:T(8,128)S(1)}, bf16[256,1024]{1,0:T(8,128)(2,1)S(1)}, f32[256,1024]{1,0:T(8,128)S(1)}) custom-call(bf16[128,2048]{1,0:T(8,128)(2,1)S(1)} %copy-done.4, bf16[128,1024]{1,0:T(8,128)(2,1)S(1)} %get-tuple-element.34.k_own, bf16[128,1024]{1,0:T(8,128)(2,1)S(1)} %get-tuple-element.35.v_own, bf16[128,2048]{1,0:T(8,128)(2,1)S(1)} %copy-done.5, ...), custom_call_target="tpu_custom_call" | custom-call | bytes 3600000 | tf_op jit(solution)/shard_map/pallas_call | solution.py:281
  9.9 4.7 %collective-permute-done.3.t_near = bf16[144,1024]{1,0:T(8,128)(2,1)S(1)} collective-permute-done((bf16[144,1024]{1,0:T(8,128)(2,1)S(1)}, bf16[144,1024]{1,0:T(8,128)(2,1)S(1)}, u32[]{:S(2)}, u32[]{:S(2)}) %collective-permute-start.3) | collective-permute-done | bytes 294944 | tf_op jit(solution)/shard_map/ppermute | solution.py:301
  14.6 2.3 %collective-permute-start.8 = (bf16[128,2048]{1,0:T(8,128)(2,1)S(1)}, bf16[128,2048]{1,0:T(8,128)(2,1)S(1)}, u32[]{:S(2)}, u32[]{:S(2)}) collective-permute-start(bf16[128,2048]{1,0:T(8,128)(2,1)S(1)} %shard_map.98), channel_id=1, source_target_pairs={{0,8},{8,16},{16,24},{24,28},{12,4},{20,12},{28,20},{4,0},{1,9},{9... | collective-permute-start | bytes 1572872 | tf_op jit(solution)/shard_map/ppermute | solution.py:308
  16.9 0.9 %collective-permute-start.10 = (bf16[128,2048]{1,0:T(8,128)(2,1)S(1)}, bf16[128,2048]{1,0:T(8,128)(2,1)S(1)}, u32[]{:S(2)}, u32[]{:S(2)}) collective-permute-start(bf16[128,2048]{1,0:T(8,128)(2,1)S(1)} %collective-permute-done.7.k_got), channel_id=1, source_target_pairs={{0,8},{8,16},{16,24},{24,28},{12,4},{20,12},{28,20},{4,0},{1,9},{9... | collective-permute-start | bytes 1572872 | tf_op jit(solution)/shard_map/ppermute | solution.py:308
  18.2 1.2 %collective-permute-start.12 = (f32[1,256]{1,0:T(1,128)S(1)}, f32[1,256]{1,0:T(1,128)S(1)}, u32[]{:S(2)}, u32[]{:S(2)}) collective-permute-start(f32[1,256]{1,0:T(1,128)S(1)} %get-tuple-element.53), channel_id=1, source_target_pairs={{0,4},{4,0},{1,5},{5,1},{2,6},{6,2},{3,7},{7,3},{8,12},{12,8},{9,1... | collective-permute-start | bytes 3080 | tf_op jit(solution)/shard_map/ppermute | solution.py:296
  20.2 1.2 %collective-permute-start.13 = (f32[1,256]{1,0:T(1,128)S(1)}, f32[1,256]{1,0:T(1,128)S(1)}, u32[]{:S(2)}, u32[]{:S(2)}) collective-permute-start(f32[1,256]{1,0:T(1,128)S(1)} %add.6.s0), channel_id=1, source_target_pairs={{0,1},{1,0},{2,3},{3,2},{4,5},{5,4},{6,7},{7,6},{8,9},{9,8},{10,11... | collective-permute-start | bytes 3080 | tf_op jit(solution)/shard_map/ppermute | solution.py:315
  21.4 1.2 %collective-permute-start.14 = (f32[1,256]{1,0:T(1,128)S(1)}, f32[1,256]{1,0:T(1,128)S(1)}, u32[]{:S(2)}, u32[]{:S(2)}) collective-permute-start(f32[1,256]{1,0:T(1,128)S(1)} %add.6.s0), channel_id=1, source_target_pairs={{0,2},{1,3},{2,0},{3,1},{4,6},{5,7},{6,4},{7,5},{8,10},{9,11},{10,... | collective-permute-start | bytes 3080 | tf_op jit(solution)/shard_map/ppermute | solution.py:315
  23.0 1.2 %collective-permute-done.14.s2 = f32[1,256]{1,0:T(1,128)S(1)} collective-permute-done((f32[1,256]{1,0:T(1,128)S(1)}, f32[1,256]{1,0:T(1,128)S(1)}, u32[]{:S(2)}, u32[]{:S(2)}) %collective-permute-start.14) | collective-permute-done | bytes 1056 | tf_op jit(solution)/shard_map/ppermute | solution.py:315
  24.2 1.8 %collective-permute-done.15.s3 = f32[1,256]{1,0:T(1,128)S(1)} collective-permute-done((f32[1,256]{1,0:T(1,128)S(1)}, f32[1,256]{1,0:T(1,128)S(1)}, u32[]{:S(2)}, u32[]{:S(2)}) %collective-permute-start.15) | collective-permute-done | bytes 1056 | tf_op jit(solution)/shard_map/ppermute | solution.py:315
  26.3 2.1 %collective-permute-start.9 = (bf16[128,2048]{1,0:T(8,128)(2,1)S(1)}, bf16[128,2048]{1,0:T(8,128)(2,1)S(1)}, u32[]{:S(2)}, u32[]{:S(2)}) collective-permute-start(bf16[128,2048]{1,0:T(8,128)(2,1)S(1)} %collective-permute-done.8.mixed_own.near_first), channel_id=1, source_target_pairs={{0,4},{4,0},{1,5},{5,1},{2,6},{6,2},{3,7},{7,3},{8,12},{12,8},{9,1... | collective-permute-start | bytes 1572872 | tf_op jit(solution)/shard_map/ppermute | solution.py:296
  28.7 3.6 %collective-permute-start.11 = (bf16[128,2048]{1,0:T(8,128)(2,1)S(1)}, bf16[128,2048]{1,0:T(8,128)(2,1)S(1)}, u32[]{:S(2)}, u32[]{:S(2)}) collective-permute-start(bf16[128,2048]{1,0:T(8,128)(2,1)S(1)} %collective-permute-done.10.k_own.near_last), channel_id=1, source_target_pairs={{0,4},{4,0},{1,5},{5,1},{2,6},{6,2},{3,7},{7,3},{8,12},{12,8},{9,1... | collective-permute-start | bytes 1572872 | tf_op jit(solution)/shard_map/ppermute | solution.py:296
  32.3 1.5 %collective-permute-done.11.k_got.near_last_got = bf16[128,2048]{1,0:T(8,128)(2,1)S(1)} collective-permute-done((bf16[128,2048]{1,0:T(8,128)(2,1)S(1)}, bf16[128,2048]{1,0:T(8,128)(2,1)S(1)}, u32[]{:S(2)}, u32[]{:S(2)}) %collective-permute-start.11) | collective-permute-done | bytes 524320 | tf_op jit(solution)/shard_map/ppermute | solution.py:296
  34.6 2.4 %shard_map.101 = (bf16[8,256,512]{2,1,0:T(8,128)(2,1)S(1)}, f32[1,1024]{1,0:T(1,128)S(1)}) custom-call(bf16[128,2048]{1,0:T(8,128)(2,1)S(1)} %copy-done.1, bf16[128,2048]{1,0:T(8,128)(2,1)S(1)} %copy-done, bf16[128,2048]{1,0:T(8,128)(2,1)S(1)} %collective-permute-done.6.second.q_got, bf16[128,2048]{1,0:T(8,128)(2,1)S(1)} %collective-permute-done.7.k_got, ...), custom_call_target="tpu_custom_call" | custom-call | bytes 7500000 | tf_op jit(solution)/shard_map/pallas_call | solution.py:281
  36.9 9.7 %collective-permute-done.16.message.values.near = bf16[400,1024]{1,0:T(8,128)(2,1)S(1)} collective-permute-done((bf16[400,1024]{1,0:T(8,128)(2,1)S(1)}, bf16[400,1024]{1,0:T(8,128)(2,1)S(1)}, u32[]{:S(2)}, u32[]{:S(2)}) %collective-permute-start.16) | collective-permute-done | bytes 819232 | tf_op jit(solution)/shard_map/ppermute | solution.py:301
  47.2 3.2 %collective-permute-start.17 = (f32[1,128]{1,0:T(1,128)S(1)}, f32[1,128]{1,0:T(1,128)S(1)}, u32[]{:S(2)}, u32[]{:S(2)}) collective-permute-start(f32[1,128]{1,0:T(1,128)S(1)} %get-tuple-element.56), channel_id=1, source_target_pairs={{0,4},{4,0},{1,5},{5,1},{2,6},{6,2},{3,7},{7,3},{8,12},{12,8},{9,1... | collective-permute-start | bytes 1544 | tf_op jit(solution)/shard_map/ppermute | solution.py:296
  51.2 1.6 %collective-permute-start.18 = (f32[1,128]{1,0:T(1,128)S(1)}, f32[1,128]{1,0:T(1,128)S(1)}, u32[]{:S(2)}, u32[]{:S(2)}) collective-permute-start(f32[1,128]{1,0:T(1,128)S(1)} %add.7.s0), channel_id=1, source_target_pairs={{0,1},{1,0},{2,3},{3,2},{4,5},{5,4},{6,7},{7,6},{8,9},{9,8},{10,11... | collective-permute-start | bytes 1544 | tf_op jit(solution)/shard_map/ppermute | solution.py:315
  52.8 2.2 %collective-permute-start.19 = (f32[1,128]{1,0:T(1,128)S(1)}, f32[1,128]{1,0:T(1,128)S(1)}, u32[]{:S(2)}, u32[]{:S(2)}) collective-permute-start(f32[1,128]{1,0:T(1,128)S(1)} %add.7.s0), channel_id=1, source_target_pairs={{0,2},{1,3},{2,0},{3,1},{4,6},{5,7},{6,4},{7,5},{8,10},{9,11},{10,... | collective-permute-start | bytes 1544 | tf_op jit(solution)/shard_map/ppermute | solution.py:315
  55.0 0.9 %collective-permute-done.19.s2 = f32[1,128]{1,0:T(1,128)S(1)} collective-permute-done((f32[1,128]{1,0:T(1,128)S(1)}, f32[1,128]{1,0:T(1,128)S(1)}, u32[]{:S(2)}, u32[]{:S(2)}) %collective-permute-start.19) | collective-permute-done | bytes 544 | tf_op jit(solution)/shard_map/ppermute | solution.py:315
  55.9 2.4 %collective-permute-done.20.s3 = f32[1,128]{1,0:T(1,128)S(1)} collective-permute-done((f32[1,128]{1,0:T(1,128)S(1)}, f32[1,128]{1,0:T(1,128)S(1)}, u32[]{:S(2)}, u32[]{:S(2)}) %collective-permute-start.20) | collective-permute-done | bytes 544 | tf_op jit(solution)/shard_map/ppermute | solution.py:315
  58.5 2.1 %collective-permute-start.21 = (bf16[128,1024]{1,0:T(8,128)(2,1)S(1)}, bf16[128,1024]{1,0:T(8,128)(2,1)S(1)}, u32[]{:S(2)}, u32[]{:S(2)}) collective-permute-start(bf16[128,1024]{1,0:T(8,128)(2,1)S(1)} %get-tuple-element.58), channel_id=1, source_target_pairs={{0,4},{4,0},{1,5},{5,1},{2,6},{6,2},{3,7},{7,3},{8,12},{12,8},{9,1... | collective-permute-start | bytes 786440 | tf_op jit(solution)/shard_map/ppermute | solution.py:296
  63.0 0.8 %shard_map.108 = bf16[128,2048]{1,0:T(8,128)(2,1)} custom-call(bf16[128,1024]{1,0:T(8,128)(2,1)S(1)} %get-tuple-element.64.kept, bf16[128,1024]{1,0:T(8,128)(2,1)S(1)} %collective-permute-done.23.got), custom_call_target="tpu_custom_call" | custom-call | bytes 1500000 | tf_op jit(solution)/shard_map/pallas_call | solution.py:281
  (57 shorter events, 11.5 us)
Async XLA Ops:
  0.7 4.1 %collective-permute-start = (bf16[128,2048]{1,0:T(8,128)(2,1)}, bf16[128,2048]{1,0:T(8,128)(2,1)S(1)}, u32[]{:S(2)}, u32[]{:S(2)}) collective-permute-start(bf16[128,2048]{1,0:T(8,128)(2,1)} %key.1), channel_id=1, source_target_pairs={{0,4},{4,0},{1,5},{5,1},{2,6},{6,2},{3,7},{7,3},{8,12},{12,8},{9,1... | collective-permute-start | bytes 1572872 | tf_op jit(solution)/shard_map/ppermute | solution.py:296
  1.4 3.3 %collective-permute-start.1 = (bf16[128,2048]{1,0:T(8,128)(2,1)}, bf16[128,2048]{1,0:T(8,128)(2,1)S(1)}, u32[]{:S(2)}, u32[]{:S(2)}) collective-permute-start(bf16[128,2048]{1,0:T(8,128)(2,1)} %value.1), channel_id=1, source_target_pairs={{0,4},{4,0},{1,5},{5,1},{2,6},{6,2},{3,7},{7,3},{8,12},{12,8},{9,1... | collective-permute-start | bytes 1572872 | tf_op jit(solution)/shard_map/ppermute | solution.py:296
  1.5 3.2 %collective-permute-start.2 = (s32[1,128]{1,0:T(1,128)}, s32[1,128]{1,0:T(1,128)S(1)}, u32[]{:S(2)}, u32[]{:S(2)}) collective-permute-start(s32[1,128]{1,0:T(1,128)} %bitcast.1), channel_id=1, source_target_pairs={{0,4},{4,0},{1,5},{5,1},{2,6},{6,2},{3,7},{7,3},{8,12},{12,8},{9,1... | collective-permute-start | bytes 1544 | tf_op jit(solution)/shard_map/ppermute | solution.py:296
  5.2 2.4 %collective-permute-start.6 = (bf16[128,2048]{1,0:T(8,128)(2,1)S(1)}, bf16[128,2048]{1,0:T(8,128)(2,1)S(1)}, u32[]{:S(2)}, u32[]{:S(2)}) collective-permute-start(bf16[128,2048]{1,0:T(8,128)(2,1)S(1)} %copy-done.1), channel_id=1, source_target_pairs={{0,4},{4,0},{1,5},{5,1},{2,6},{6,2},{3,7},{7,3},{8,12},{12,8},{9,1... | collective-permute-start | bytes 1572872 | tf_op jit(solution)/shard_map/ppermute | solution.py:296
  5.7 2.3 %collective-permute-start.4 = (bf16[128,2048]{1,0:T(8,128)(2,1)S(1)}, bf16[128,2048]{1,0:T(8,128)(2,1)S(1)}, u32[]{:S(2)}, u32[]{:S(2)}) collective-permute-start(bf16[128,2048]{1,0:T(8,128)(2,1)S(1)} %copy-done.4), channel_id=1, source_target_pairs={{0,4},{4,0},{1,5},{5,1},{2,6},{6,2},{3,7},{7,3},{8,12},{12,8},{9,1... | collective-permute-start | bytes 1572872 | tf_op jit(solution)/shard_map/ppermute | solution.py:296
  5.8 2.9 %collective-permute-start.5 = (bf16[128,2048]{1,0:T(8,128)(2,1)S(1)}, bf16[128,2048]{1,0:T(8,128)(2,1)S(1)}, u32[]{:S(2)}, u32[]{:S(2)}) collective-permute-start(bf16[128,2048]{1,0:T(8,128)(2,1)S(1)} %copy-done.5), channel_id=1, source_target_pairs={{0,4},{4,0},{1,5},{5,1},{2,6},{6,2},{3,7},{7,3},{8,12},{12,8},{9,1... | collective-permute-start | bytes 1572872 | tf_op jit(solution)/shard_map/ppermute | solution.py:296
  6.2 8.4 %collective-permute-start.7 = (bf16[128,2048]{1,0:T(8,128)(2,1)S(1)}, bf16[128,2048]{1,0:T(8,128)(2,1)S(1)}, u32[]{:S(2)}, u32[]{:S(2)}) collective-permute-start(bf16[128,2048]{1,0:T(8,128)(2,1)S(1)} %copy-done), channel_id=1, source_target_pairs={{0,4},{4,0},{1,5},{5,1},{2,6},{6,2},{3,7},{7,3},{8,12},{12,8},{9,1... | collective-permute-start | bytes 1572872 | tf_op jit(solution)/shard_map/ppermute | solution.py:296
  6.4 8.2 %collective-permute-start.3 = (bf16[144,1024]{1,0:T(8,128)(2,1)S(1)}, bf16[144,1024]{1,0:T(8,128)(2,1)S(1)}, u32[]{:S(2)}, u32[]{:S(2)}) collective-permute-start(bf16[144,1024]{1,0:T(8,128)(2,1)S(1)} %get-tuple-element.37), channel_id=1, source_target_pairs={{0,8},{8,16},{16,24},{24,0},{1,9},{9,17},{17,25},{25,1},{2,10},{10... | collective-permute-start | bytes 884744 | tf_op jit(solution)/shard_map/ppermute | solution.py:301
  14.6 11.7 %collective-permute-start.8 = (bf16[128,2048]{1,0:T(8,128)(2,1)S(1)}, bf16[128,2048]{1,0:T(8,128)(2,1)S(1)}, u32[]{:S(2)}, u32[]{:S(2)}) collective-permute-start(bf16[128,2048]{1,0:T(8,128)(2,1)S(1)} %shard_map.98), channel_id=1, source_target_pairs={{0,8},{8,16},{16,24},{24,28},{12,4},{20,12},{28,20},{4,0},{1,9},{9... | collective-permute-start | bytes 1572872 | tf_op jit(solution)/shard_map/ppermute | solution.py:308
  16.9 11.7 %collective-permute-start.10 = (bf16[128,2048]{1,0:T(8,128)(2,1)S(1)}, bf16[128,2048]{1,0:T(8,128)(2,1)S(1)}, u32[]{:S(2)}, u32[]{:S(2)}) collective-permute-start(bf16[128,2048]{1,0:T(8,128)(2,1)S(1)} %collective-permute-done.7.k_got), channel_id=1, source_target_pairs={{0,8},{8,16},{16,24},{24,28},{12,4},{20,12},{28,20},{4,0},{1,9},{9... | collective-permute-start | bytes 1572872 | tf_op jit(solution)/shard_map/ppermute | solution.py:308
  18.2 2.0 %collective-permute-start.12 = (f32[1,256]{1,0:T(1,128)S(1)}, f32[1,256]{1,0:T(1,128)S(1)}, u32[]{:S(2)}, u32[]{:S(2)}) collective-permute-start(f32[1,256]{1,0:T(1,128)S(1)} %get-tuple-element.53), channel_id=1, source_target_pairs={{0,4},{4,0},{1,5},{5,1},{2,6},{6,2},{3,7},{7,3},{8,12},{12,8},{9,1... | collective-permute-start | bytes 3080 | tf_op jit(solution)/shard_map/ppermute | solution.py:296
  20.2 2.7 %collective-permute-start.13 = (f32[1,256]{1,0:T(1,128)S(1)}, f32[1,256]{1,0:T(1,128)S(1)}, u32[]{:S(2)}, u32[]{:S(2)}) collective-permute-start(f32[1,256]{1,0:T(1,128)S(1)} %add.6.s0), channel_id=1, source_target_pairs={{0,1},{1,0},{2,3},{3,2},{4,5},{5,4},{6,7},{7,6},{8,9},{9,8},{10,11... | collective-permute-start | bytes 3080 | tf_op jit(solution)/shard_map/ppermute | solution.py:315
  21.4 2.7 %collective-permute-start.14 = (f32[1,256]{1,0:T(1,128)S(1)}, f32[1,256]{1,0:T(1,128)S(1)}, u32[]{:S(2)}, u32[]{:S(2)}) collective-permute-start(f32[1,256]{1,0:T(1,128)S(1)} %add.6.s0), channel_id=1, source_target_pairs={{0,2},{1,3},{2,0},{3,1},{4,6},{5,7},{6,4},{7,5},{8,10},{9,11},{10,... | collective-permute-start | bytes 3080 | tf_op jit(solution)/shard_map/ppermute | solution.py:315
  22.7 3.3 %collective-permute-start.15 = (f32[1,256]{1,0:T(1,128)S(1)}, f32[1,256]{1,0:T(1,128)S(1)}, u32[]{:S(2)}, u32[]{:S(2)}) collective-permute-start(f32[1,256]{1,0:T(1,128)S(1)} %add.6.s0), channel_id=1, source_target_pairs={{0,3},{1,2},{2,1},{3,0},{4,7},{5,6},{6,5},{7,4},{8,11},{9,10},{10,... | collective-permute-start | bytes 3080 | tf_op jit(solution)/shard_map/ppermute | solution.py:315
  26.2 20.4 %collective-permute-start.16 = (bf16[400,1024]{1,0:T(8,128)(2,1)S(1)}, bf16[400,1024]{1,0:T(8,128)(2,1)S(1)}, u32[]{:S(2)}, u32[]{:S(2)}) collective-permute-start(bf16[400,1024]{1,0:T(8,128)(2,1)S(1)} %shard_map.102.values), channel_id=1, source_target_pairs={{0,8},{8,16},{16,24},{24,0},{1,9},{9,17},{17,25},{25,1},{2,10},{10... | collective-permute-start | bytes 2457608 | tf_op jit(solution)/shard_map/ppermute | solution.py:301
  26.3 6.0 %collective-permute-start.9 = (bf16[128,2048]{1,0:T(8,128)(2,1)S(1)}, bf16[128,2048]{1,0:T(8,128)(2,1)S(1)}, u32[]{:S(2)}, u32[]{:S(2)}) collective-permute-start(bf16[128,2048]{1,0:T(8,128)(2,1)S(1)} %collective-permute-done.8.mixed_own.near_first), channel_id=1, source_target_pairs={{0,4},{4,0},{1,5},{5,1},{2,6},{6,2},{3,7},{7,3},{8,12},{12,8},{9,1... | collective-permute-start | bytes 1572872 | tf_op jit(solution)/shard_map/ppermute | solution.py:296
  28.7 5.1 %collective-permute-start.11 = (bf16[128,2048]{1,0:T(8,128)(2,1)S(1)}, bf16[128,2048]{1,0:T(8,128)(2,1)S(1)}, u32[]{:S(2)}, u32[]{:S(2)}) collective-permute-start(bf16[128,2048]{1,0:T(8,128)(2,1)S(1)} %collective-permute-done.10.k_own.near_last), channel_id=1, source_target_pairs={{0,4},{4,0},{1,5},{5,1},{2,6},{6,2},{3,7},{7,3},{8,12},{12,8},{9,1... | collective-permute-start | bytes 1572872 | tf_op jit(solution)/shard_map/ppermute | solution.py:296
  46.8 13.7 %collective-permute-start.22 = (bf16[144,1024]{1,0:T(8,128)(2,1)S(1)}, bf16[144,1024]{1,0:T(8,128)(2,1)S(1)}, u32[]{:S(2)}, u32[]{:S(2)}) collective-permute-start(bf16[144,1024]{1,0:T(8,128)(2,1)S(1)} %shard_map.106), channel_id=1, source_target_pairs={{0,8},{8,16},{16,24},{24,0},{1,9},{9,17},{17,25},{25,1},{2,10},{10... | collective-permute-start | bytes 884744 | tf_op jit(solution)/shard_map/ppermute | solution.py:301
  47.2 4.0 %collective-permute-start.17 = (f32[1,128]{1,0:T(1,128)S(1)}, f32[1,128]{1,0:T(1,128)S(1)}, u32[]{:S(2)}, u32[]{:S(2)}) collective-permute-start(f32[1,128]{1,0:T(1,128)S(1)} %get-tuple-element.56), channel_id=1, source_target_pairs={{0,4},{4,0},{1,5},{5,1},{2,6},{6,2},{3,7},{7,3},{8,12},{12,8},{9,1... | collective-permute-start | bytes 1544 | tf_op jit(solution)/shard_map/ppermute | solution.py:296
  51.2 3.8 %collective-permute-start.18 = (f32[1,128]{1,0:T(1,128)S(1)}, f32[1,128]{1,0:T(1,128)S(1)}, u32[]{:S(2)}, u32[]{:S(2)}) collective-permute-start(f32[1,128]{1,0:T(1,128)S(1)} %add.7.s0), channel_id=1, source_target_pairs={{0,1},{1,0},{2,3},{3,2},{4,5},{5,4},{6,7},{7,6},{8,9},{9,8},{10,11... | collective-permute-start | bytes 1544 | tf_op jit(solution)/shard_map/ppermute | solution.py:315
  52.8 3.1 %collective-permute-start.19 = (f32[1,128]{1,0:T(1,128)S(1)}, f32[1,128]{1,0:T(1,128)S(1)}, u32[]{:S(2)}, u32[]{:S(2)}) collective-permute-start(f32[1,128]{1,0:T(1,128)S(1)} %add.7.s0), channel_id=1, source_target_pairs={{0,2},{1,3},{2,0},{3,1},{4,6},{5,7},{6,4},{7,5},{8,10},{9,11},{10,... | collective-permute-start | bytes 1544 | tf_op jit(solution)/shard_map/ppermute | solution.py:315
  55.0 3.3 %collective-permute-start.20 = (f32[1,128]{1,0:T(1,128)S(1)}, f32[1,128]{1,0:T(1,128)S(1)}, u32[]{:S(2)}, u32[]{:S(2)}) collective-permute-start(f32[1,128]{1,0:T(1,128)S(1)} %add.7.s0), channel_id=1, source_target_pairs={{0,3},{1,2},{2,1},{3,0},{4,7},{5,6},{6,5},{7,4},{8,11},{9,10},{10,... | collective-permute-start | bytes 1544 | tf_op jit(solution)/shard_map/ppermute | solution.py:315
  58.5 3.2 %collective-permute-start.21 = (bf16[128,1024]{1,0:T(8,128)(2,1)S(1)}, bf16[128,1024]{1,0:T(8,128)(2,1)S(1)}, u32[]{:S(2)}, u32[]{:S(2)}) collective-permute-start(bf16[128,1024]{1,0:T(8,128)(2,1)S(1)} %get-tuple-element.58), channel_id=1, source_target_pairs={{0,4},{4,0},{1,5},{5,1},{2,6},{6,2},{3,7},{7,3},{8,12},{12,8},{9,1... | collective-permute-start | bytes 786440 | tf_op jit(solution)/shard_map/ppermute | solution.py:296
  61.4 1.6 %collective-permute-start.23 = (bf16[128,1024]{1,0:T(8,128)(2,1)S(1)}, bf16[128,1024]{1,0:T(8,128)(2,1)S(1)}, u32[]{:S(2)}, u32[]{:S(2)}) collective-permute-start(bf16[128,1024]{1,0:T(8,128)(2,1)S(1)} %get-tuple-element.65), channel_id=1, source_target_pairs={{0,4},{4,0},{1,5},{5,1},{2,6},{6,2},{3,7},{7,3},{8,12},{12,8},{9,1... | collective-permute-start | bytes 786440 | tf_op jit(solution)/shard_map/ppermute | solution.py:296
  (8 other events, 18.1 us)

commit v3 on v2

--- a/solution.py
+++ b/solution.py
@@ -111,7 +111,7 @@
 
 def intra_kernel(
     q_own, k_own, v_own, g_own, q_got, k_got, v_got, g_got, gain, docs,
-    intra, q_out, gate_out, k_all, v_all, g_all,
+    intra, q_out, gate_out, squares, k_all, v_all, g_all,
 ):
     n, width = intra.shape
     tb = n // 2
@@ -126,41 +126,39 @@
     same = jnp.concatenate([d, d], axis=1) == docs[...]
     visible = same & (row >= col)
     gains = gain[:, mine(width)].astype(F32)
+    total = jnp.zeros((n, DH), F32)
     for h in range(width // DH):
         cols = slice(h * DH, (h + 1) * DH)
         scores = dot(q_out[:, cols], k_all[:, cols], ((1,), (1,)))
         weights = jnp.where(visible, scores, 0.0).astype(BF16)
-        intra[:, cols] = dot(weights, v_all[:, cols])
+        value = dot(weights, v_all[:, cols])
+        intra[:, cols] = value
+        total += value * value
         gate = jax.nn.sigmoid(g_all[:, cols].astype(F32))
         gate_out[:, cols] = gate * gains[:, cols]
-
-
-def mixed_kernel(intra, q, t_near, docs, mixed, squares):
+    squares[...] = lane_sums(total)
+
+
+def mixed_kernel(intra, q, t_near, t_far, docs, mixed, squares):
     n, width = q.shape
+    tb = n // 2
     seen = column(docs[...]) == message_docs(t_near, chip() >= 1)[2]
+    both = spanning(t_near, t_far, docs)
     total = jnp.zeros((n, DH), F32)
     for h in range(width // DH):
         cols = slice(h * DH, (h + 1) * DH)
-        carried = dot(q[:, cols], t_near[:DH, cols])
-        value = intra[:, cols] + jnp.where(seen, carried, 0.0)
+        value = intra[:, cols] + jnp.where(seen, dot(q[:, cols], t_near[:DH, cols]), 0.0)
+        first = jnp.where(both, dot(q[:tb, cols], t_far[:DH, cols]), 0.0)
+        value = jnp.concatenate([value[:tb] + first, value[tb:]], axis=0)
         mixed[:, cols] = value
         total += value * value
     squares[...] = lane_sums(total)
 
 
-def second_kernel(mixed, q, t_near, message, docs, fixed, squares):
-    n, width = fixed.shape
+def spanning(t_near, t_far, docs):
     near = message_docs(t_near, chip() >= 1)[2]
-    far = message_docs(message, chip() >= 2)[2]
-    seen = (column(docs[:, :n]) == near) & (near == far)
-    total = jnp.zeros((n, DH), F32)
-    for h in range(width // DH):
-        cols = slice(h * DH, (h + 1) * DH)
-        carried = dot(q[:n, cols], message[2 * n : 2 * n + DH, cols])
-        value = mixed[:n, cols] + jnp.where(seen, carried, 0.0)
-        fixed[:, cols] = value
-        total += value * value
-    squares[...] = lane_sums(total)
+    far = message_docs(t_far, chip() >= 2)[2]
+    return (column(docs[:, : docs.shape[1] // 2]) == near) & (near == far)
 
 
 def normed(columns, mixed, gate, sums, out):
@@ -170,18 +168,14 @@
         out[:, cols] = (mixed[:, cols] * scale * gate[:, cols]).astype(BF16)
 
 
-def norm_kernel(columns, mixed, gate, s0, s1, s2, s3, t_near, out):
-    n = mixed.shape[0]
-    normed(columns, mixed, gate, (s0, s1, s2, s3), out.at[pl.ds(0, n)])
-    out[n:, :] = t_near[...]
-
-
-def output_kernel(columns, fixed, gate, s0, s1, s2, s3, values, first, out, sent):
-    tb = fixed.shape[0]
-    normed(columns, fixed, gate.at[pl.ds(0, tb)], (s0, s1, s2, s3), first)
-    top = inner() == 0
-    out[...] = jnp.where(top, first[...], values[tb : 2 * tb, :])
-    sent[...] = jnp.where(top, values[tb : 2 * tb, :], first[...])
+def norm_kernel(columns, mixed, gate, s0, s1, s2, out):
+    normed(columns, mixed, gate, (s0, s1, s2), out)
+
+
+def output_kernel(columns, mixed, gate, s0, s1, s2, out, kept, sent):
+    tb = kept.shape[0]
+    normed(columns, mixed, gate, (s0, s1, s2), out)
+    kept[...], sent[...] = in_order(out[:tb, :], out[tb:, :])
 
 
 def softmax_part(q, k, visible):
@@ -198,26 +192,30 @@
     out[...] = jnp.where(inner() == 0, first[...], second[...])
 
 
-def far_kernel(mixed_own, mixed_got, k_own, k_got, t_near, docs, weights, lse):
-    tb, local = k_own.shape
-    width = local // 2
+def far_kernel(own, got, k_own, k_got, t_near, docs, weights, lse, k_all):
+    tb, width = k_own.shape[0], k_all.shape[1]
+    n = 2 * tb
+    cols = mine(width)
+    k_all[:tb, :], queries = in_order(own[:, cols], got[:, cols])
+    place(k_all.at[tb:], k_own, k_got)
     near = message_docs(t_near, chip() >= 1)
-    last = docs[:, 2 * tb - 1 :]
-    visible = jnp.broadcast_to((near[1] == last) & (near[2] == last), (tb, tb))
-    for h in range(width // DH):
-        cols = head(width, h)
-        queries = in_order(mixed_own[:, cols], mixed_got[:, cols])[1]
-        keys = in_order(k_own[:, cols], k_got[:, cols])[0]
-        weights[h], top = softmax_part(queries, keys, visible)
-        lse[:, h * DH : (h + 1) * DH] = as_row(top)
-
-
-def answer_kernel(weights, lse, values, out):
-    tb = weights.shape[1]
-    width = values.shape[1]
-    for h in range(width // DH):
-        cols = slice(h * DH, (h + 1) * DH)
-        out[:tb, cols] = dot(weights[h], values[tb : 2 * tb, cols]).astype(BF16)
+    last = docs[:, n - 1 :]
+    key_docs = jnp.concatenate([near[1], docs[...]], axis=1)
+    visible = jnp.broadcast_to((key_docs == last) & (near[2] == last), (tb, 3 * tb))
+    for h in range(width // DH):
+        cols = slice(h * DH, (h + 1) * DH)
+        weights[h], top = softmax_part(queries[:, cols], k_all[:, cols], visible)
+        lse[:, cols] = as_row(top)
+
+
+def answer_kernel(weights, lse, near_values, values, out):
+    n, width = values.shape
+    tb = n // 2
+    for h in range(width // DH):
+        cols = slice(h * DH, (h + 1) * DH)
+        total = dot(weights[h, :, :tb], near_values[tb:, cols])
+        total += dot(weights[h, :, tb:], values[:, cols])
+        out[:tb, cols] = total.astype(BF16)
     high, middle, low = split(lse[...])
     rows = [high, middle, low, jnp.zeros((PAD - 3, width), BF16)]
     out[tb:, :] = jnp.concatenate([r.astype(F32) for r in rows], axis=0).astype(BF16)
@@ -225,7 +223,7 @@
 
 def weights_kernel(
     q_own, k_own, q_got, k_got, near_first, near_first_got, near_last, near_last_got,
-    t_near, docs, weights, lse, q_all, k_all,
+    t_near, docs, weights, first_weights, first_lse, q_all, k_all,
 ):
     n, width = q_all.shape
     tb = n // 2
@@ -244,31 +242,44 @@
     visible = same & (row >= col)
     for h in range(width // DH):
         cols = slice(h * DH, (h + 1) * DH)
-        weights[h], top = softmax_part(q_all[:, cols], k_all[:, cols], visible)
-        lse[:, cols] = as_row(top[:tb])
-
-
-def attend_kernel(weights, lse, answer, near, first, values, t_near, docs, out, sent):
-    tb, width = first.shape
-    n = 2 * tb
-    near_last = message_docs(t_near, chip() >= 2)[2]
-    asked = column(docs[:, :tb]) == near_last
-    for h in range(width // DH):
-        cols = slice(h * DH, (h + 1) * DH)
-        total = dot(weights[h, :, :n], near[:n, cols])
-        total += dot(weights[h, :, n : n + tb], first[:, cols])
-        total += dot(weights[h, :, n + tb :], values[tb:n, cols])
+        weights[h], _ = softmax_part(q_all[:, cols], k_all[:, cols], visible)
+        block = slice(n, n + tb)
+        first_weights[h], top = softmax_part(
+            q_all[:tb, cols], k_all[block, cols], visible[:tb, block]
+        )
+        first_lse[:, cols] = as_row(top)
+
+
+def attend_kernel(weights, near, values, kept, sent):
+    n, width = values.shape
+    tb = n // 2
+    top = inner() == 0
+    for h in range(width // DH):
+        cols = slice(h * DH, (h + 1) * DH)
+        total = dot(weights[h, :, :n], near[:, cols])
+        total += dot(weights[h, :, n:], values[:, cols])
+        first, last = total[:tb].astype(BF16), total[tb:].astype(BF16)
+        kept[:, cols] = jnp.where(top, first, last)
+        sent[:, cols] = jnp.where(top, last, first)
+
+
+def merge_kernel(
+    weights, lse, values, answer, t_near, t_far, docs, kept, sent, new_kept, new_sent
+):
+    tb, width = kept.shape
+    asked = spanning(t_near, t_far, docs)
+    top_block = inner() == 0
+    for h in range(width // DH):
+        cols = slice(h * DH, (h + 1) * DH)
         far_lse = sum(answer[tb + i : tb + i + 1, cols].astype(F32) for i in range(3))
-        far_lse = jnp.where(asked, column(far_lse), NONE)
-        here_lse = column(lse[:, cols])
-        top = jnp.maximum(far_lse, here_lse)
-        far, here = jnp.exp(far_lse - top), jnp.exp(here_lse - top)
-        part = jnp.where(asked, far * answer[:tb, cols].astype(F32), 0.0)
-        upper = ((here * total[:tb] + part) / (here + far)).astype(BF16)
-        lower = total[tb:].astype(BF16)
-        is_first = inner() == 0
-        out[:, cols] = jnp.where(is_first, upper, lower)
-        sent[:, cols] = jnp.where(is_first, lower, upper)
+        top = jnp.maximum(far_lse, lse[:, cols])
+        far, here = jnp.exp(far_lse - top), jnp.exp(lse[:, cols] - top)
+        far, here = column(far / (far + here)), column(here / (far + here))
+        merged = here * dot(weights[h], values[:tb, cols]) + far * answer[:tb, cols].astype(F32)
+        before, other = in_order(kept[:, cols], sent[:, cols])
+        rows = jnp.where(asked, merged.astype(BF16), before)
+        new_kept[:, cols] = jnp.where(top_block, rows, other)
+        new_sent[:, cols] = jnp.where(top_block, other, rows)
 
 
 def join_kernel(kept, got, out):
@@ -296,8 +307,10 @@
     return lax.ppermute(x, "inner", [(0, 1), (1, 0)])
 
 
-def next_chip(x):
+def next_chip(x, line=False):
     chips = lax.axis_size("outer")
+    if line:
+        return lax.ppermute(x, "outer", [(i, i + 1) for i in range(chips - 1)])
     return lax.ppermute(x, "outer", [(i, (i + 1) % chips) for i in range(chips)])
 
 
@@ -308,15 +321,17 @@
     return lax.ppermute(x, ("outer", "inner"), up + down)
 
 
+def other_heads(x):
+    size = lax.axis_size("heads")
+    if size != 4:
+        return [lax.psum(x, "heads") - x, jnp.zeros_like(x)]
+    one = lax.ppermute(x, "heads", [(i, i ^ 1) for i in range(size)])
+    return [one, lax.ppermute(x + one, "heads", [(i, i ^ 2) for i in range(size)])]
+
+
 def over_heads(x):
-    size = lax.axis_size("heads")
     x = x + swap(x)
-    if size == 4:
-        others = [lax.ppermute(x, "heads", [(i, i ^ k) for i in range(size)]) for k in (1, 2, 3)]
-        return [x, *others]
-    total = lax.psum(x, "heads")
-    zero = jnp.zeros_like(total)
-    return [total, zero, zero, zero]
+    return [x, *other_heads(x)]
 
 
 def per_device(
@@ -338,10 +353,7 @@
     got_docs = swap(own_docs)
     lk_got, lv_got = swap(lin_key), swap(lin_value)
     keys, values, own_docs = run(
-        cut_kernel,
-        [lin_key, lin_value, own_docs],
-        [block, block, ((1, tb), F32)],
-        us=2.0,
+        cut_kernel, [lin_key, lin_value, own_docs], [block, block, ((1, tb), F32)], us=2.0
     )
     t_msg, docs = run(
         state_kernel,
@@ -349,73 +361,75 @@
         [((DH + PAD, width), BF16), ((1, n), F32)],
     )
     t_near = next_chip(t_msg)
+    raw_key = soft_key
     lin_query, gate_input, soft_query, soft_key, _ = tie(
         (lin_query, gate_input, soft_query, soft_key, t_msg)
     )
     lq_got, g_got = swap(lin_query), swap(gate_input)
     sq_got, sk_got = swap(soft_query), swap(soft_key)
-    out_first = run(pick_kernel, [soft_key, sq_got], [((tb, local), BF16)], us=0.3)
-    intra, queries, gate = run(
+    intra, queries, gate, squares = run(
         intra_kernel,
         [
             lin_query, keys, values, gate_input, lq_got, lk_got, lv_got, g_got,
             norm_gain[None], docs,
         ],
-        [((n, width), F32), whole, ((n, width), F32)],
+        [((n, width), F32), whole, ((n, width), F32), ((1, n), F32)],
         [scratch] * 3,
         us=1.2,
     )
-    t_near, intra, out_first, out_last = tie((t_near, intra, out_first, sk_got))
-    first_own, last_own = both_ways(out_first), both_ways(out_last)
+    chip_squares = squares + swap(squares)
+    sums = [chip_squares, *other_heads(chip_squares)]
+    t_far = next_chip(t_near, line=True)
+    sums, t_far = tie((sums, t_far))
+    early = run(functools.partial(norm_kernel, columns), [intra, gate, *sums], [whole], us=0.3)
+    first_own = both_ways(tie((raw_key, t_msg))[0])
+    out_last = run(pick_kernel, [sk_got, sq_got], [((tb, local), BF16)], us=0.3)
+    last_own = both_ways(tie((out_last, chip_squares))[0])
+    near_values = next_chip(early, line=True)
+    mixed, squares = run(
+        mixed_kernel, [intra, queries, t_near, t_far, docs], [((n, width), F32), ((1, n), F32)]
+    )
+    values, lin_kept, lin_sent = run(
+        functools.partial(output_kernel, columns),
+        [mixed, gate, *over_heads(squares)],
+        [whole, block, block],
+        us=0.3,
+    )
     first_got, last_got = swap(first_own), swap(last_own)
-    mixed, squares = run(
-        mixed_kernel, [intra, queries, t_near, docs], [((n, width), F32), ((1, n), F32)]
-    )
-    values = run(
-        functools.partial(norm_kernel, columns),
-        [mixed, gate, *over_heads(squares), t_near],
-        [((n + DH + PAD, width), BF16)],
-        us=0.3,
-    )
-    near_values = next_chip(values)
     far_weights, far_lse = run(
         far_kernel,
-        [first_own, first_got, last_own, last_got, t_near, docs],
-        [((heads, tb, tb), BF16), ((1, width), F32)],
-    )
-    weights, lse = run(
+        [last_own, last_got, soft_key, sk_got, t_near, docs],
+        [((heads, tb, 3 * tb), BF16), ((1, width), F32)],
+        [pltpu.VMEM((3 * tb, width), BF16)],
+        us=1.0,
+    )
+    far_weights, near_values = tie((far_weights, near_values))
+    weights, first_weights, first_lse = run(
         weights_kernel,
         [
             soft_query, soft_key, sq_got, sk_got, first_own, first_got, last_own, last_got,
             t_near, docs,
         ],
-        [((heads, n, 2 * n), BF16), ((1, width), F32)],
+        [((heads, n, 2 * n), BF16), ((heads, tb, tb), BF16), ((1, width), F32)],
         [scratch, pltpu.VMEM((2 * n, width), BF16)],
         us=2.5,
     )
-    far_weights, weights, near_values = tie((far_weights, weights, near_values))
+    values, near_values = tie((values, near_values))
     answer = next_chip(
         run(
-            answer_kernel, [far_weights, far_lse, near_values], [((tb + PAD, width), BF16)], us=0.3
-        )
-    )
-    fixed, squares = run(
-        second_kernel,
-        [mixed, queries, t_near, near_values, docs],
-        [((tb, width), F32), ((1, tb), F32)],
-    )
-    first, kept, sent = run(
-        functools.partial(output_kernel, columns),
-        [fixed, gate, *over_heads(squares), values],
-        [block] * 3,
-        us=0.3,
-    )
-    linear_out = joined(kept, sent)
+            answer_kernel,
+            [far_weights, far_lse, near_values, values],
+            [((tb + PAD, width), BF16)],
+            us=0.3,
+        ),
+        line=True,
+    )
+    linear_out = joined(lin_kept, lin_sent)
+    kept, sent = run(attend_kernel, [weights, near_values, values], [block, block], us=0.8)
     kept, sent = run(
-        attend_kernel,
-        [weights, lse, answer, near_values, first, values, t_near, docs],
+        merge_kernel,
+        [first_weights, first_lse, values, answer, t_near, t_far, docs, kept, sent],
         [block, block],
-        us=1.0,
     )
     return linear_out, joined(kept, sent)
 

time: 64.1 us -> 58.9 us (0.919)
  waiting for transfers between devices: 25.9 us -> 19.3 us
  Pallas kernels: 8.73 us -> 9.81 us
    ppermute x3 -> x1, waiting for transfers between devices: 14.4 us -> 4.37 us  [next_chip(): lax.ppermute(x, 'outer', [(i, (i + 1) % chips) for i in range(chips)])]
    ppermute x6 -> x7, starting transfers between devices: 6.45 us -> 13.9 us  [the longest x3 9.32 us: next_chip(): return lax.ppermute(x, 'outer', [(i, i + 1) for i in range(chips - 1)])]
    ppermute x6 -> x7, waiting for transfers between devices: 6.41 us -> 12.3 us  [the longest x3 6 us: next_chip(): return lax.ppermute(x, 'outer', [(i, i + 1) for i in range(chips - 1)])]
    ppermute x13, starting transfers between devices: 14.2 us -> 9.49 us  [swap(): return lax.ppermute(x, 'inner', [(0, 1), (1, 0)])]
    ppermute x2, starting transfers between devices: 3.21 us -> 0.42 us  [both_ways(): return lax.ppermute(x, ('outer', 'inner'), up + down)]
    ppermute x13, waiting for transfers between devices: 4.82 us -> 2.7 us  [swap(): return lax.ppermute(x, 'inner', [(0, 1), (1, 0)])]
    pallas_call x14, Pallas kernels: 8.73 us -> 9.81 us  [run(): pl.pallas_call(kernel, out_shape=[jax.ShapeDtypeStruct(*o) for o in outs]...]
    ppermute x3 -> x1, starting transfers between devices: 1.42 us -> 1.3 us  [next_chip(): lax.ppermute(x, 'outer', [(i, (i + 1) % chips) for i in range(chips)])]
  transfers between devices with their start and end apart: 24 -> 23, of which waited for: 15 -> 12; matrix products, arithmetic and copies ran while one was open for 0% -> 0% of each run, Pallas kernels for 11% -> 15%
where the time goes in v3:
time: 58.9 us; the launch traced here: 58.4 us
  starting transfers between devices  25.1 us (43%)
  waiting for transfers between devices  19.3 us (33%)
  Pallas kernels  9.81 us (17%)
  local copies, waits for them, and re-layouts  3.31 us (6%)
  between operations  0.82 us (1%)
    pallas_call x14, Pallas kernels, run(): pl.pallas_call(kernel, out_shape=[jax.ShapeDtypeStruct(*o) for o in outs]...  9.81 us
    ppermute x13, starting transfers between devices, swap(): return lax.ppermute(x, 'inner', [(0, 1), (1, 0)])  9.49 us
    ppermute x3, starting transfers between devices, next_chip(): return lax.ppermute(x, 'outer', [(i, i + 1) for i in range(chips - 1)])  9.32 us
    ppermute x3, waiting for transfers between devices, next_chip(): return lax.ppermute(x, 'outer', [(i, i + 1) for i in range(chips - 1)])  6 us
    ppermute x1, waiting for transfers between devices, next_chip(): lax.ppermute(x, 'outer', [(i, (i + 1) % chips) for i in range(chips)])  4.37 us
    unnamed x16, local copies, waits for them, and re-layouts  3.3 us
    ppermute x2, waiting for transfers between devices, other_heads(): one = lax.ppermute(x, 'heads', [(i, i ^ 1) for i in range(size)])  3.16 us
    ppermute x2, waiting for transfers between devices, other_heads(): lax.ppermute(x + one, 'heads', [(i, i ^ 2) for i in range(size)])  3.1 us
  transfers between devices with their start and end apart: 23, of which 12 were waited for; matrix products, arithmetic and copies ran while one was open for 0% of the time, Pallas kernels for 15%

profile of v3, /device:TPU:9, one launch (start us, length us, event | category | flops | bytes accessed | tf_op | source)
XLA Modules:
  0.0 58.4 jit_solution(17375351985528112832)
XLA Ops:
  2.9 1.0 %copy-done.3 = bf16[128,2048]{1,0:T(8,128)(2,1)S(1)} copy-done((bf16[128,2048]{1,0:T(8,128)(2,1)S(1)}, bf16[128,2048]{1,0:T(8,128)(2,1)}, u32[]{:S(2)}) %copy-start.3) | copy-done | bytes 524312
  6.7 1.3 %collective-permute-start.5 = (bf16[144,1024]{1,0:T(8,128)(2,1)S(1)}, bf16[144,1024]{1,0:T(8,128)(2,1)S(1)}, u32[]{:S(2)}, u32[]{:S(2)}) collective-permute-start(bf16[144,1024]{1,0:T(8,128)(2,1)S(1)} %get-tuple-element.42), channel_id=1, source_target_pairs={{0,8},{8,16},{16,24},{24,0},{1,9},{9,17},{17,25},{25,1},{2,10},{10... | collective-permute-start | bytes 884744 | tf_op jit(solution)/shard_map/ppermute | solution.py:314
  8.3 1.2 %shard_map.97 = (f32[256,1024]{1,0:T(8,128)S(1)}, bf16[256,1024]{1,0:T(8,128)(2,1)S(1)}, f32[256,1024]{1,0:T(8,128)S(1)}, f32[1,256]{1,0:T(1,128)S(1)}) custom-call(bf16[128,2048]{1,0:T(8,128)(2,1)S(1)} %copy-done.4, bf16[128,1024]{1,0:T(8,128)(2,1)S(1)} %get-tuple-element.39.k_own, bf16[128,1024]{1,0:T(8,128)(2,1)S(1)} %get-tuple-element.40.v_own, ...), custom_call_target="tpu_custom_call" | custom-call | bytes 3600000 | tf_op jit(solution)/shard_map/pallas_call | solution.py:292
  10.8 4.4 %collective-permute-done.5.t_near = bf16[144,1024]{1,0:T(8,128)(2,1)S(1)} collective-permute-done((bf16[144,1024]{1,0:T(8,128)(2,1)S(1)}, bf16[144,1024]{1,0:T(8,128)(2,1)S(1)}, u32[]{:S(2)}, u32[]{:S(2)}) %collective-permute-start.5) | collective-permute-done | bytes 294944 | tf_op jit(solution)/shard_map/ppermute | solution.py:314
  15.2 3.2 %collective-permute-start.9 = (bf16[144,1024]{1,0:T(8,128)(2,1)S(1)}, bf16[144,1024]{1,0:T(8,128)(2,1)S(1)}, u32[]{:S(2)}, u32[]{:S(2)}) collective-permute-start(bf16[144,1024]{1,0:T(8,128)(2,1)S(1)} %collective-permute-done.5.t_near), channel_id=1, source_target_pairs={{0,8},{8,16},{16,24},{1,9},{9,17},{17,25},{2,10},{10,18},{18,26},{... | collective-permute-start | bytes 884744 | tf_op jit(solution)/shard_map/ppermute | solution.py:313
  18.8 1.1 %collective-permute-start.7 = (f32[1,256]{1,0:T(1,128)S(1)}, f32[1,256]{1,0:T(1,128)S(1)}, u32[]{:S(2)}, u32[]{:S(2)}) collective-permute-start(f32[1,256]{1,0:T(1,128)S(1)} %add.12.s0), channel_id=1, source_target_pairs={{0,1},{1,0},{2,3},{3,2},{4,5},{5,4},{6,7},{7,6},{8,9},{9,8},{10,11... | collective-permute-start | bytes 3080 | tf_op jit(solution)/shard_map/ppermute | solution.py:328
  19.9 1.7 %collective-permute-done.7.s1 = f32[1,256]{1,0:T(1,128)S(1)} collective-permute-done((f32[1,256]{1,0:T(1,128)S(1)}, f32[1,256]{1,0:T(1,128)S(1)}, u32[]{:S(2)}, u32[]{:S(2)}) %collective-permute-start.7) | collective-permute-done | bytes 1056 | tf_op jit(solution)/shard_map/ppermute | solution.py:328
  21.5 1.1 %collective-permute-start.8 = (f32[1,256]{1,0:T(1,128)S(1)}, f32[1,256]{1,0:T(1,128)S(1)}, u32[]{:S(2)}, u32[]{:S(2)}) collective-permute-start(f32[1,256]{1,0:T(1,128)S(1)} %add.13), channel_id=1, source_target_pairs={{0,2},{1,3},{2,0},{3,1},{4,6},{5,7},{6,4},{7,5},{8,10},{9,11},{10,... | collective-permute-start | bytes 3080 | tf_op jit(solution)/shard_map/ppermute | solution.py:329
  22.6 1.6 %collective-permute-done.8.s2 = f32[1,256]{1,0:T(1,128)S(1)} collective-permute-done((f32[1,256]{1,0:T(1,128)S(1)}, f32[1,256]{1,0:T(1,128)S(1)}, u32[]{:S(2)}, u32[]{:S(2)}) %collective-permute-start.8) | collective-permute-done | bytes 1056 | tf_op jit(solution)/shard_map/ppermute | solution.py:329
  24.2 2.1 %collective-permute-done.9.t_far = bf16[144,1024]{1,0:T(8,128)(2,1)S(1)} collective-permute-done((bf16[144,1024]{1,0:T(8,128)(2,1)S(1)}, bf16[144,1024]{1,0:T(8,128)(2,1)S(1)}, u32[]{:S(2)}, u32[]{:S(2)}) %collective-permute-start.9) | collective-permute-done | bytes 294944 | tf_op jit(solution)/shard_map/ppermute | solution.py:313
  26.4 2.0 %collective-permute-start.19 = (bf16[128,2048]{1,0:T(8,128)(2,1)S(1)}, bf16[128,2048]{1,0:T(8,128)(2,1)S(1)}, u32[]{:S(2)}, u32[]{:S(2)}) collective-permute-start(bf16[128,2048]{1,0:T(8,128)(2,1)S(1)} %collective-permute-done.18.near_last.own), channel_id=1, source_target_pairs={{0,4},{4,0},{1,5},{5,1},{2,6},{6,2},{3,7},{7,3},{8,12},{12,8},{9,1... | collective-permute-start | bytes 1572872 | tf_op jit(solution)/shard_map/ppermute | solution.py:307
  28.6 2.9 %collective-permute-start.20 = (bf16[256,1024]{1,0:T(8,128)(2,1)S(1)}, bf16[256,1024]{1,0:T(8,128)(2,1)S(1)}, u32[]{:S(2)}, u32[]{:S(2)}) collective-permute-start(bf16[256,1024]{1,0:T(8,128)(2,1)S(1)} %shard_map.104), channel_id=1, source_target_pairs={{0,8},{8,16},{16,24},{1,9},{9,17},{17,25},{2,10},{10,18},{18,26},{... | collective-permute-start | bytes 1572872 | tf_op jit(solution)/shard_map/ppermute | solution.py:313
  31.5 2.2 %collective-permute-start.17 = (bf16[128,2048]{1,0:T(8,128)(2,1)S(1)}, bf16[128,2048]{1,0:T(8,128)(2,1)S(1)}, u32[]{:S(2)}, u32[]{:S(2)}) collective-permute-start(bf16[128,2048]{1,0:T(8,128)(2,1)S(1)} %collective-permute-done.16.near_first), channel_id=1, source_target_pairs={{0,4},{4,0},{1,5},{5,1},{2,6},{6,2},{3,7},{7,3},{8,12},{12,8},{9,1... | collective-permute-start | bytes 1572872 | tf_op jit(solution)/shard_map/ppermute | solution.py:307
  34.4 1.1 %collective-permute-done.10 = f32[1,256]{1,0:T(1,128)S(1)} collective-permute-done((f32[1,256]{1,0:T(1,128)S(1)}, f32[1,256]{1,0:T(1,128)S(1)}, u32[]{:S(2)}, u32[]{:S(2)}) %collective-permute-start.10) | collective-permute-done | bytes 1056 | tf_op jit(solution)/shard_map/ppermute | solution.py:307
  35.5 1.2 %collective-permute-start.11 = (f32[1,256]{1,0:T(1,128)S(1)}, f32[1,256]{1,0:T(1,128)S(1)}, u32[]{:S(2)}, u32[]{:S(2)}) collective-permute-start(f32[1,256]{1,0:T(1,128)S(1)} %add.14.s0), channel_id=1, source_target_pairs={{0,1},{1,0},{2,3},{3,2},{4,5},{5,4},{6,7},{7,6},{8,9},{9,8},{10,11... | collective-permute-start | bytes 3080 | tf_op jit(solution)/shard_map/ppermute | solution.py:328
  36.7 1.5 %collective-permute-done.11.s1 = f32[1,256]{1,0:T(1,128)S(1)} collective-permute-done((f32[1,256]{1,0:T(1,128)S(1)}, f32[1,256]{1,0:T(1,128)S(1)}, u32[]{:S(2)}, u32[]{:S(2)}) %collective-permute-start.11) | collective-permute-done | bytes 1056 | tf_op jit(solution)/shard_map/ppermute | solution.py:328
  38.2 1.2 %collective-permute-start.12 = (f32[1,256]{1,0:T(1,128)S(1)}, f32[1,256]{1,0:T(1,128)S(1)}, u32[]{:S(2)}, u32[]{:S(2)}) collective-permute-start(f32[1,256]{1,0:T(1,128)S(1)} %add.15), channel_id=1, source_target_pairs={{0,2},{1,3},{2,0},{3,1},{4,6},{5,7},{6,4},{7,5},{8,10},{9,11},{10,... | collective-permute-start | bytes 3080 | tf_op jit(solution)/shard_map/ppermute | solution.py:329
  39.5 1.5 %collective-permute-done.12.s2 = f32[1,256]{1,0:T(1,128)S(1)} collective-permute-done((f32[1,256]{1,0:T(1,128)S(1)}, f32[1,256]{1,0:T(1,128)S(1)}, u32[]{:S(2)}, u32[]{:S(2)}) %collective-permute-start.12) | collective-permute-done | bytes 1056 | tf_op jit(solution)/shard_map/ppermute | solution.py:329
  42.2 1.9 %collective-permute-done.20.near_values.near = bf16[256,1024]{1,0:T(8,128)(2,1)S(1)} collective-permute-done((bf16[256,1024]{1,0:T(8,128)(2,1)S(1)}, bf16[256,1024]{1,0:T(8,128)(2,1)S(1)}, u32[]{:S(2)}, u32[]{:S(2)}) %collective-permute-start.20) | collective-permute-done | bytes 524320 | tf_op jit(solution)/shard_map/ppermute | solution.py:313
  44.6 3.2 %collective-permute-start.21 = (bf16[144,1024]{1,0:T(8,128)(2,1)S(1)}, bf16[144,1024]{1,0:T(8,128)(2,1)S(1)}, u32[]{:S(2)}, u32[]{:S(2)}) collective-permute-start(bf16[144,1024]{1,0:T(8,128)(2,1)S(1)} %shard_map.105), channel_id=1, source_target_pairs={{0,8},{8,16},{16,24},{1,9},{9,17},{17,25},{2,10},{10,18},{18,26},{... | collective-permute-start | bytes 884744 | tf_op jit(solution)/shard_map/ppermute | solution.py:313
  47.8 1.1 %collective-permute-start.13 = (bf16[128,1024]{1,0:T(8,128)(2,1)S(1)}, bf16[128,1024]{1,0:T(8,128)(2,1)S(1)}, u32[]{:S(2)}, u32[]{:S(2)}) collective-permute-start(bf16[128,1024]{1,0:T(8,128)(2,1)S(1)} %get-tuple-element.54), channel_id=1, source_target_pairs={{0,4},{4,0},{1,5},{5,1},{2,6},{6,2},{3,7},{7,3},{8,12},{12,8},{9,1... | collective-permute-start | bytes 786440 | tf_op jit(solution)/shard_map/ppermute | solution.py:307
  48.9 2.7 %shard_map.102 = (bf16[8,256,512]{2,1,0:T(8,128)(2,1)S(1)}, bf16[8,128,128]{2,1,0:T(8,128)(2,1)S(1)}, f32[1,1024]{1,0:T(1,128)S(1)}) custom-call(bf16[128,2048]{1,0:T(8,128)(2,1)S(1)} %copy-done.1, bf16[128,2048]{1,0:T(8,128)(2,1)S(1)} %copy-done, bf16[128,2048]{1,0:T(8,128)(2,1)S(1)} %collective-permute-done.14.second.q_got, ...), custom_call_target="tpu_custom_call" | custom-call | bytes 7500000 | tf_op jit(solution)/shard_map/pallas_call | solution.py:292
  52.4 1.9 %collective-permute-done.21.answer = bf16[144,1024]{1,0:T(8,128)(2,1)S(1)} collective-permute-done((bf16[144,1024]{1,0:T(8,128)(2,1)S(1)}, bf16[144,1024]{1,0:T(8,128)(2,1)S(1)}, u32[]{:S(2)}, u32[]{:S(2)}) %collective-permute-start.21) | collective-permute-done | bytes 294944 | tf_op jit(solution)/shard_map/ppermute | solution.py:313
  54.7 1.7 %collective-permute-start.22 = (bf16[128,1024]{1,0:T(8,128)(2,1)S(1)}, bf16[128,1024]{1,0:T(8,128)(2,1)S(1)}, u32[]{:S(2)}, u32[]{:S(2)}) collective-permute-start(bf16[128,1024]{1,0:T(8,128)(2,1)S(1)} %get-tuple-element.75), channel_id=1, source_target_pairs={{0,4},{4,0},{1,5},{5,1},{2,6},{6,2},{3,7},{7,3},{8,12},{12,8},{9,1... | collective-permute-start | bytes 786440 | tf_op jit(solution)/shard_map/ppermute | solution.py:307
  (57 shorter events, 12.6 us)
Async XLA Ops:
  0.6 5.7 %copy-start = (bf16[128,2048]{1,0:T(8,128)(2,1)S(1)}, bf16[128,2048]{1,0:T(8,128)(2,1)}, u32[]{:S(2)}) copy-start(bf16[128,2048]{1,0:T(8,128)(2,1)} %k_own.1) | copy-start | bytes 1572868
  0.7 4.1 %collective-permute-start = (bf16[128,2048]{1,0:T(8,128)(2,1)}, bf16[128,2048]{1,0:T(8,128)(2,1)S(1)}, u32[]{:S(2)}, u32[]{:S(2)}) collective-permute-start(bf16[128,2048]{1,0:T(8,128)(2,1)} %key.1), channel_id=1, source_target_pairs={{0,4},{4,0},{1,5},{5,1},{2,6},{6,2},{3,7},{7,3},{8,12},{12,8},{9,1... | collective-permute-start | bytes 1572872 | tf_op jit(solution)/shard_map/ppermute | solution.py:307
  1.4 3.3 %collective-permute-start.1 = (bf16[128,2048]{1,0:T(8,128)(2,1)}, bf16[128,2048]{1,0:T(8,128)(2,1)S(1)}, u32[]{:S(2)}, u32[]{:S(2)}) collective-permute-start(bf16[128,2048]{1,0:T(8,128)(2,1)} %value.1), channel_id=1, source_target_pairs={{0,4},{4,0},{1,5},{5,1},{2,6},{6,2},{3,7},{7,3},{8,12},{12,8},{9,1... | collective-permute-start | bytes 1572872 | tf_op jit(solution)/shard_map/ppermute | solution.py:307
  1.5 3.2 %collective-permute-start.2 = (s32[1,128]{1,0:T(1,128)}, s32[1,128]{1,0:T(1,128)S(1)}, u32[]{:S(2)}, u32[]{:S(2)}) collective-permute-start(s32[1,128]{1,0:T(1,128)} %bitcast.1), channel_id=1, source_target_pairs={{0,4},{4,0},{1,5},{5,1},{2,6},{6,2},{3,7},{7,3},{8,12},{12,8},{9,1... | collective-permute-start | bytes 1544 | tf_op jit(solution)/shard_map/ppermute | solution.py:307
  5.7 2.3 %collective-permute-start.3 = (bf16[128,2048]{1,0:T(8,128)(2,1)S(1)}, bf16[128,2048]{1,0:T(8,128)(2,1)S(1)}, u32[]{:S(2)}, u32[]{:S(2)}) collective-permute-start(bf16[128,2048]{1,0:T(8,128)(2,1)S(1)} %copy-done.4), channel_id=1, source_target_pairs={{0,4},{4,0},{1,5},{5,1},{2,6},{6,2},{3,7},{7,3},{8,12},{12,8},{9,1... | collective-permute-start | bytes 1572872 | tf_op jit(solution)/shard_map/ppermute | solution.py:307
  5.8 2.5 %collective-permute-start.4 = (bf16[128,2048]{1,0:T(8,128)(2,1)S(1)}, bf16[128,2048]{1,0:T(8,128)(2,1)S(1)}, u32[]{:S(2)}, u32[]{:S(2)}) collective-permute-start(bf16[128,2048]{1,0:T(8,128)(2,1)S(1)} %copy-done.5), channel_id=1, source_target_pairs={{0,4},{4,0},{1,5},{5,1},{2,6},{6,2},{3,7},{7,3},{8,12},{12,8},{9,1... | collective-permute-start | bytes 1572872 | tf_op jit(solution)/shard_map/ppermute | solution.py:307
  6.2 3.6 %collective-permute-start.14 = (bf16[128,2048]{1,0:T(8,128)(2,1)S(1)}, bf16[128,2048]{1,0:T(8,128)(2,1)S(1)}, u32[]{:S(2)}, u32[]{:S(2)}) collective-permute-start(bf16[128,2048]{1,0:T(8,128)(2,1)S(1)} %copy-done.1), channel_id=1, source_target_pairs={{0,4},{4,0},{1,5},{5,1},{2,6},{6,2},{3,7},{7,3},{8,12},{12,8},{9,1... | collective-permute-start | bytes 1572872 | tf_op jit(solution)/shard_map/ppermute | solution.py:307
  6.4 3.5 %collective-permute-start.15 = (bf16[128,2048]{1,0:T(8,128)(2,1)S(1)}, bf16[128,2048]{1,0:T(8,128)(2,1)S(1)}, u32[]{:S(2)}, u32[]{:S(2)}) collective-permute-start(bf16[128,2048]{1,0:T(8,128)(2,1)S(1)} %copy-done), channel_id=1, source_target_pairs={{0,4},{4,0},{1,5},{5,1},{2,6},{6,2},{3,7},{7,3},{8,12},{12,8},{9,1... | collective-permute-start | bytes 1572872 | tf_op jit(solution)/shard_map/ppermute | solution.py:307
  6.7 8.5 %collective-permute-start.5 = (bf16[144,1024]{1,0:T(8,128)(2,1)S(1)}, bf16[144,1024]{1,0:T(8,128)(2,1)S(1)}, u32[]{:S(2)}, u32[]{:S(2)}) collective-permute-start(bf16[144,1024]{1,0:T(8,128)(2,1)S(1)} %get-tuple-element.42), channel_id=1, source_target_pairs={{0,8},{8,16},{16,24},{24,0},{1,9},{9,17},{17,25},{25,1},{2,10},{10... | collective-permute-start | bytes 884744 | tf_op jit(solution)/shard_map/ppermute | solution.py:314
  9.6 1.2 %collective-permute-start.6 = (f32[1,256]{1,0:T(1,128)S(1)}, f32[1,256]{1,0:T(1,128)S(1)}, u32[]{:S(2)}, u32[]{:S(2)}) collective-permute-start(f32[1,256]{1,0:T(1,128)S(1)} %get-tuple-element.48), channel_id=1, source_target_pairs={{0,4},{4,0},{1,5},{5,1},{2,6},{6,2},{3,7},{7,3},{8,12},{12,8},{9,1... | collective-permute-start | bytes 3080 | tf_op jit(solution)/shard_map/ppermute | solution.py:307
  10.8 15.6 %collective-permute-start.18 = (bf16[128,2048]{1,0:T(8,128)(2,1)S(1)}, bf16[128,2048]{1,0:T(8,128)(2,1)S(1)}, u32[]{:S(2)}, u32[]{:S(2)}) collective-permute-start(bf16[128,2048]{1,0:T(8,128)(2,1)S(1)} %shard_map.101), channel_id=1, source_target_pairs={{0,8},{8,16},{16,24},{24,28},{12,4},{20,12},{28,20},{4,0},{1,9},{9... | collective-permute-start | bytes 1572872 | tf_op jit(solution)/shard_map/ppermute | solution.py:321
  15.2 11.2 %collective-permute-start.9 = (bf16[144,1024]{1,0:T(8,128)(2,1)S(1)}, bf16[144,1024]{1,0:T(8,128)(2,1)S(1)}, u32[]{:S(2)}, u32[]{:S(2)}) collective-permute-start(bf16[144,1024]{1,0:T(8,128)(2,1)S(1)} %collective-permute-done.5.t_near), channel_id=1, source_target_pairs={{0,8},{8,16},{16,24},{1,9},{9,17},{17,25},{2,10},{10,18},{18,26},{... | collective-permute-start | bytes 884744 | tf_op jit(solution)/shard_map/ppermute | solution.py:313
  18.4 13.1 %collective-permute-start.16 = (bf16[128,2048]{1,0:T(8,128)(2,1)S(1)}, bf16[128,2048]{1,0:T(8,128)(2,1)S(1)}, u32[]{:S(2)}, u32[]{:S(2)}) collective-permute-start(bf16[128,2048]{1,0:T(8,128)(2,1)S(1)} %copy-done), channel_id=1, source_target_pairs={{0,8},{8,16},{16,24},{24,28},{12,4},{20,12},{28,20},{4,0},{1,9},{9... | collective-permute-start | bytes 1572872 | tf_op jit(solution)/shard_map/ppermute | solution.py:321
  18.8 2.7 %collective-permute-start.7 = (f32[1,256]{1,0:T(1,128)S(1)}, f32[1,256]{1,0:T(1,128)S(1)}, u32[]{:S(2)}, u32[]{:S(2)}) collective-permute-start(f32[1,256]{1,0:T(1,128)S(1)} %add.12.s0), channel_id=1, source_target_pairs={{0,1},{1,0},{2,3},{3,2},{4,5},{5,4},{6,7},{7,6},{8,9},{9,8},{10,11... | collective-permute-start | bytes 3080 | tf_op jit(solution)/shard_map/ppermute | solution.py:328
  21.5 2.7 %collective-permute-start.8 = (f32[1,256]{1,0:T(1,128)S(1)}, f32[1,256]{1,0:T(1,128)S(1)}, u32[]{:S(2)}, u32[]{:S(2)}) collective-permute-start(f32[1,256]{1,0:T(1,128)S(1)} %add.13), channel_id=1, source_target_pairs={{0,2},{1,3},{2,0},{3,1},{4,6},{5,7},{6,4},{7,5},{8,10},{9,11},{10,... | collective-permute-start | bytes 3080 | tf_op jit(solution)/shard_map/ppermute | solution.py:329
  26.4 14.8 %collective-permute-start.19 = (bf16[128,2048]{1,0:T(8,128)(2,1)S(1)}, bf16[128,2048]{1,0:T(8,128)(2,1)S(1)}, u32[]{:S(2)}, u32[]{:S(2)}) collective-permute-start(bf16[128,2048]{1,0:T(8,128)(2,1)S(1)} %collective-permute-done.18.near_last.own), channel_id=1, source_target_pairs={{0,4},{4,0},{1,5},{5,1},{2,6},{6,2},{3,7},{7,3},{8,12},{12,8},{9,1... | collective-permute-start | bytes 1572872 | tf_op jit(solution)/shard_map/ppermute | solution.py:307
  28.6 15.6 %collective-permute-start.20 = (bf16[256,1024]{1,0:T(8,128)(2,1)S(1)}, bf16[256,1024]{1,0:T(8,128)(2,1)S(1)}, u32[]{:S(2)}, u32[]{:S(2)}) collective-permute-start(bf16[256,1024]{1,0:T(8,128)(2,1)S(1)} %shard_map.104), channel_id=1, source_target_pairs={{0,8},{8,16},{16,24},{1,9},{9,17},{17,25},{2,10},{10,18},{18,26},{... | collective-permute-start | bytes 1572872 | tf_op jit(solution)/shard_map/ppermute | solution.py:313
  31.5 17.4 %collective-permute-start.17 = (bf16[128,2048]{1,0:T(8,128)(2,1)S(1)}, bf16[128,2048]{1,0:T(8,128)(2,1)S(1)}, u32[]{:S(2)}, u32[]{:S(2)}) collective-permute-start(bf16[128,2048]{1,0:T(8,128)(2,1)S(1)} %collective-permute-done.16.near_first), channel_id=1, source_target_pairs={{0,4},{4,0},{1,5},{5,1},{2,6},{6,2},{3,7},{7,3},{8,12},{12,8},{9,1... | collective-permute-start | bytes 1572872 | tf_op jit(solution)/shard_map/ppermute | solution.py:307
  34.3 1.2 %collective-permute-start.10 = (f32[1,256]{1,0:T(1,128)S(1)}, f32[1,256]{1,0:T(1,128)S(1)}, u32[]{:S(2)}, u32[]{:S(2)}) collective-permute-start(f32[1,256]{1,0:T(1,128)S(1)} %get-tuple-element.52), channel_id=1, source_target_pairs={{0,4},{4,0},{1,5},{5,1},{2,6},{6,2},{3,7},{7,3},{8,12},{12,8},{9,1... | collective-permute-start | bytes 3080 | tf_op jit(solution)/shard_map/ppermute | solution.py:307
  35.5 2.7 %collective-permute-start.11 = (f32[1,256]{1,0:T(1,128)S(1)}, f32[1,256]{1,0:T(1,128)S(1)}, u32[]{:S(2)}, u32[]{:S(2)}) collective-permute-start(f32[1,256]{1,0:T(1,128)S(1)} %add.14.s0), channel_id=1, source_target_pairs={{0,1},{1,0},{2,3},{3,2},{4,5},{5,4},{6,7},{7,6},{8,9},{9,8},{10,11... | collective-permute-start | bytes 3080 | tf_op jit(solution)/shard_map/ppermute | solution.py:328
  38.2 2.7 %collective-permute-start.12 = (f32[1,256]{1,0:T(1,128)S(1)}, f32[1,256]{1,0:T(1,128)S(1)}, u32[]{:S(2)}, u32[]{:S(2)}) collective-permute-start(f32[1,256]{1,0:T(1,128)S(1)} %add.15), channel_id=1, source_target_pairs={{0,2},{1,3},{2,0},{3,1},{4,6},{5,7},{6,4},{7,5},{8,10},{9,11},{10,... | collective-permute-start | bytes 3080 | tf_op jit(solution)/shard_map/ppermute | solution.py:329
  44.6 9.7 %collective-permute-start.21 = (bf16[144,1024]{1,0:T(8,128)(2,1)S(1)}, bf16[144,1024]{1,0:T(8,128)(2,1)S(1)}, u32[]{:S(2)}, u32[]{:S(2)}) collective-permute-start(bf16[144,1024]{1,0:T(8,128)(2,1)S(1)} %shard_map.105), channel_id=1, source_target_pairs={{0,8},{8,16},{16,24},{1,9},{9,17},{17,25},{2,10},{10,18},{18,26},{... | collective-permute-start | bytes 884744 | tf_op jit(solution)/shard_map/ppermute | solution.py:313
  47.8 8.6 %collective-permute-start.13 = (bf16[128,1024]{1,0:T(8,128)(2,1)S(1)}, bf16[128,1024]{1,0:T(8,128)(2,1)S(1)}, u32[]{:S(2)}, u32[]{:S(2)}) collective-permute-start(bf16[128,1024]{1,0:T(8,128)(2,1)S(1)} %get-tuple-element.54), channel_id=1, source_target_pairs={{0,4},{4,0},{1,5},{5,1},{2,6},{6,2},{3,7},{7,3},{8,12},{12,8},{9,1... | collective-permute-start | bytes 786440 | tf_op jit(solution)/shard_map/ppermute | solution.py:307
  54.7 2.9 %collective-permute-start.22 = (bf16[128,1024]{1,0:T(8,128)(2,1)S(1)}, bf16[128,1024]{1,0:T(8,128)(2,1)S(1)}, u32[]{:S(2)}, u32[]{:S(2)}) collective-permute-start(bf16[128,1024]{1,0:T(8,128)(2,1)S(1)} %get-tuple-element.75), channel_id=1, source_target_pairs={{0,4},{4,0},{1,5},{5,1},{2,6},{6,2},{3,7},{7,3},{8,12},{12,8},{9,1... | collective-permute-start | bytes 786440 | tf_op jit(solution)/shard_map/ppermute | solution.py:307
  (7 other events, 13.9 us)

commit v4 on v3

--- a/solution.py
+++ b/solution.py
@@ -9,7 +9,7 @@
 from jax.sharding import PartitionSpec as P
 
 DH = 128
-PAD = 16
+PAD = 8
 F32 = jnp.float32
 BF16 = jnp.bfloat16
 NONE = -1e30

time: 58.9 us -> 58 us (0.985)
  waiting for transfers between devices: 19.3 us -> 18.6 us
where the time goes in v4:
time: 58 us; the launch traced here: 57.5 us
  starting transfers between devices  24.9 us (43%)
  waiting for transfers between devices  18.6 us (32%)
  Pallas kernels  9.81 us (17%)
  local copies, waits for them, and re-layouts  3.31 us (6%)
  between operations  0.82 us (1%)
    ppermute x13, starting transfers between devices, swap(): return lax.ppermute(x, 'inner', [(0, 1), (1, 0)])  9.83 us
    pallas_call x14, Pallas kernels, run(): pl.pallas_call(kernel, out_shape=[jax.ShapeDtypeStruct(*o) for o in outs]...  9.81 us
    ppermute x3, starting transfers between devices, next_chip(): return lax.ppermute(x, 'outer', [(i, i + 1) for i in range(chips - 1)])  8.8 us
    ppermute x3, waiting for transfers between devices, next_chip(): return lax.ppermute(x, 'outer', [(i, i + 1) for i in range(chips - 1)])  5.65 us
    ppermute x1, waiting for transfers between devices, next_chip(): lax.ppermute(x, 'outer', [(i, (i + 1) % chips) for i in range(chips)])  4.02 us
    unnamed x16, local copies, waits for them, and re-layouts  3.3 us
    ppermute x2, waiting for transfers between devices, other_heads(): one = lax.ppermute(x, 'heads', [(i, i ^ 1) for i in range(size)])  3.16 us
    ppermute x2, waiting for transfers between devices, other_heads(): lax.ppermute(x + one, 'heads', [(i, i ^ 2) for i in range(size)])  3.1 us
  transfers between devices with their start and end apart: 23, of which 12 were waited for; matrix products, arithmetic and copies ran while one was open for 0% of the time, Pallas kernels for 15%

profile of v4, /device:TPU:9, one launch (start us, length us, event | category | flops | bytes accessed | tf_op | source)
XLA Modules:
  0.0 57.5 jit_solution(13612300476130818173)
XLA Ops:
  1.9 1.0 %copy-done.2 = bf16[128,2048]{1,0:T(8,128)(2,1)S(1)} copy-done((bf16[128,2048]{1,0:T(8,128)(2,1)S(1)}, bf16[128,2048]{1,0:T(8,128)(2,1)}, u32[]{:S(2)}) %copy-start.2) | copy-done | bytes 524312
  6.7 1.3 %collective-permute-start.5 = (bf16[136,1024]{1,0:T(8,128)(2,1)S(1)}, bf16[136,1024]{1,0:T(8,128)(2,1)S(1)}, u32[]{:S(2)}, u32[]{:S(2)}) collective-permute-start(bf16[136,1024]{1,0:T(8,128)(2,1)S(1)} %get-tuple-element.42), channel_id=1, source_target_pairs={{0,8},{8,16},{16,24},{24,0},{1,9},{9,17},{17,25},{25,1},{2,10},{10... | collective-permute-start | bytes 835592 | tf_op jit(solution)/shard_map/ppermute | solution.py:314
  8.3 1.2 %shard_map.97 = (f32[256,1024]{1,0:T(8,128)S(1)}, bf16[256,1024]{1,0:T(8,128)(2,1)S(1)}, f32[256,1024]{1,0:T(8,128)S(1)}, f32[1,256]{1,0:T(1,128)S(1)}) custom-call(bf16[128,2048]{1,0:T(8,128)(2,1)S(1)} %copy-done.4, bf16[128,1024]{1,0:T(8,128)(2,1)S(1)} %get-tuple-element.39.k_own, bf16[128,1024]{1,0:T(8,128)(2,1)S(1)} %get-tuple-element.40.v_own, ...), custom_call_target="tpu_custom_call" | custom-call | bytes 3600000 | tf_op jit(solution)/shard_map/pallas_call | solution.py:292
  10.8 4.0 %collective-permute-done.5.t_near = bf16[136,1024]{1,0:T(8,128)(2,1)S(1)} collective-permute-done((bf16[136,1024]{1,0:T(8,128)(2,1)S(1)}, bf16[136,1024]{1,0:T(8,128)(2,1)S(1)}, u32[]{:S(2)}, u32[]{:S(2)}) %collective-permute-start.5) | collective-permute-done | bytes 278560 | tf_op jit(solution)/shard_map/ppermute | solution.py:314
  14.8 3.2 %collective-permute-start.9 = (bf16[136,1024]{1,0:T(8,128)(2,1)S(1)}, bf16[136,1024]{1,0:T(8,128)(2,1)S(1)}, u32[]{:S(2)}, u32[]{:S(2)}) collective-permute-start(bf16[136,1024]{1,0:T(8,128)(2,1)S(1)} %collective-permute-done.5.t_near), channel_id=1, source_target_pairs={{0,8},{8,16},{16,24},{1,9},{9,17},{17,25},{2,10},{10,18},{18,26},{... | collective-permute-start | bytes 835592 | tf_op jit(solution)/shard_map/ppermute | solution.py:313
  18.4 1.1 %collective-permute-start.7 = (f32[1,256]{1,0:T(1,128)S(1)}, f32[1,256]{1,0:T(1,128)S(1)}, u32[]{:S(2)}, u32[]{:S(2)}) collective-permute-start(f32[1,256]{1,0:T(1,128)S(1)} %add.12.s0), channel_id=1, source_target_pairs={{0,1},{1,0},{2,3},{3,2},{4,5},{5,4},{6,7},{7,6},{8,9},{9,8},{10,11... | collective-permute-start | bytes 3080 | tf_op jit(solution)/shard_map/ppermute | solution.py:328
  19.5 1.7 %collective-permute-done.7.s1 = f32[1,256]{1,0:T(1,128)S(1)} collective-permute-done((f32[1,256]{1,0:T(1,128)S(1)}, f32[1,256]{1,0:T(1,128)S(1)}, u32[]{:S(2)}, u32[]{:S(2)}) %collective-permute-start.7) | collective-permute-done | bytes 1056 | tf_op jit(solution)/shard_map/ppermute | solution.py:328
  21.2 1.1 %collective-permute-start.8 = (f32[1,256]{1,0:T(1,128)S(1)}, f32[1,256]{1,0:T(1,128)S(1)}, u32[]{:S(2)}, u32[]{:S(2)}) collective-permute-start(f32[1,256]{1,0:T(1,128)S(1)} %add.13), channel_id=1, source_target_pairs={{0,2},{1,3},{2,0},{3,1},{4,6},{5,7},{6,4},{7,5},{8,10},{9,11},{10,... | collective-permute-start | bytes 3080 | tf_op jit(solution)/shard_map/ppermute | solution.py:329
  22.2 1.6 %collective-permute-done.8.s2 = f32[1,256]{1,0:T(1,128)S(1)} collective-permute-done((f32[1,256]{1,0:T(1,128)S(1)}, f32[1,256]{1,0:T(1,128)S(1)}, u32[]{:S(2)}, u32[]{:S(2)}) %collective-permute-start.8) | collective-permute-done | bytes 1056 | tf_op jit(solution)/shard_map/ppermute | solution.py:329
  23.9 1.8 %collective-permute-done.9.t_far = bf16[136,1024]{1,0:T(8,128)(2,1)S(1)} collective-permute-done((bf16[136,1024]{1,0:T(8,128)(2,1)S(1)}, bf16[136,1024]{1,0:T(8,128)(2,1)S(1)}, u32[]{:S(2)}, u32[]{:S(2)}) %collective-permute-start.9) | collective-permute-done | bytes 278560 | tf_op jit(solution)/shard_map/ppermute | solution.py:313
  25.7 2.3 %collective-permute-start.19 = (bf16[128,2048]{1,0:T(8,128)(2,1)S(1)}, bf16[128,2048]{1,0:T(8,128)(2,1)S(1)}, u32[]{:S(2)}, u32[]{:S(2)}) collective-permute-start(bf16[128,2048]{1,0:T(8,128)(2,1)S(1)} %collective-permute-done.18.near_last.own), channel_id=1, source_target_pairs={{0,4},{4,0},{1,5},{5,1},{2,6},{6,2},{3,7},{7,3},{8,12},{12,8},{9,1... | collective-permute-start | bytes 1572872 | tf_op jit(solution)/shard_map/ppermute | solution.py:307
  28.2 2.6 %collective-permute-start.20 = (bf16[256,1024]{1,0:T(8,128)(2,1)S(1)}, bf16[256,1024]{1,0:T(8,128)(2,1)S(1)}, u32[]{:S(2)}, u32[]{:S(2)}) collective-permute-start(bf16[256,1024]{1,0:T(8,128)(2,1)S(1)} %shard_map.104), channel_id=1, source_target_pairs={{0,8},{8,16},{16,24},{1,9},{9,17},{17,25},{2,10},{10,18},{18,26},{... | collective-permute-start | bytes 1572872 | tf_op jit(solution)/shard_map/ppermute | solution.py:313
  30.8 2.2 %collective-permute-start.17 = (bf16[128,2048]{1,0:T(8,128)(2,1)S(1)}, bf16[128,2048]{1,0:T(8,128)(2,1)S(1)}, u32[]{:S(2)}, u32[]{:S(2)}) collective-permute-start(bf16[128,2048]{1,0:T(8,128)(2,1)S(1)} %collective-permute-done.16.near_first), channel_id=1, source_target_pairs={{0,4},{4,0},{1,5},{5,1},{2,6},{6,2},{3,7},{7,3},{8,12},{12,8},{9,1... | collective-permute-start | bytes 1572872 | tf_op jit(solution)/shard_map/ppermute | solution.py:307
  33.6 1.1 %collective-permute-done.10 = f32[1,256]{1,0:T(1,128)S(1)} collective-permute-done((f32[1,256]{1,0:T(1,128)S(1)}, f32[1,256]{1,0:T(1,128)S(1)}, u32[]{:S(2)}, u32[]{:S(2)}) %collective-permute-start.10) | collective-permute-done | bytes 1056 | tf_op jit(solution)/shard_map/ppermute | solution.py:307
  34.8 1.2 %collective-permute-start.11 = (f32[1,256]{1,0:T(1,128)S(1)}, f32[1,256]{1,0:T(1,128)S(1)}, u32[]{:S(2)}, u32[]{:S(2)}) collective-permute-start(f32[1,256]{1,0:T(1,128)S(1)} %add.14.s0), channel_id=1, source_target_pairs={{0,1},{1,0},{2,3},{3,2},{4,5},{5,4},{6,7},{7,6},{8,9},{9,8},{10,11... | collective-permute-start | bytes 3080 | tf_op jit(solution)/shard_map/ppermute | solution.py:328
  36.0 1.5 %collective-permute-done.11.s1 = f32[1,256]{1,0:T(1,128)S(1)} collective-permute-done((f32[1,256]{1,0:T(1,128)S(1)}, f32[1,256]{1,0:T(1,128)S(1)}, u32[]{:S(2)}, u32[]{:S(2)}) %collective-permute-start.11) | collective-permute-done | bytes 1056 | tf_op jit(solution)/shard_map/ppermute | solution.py:328
  37.5 1.2 %collective-permute-start.12 = (f32[1,256]{1,0:T(1,128)S(1)}, f32[1,256]{1,0:T(1,128)S(1)}, u32[]{:S(2)}, u32[]{:S(2)}) collective-permute-start(f32[1,256]{1,0:T(1,128)S(1)} %add.15), channel_id=1, source_target_pairs={{0,2},{1,3},{2,0},{3,1},{4,6},{5,7},{6,4},{7,5},{8,10},{9,11},{10,... | collective-permute-start | bytes 3080 | tf_op jit(solution)/shard_map/ppermute | solution.py:329
  38.7 1.5 %collective-permute-done.12.s2 = f32[1,256]{1,0:T(1,128)S(1)} collective-permute-done((f32[1,256]{1,0:T(1,128)S(1)}, f32[1,256]{1,0:T(1,128)S(1)}, u32[]{:S(2)}, u32[]{:S(2)}) %collective-permute-start.12) | collective-permute-done | bytes 1056 | tf_op jit(solution)/shard_map/ppermute | solution.py:329
  41.5 2.2 %collective-permute-done.20.near_values.near = bf16[256,1024]{1,0:T(8,128)(2,1)S(1)} collective-permute-done((bf16[256,1024]{1,0:T(8,128)(2,1)S(1)}, bf16[256,1024]{1,0:T(8,128)(2,1)S(1)}, u32[]{:S(2)}, u32[]{:S(2)}) %collective-permute-start.20) | collective-permute-done | bytes 524320 | tf_op jit(solution)/shard_map/ppermute | solution.py:313
  44.1 3.0 %collective-permute-start.21 = (bf16[136,1024]{1,0:T(8,128)(2,1)S(1)}, bf16[136,1024]{1,0:T(8,128)(2,1)S(1)}, u32[]{:S(2)}, u32[]{:S(2)}) collective-permute-start(bf16[136,1024]{1,0:T(8,128)(2,1)S(1)} %shard_map.105), channel_id=1, source_target_pairs={{0,8},{8,16},{16,24},{1,9},{9,17},{17,25},{2,10},{10,18},{18,26},{... | collective-permute-start | bytes 835592 | tf_op jit(solution)/shard_map/ppermute | solution.py:313
  47.1 1.1 %collective-permute-start.13 = (bf16[128,1024]{1,0:T(8,128)(2,1)S(1)}, bf16[128,1024]{1,0:T(8,128)(2,1)S(1)}, u32[]{:S(2)}, u32[]{:S(2)}) collective-permute-start(bf16[128,1024]{1,0:T(8,128)(2,1)S(1)} %get-tuple-element.54), channel_id=1, source_target_pairs={{0,4},{4,0},{1,5},{5,1},{2,6},{6,2},{3,7},{7,3},{8,12},{12,8},{9,1... | collective-permute-start | bytes 786440 | tf_op jit(solution)/shard_map/ppermute | solution.py:307
  48.2 2.7 %shard_map.102 = (bf16[8,256,512]{2,1,0:T(8,128)(2,1)S(1)}, bf16[8,128,128]{2,1,0:T(8,128)(2,1)S(1)}, f32[1,1024]{1,0:T(1,128)S(1)}) custom-call(bf16[128,2048]{1,0:T(8,128)(2,1)S(1)} %copy-done.1, bf16[128,2048]{1,0:T(8,128)(2,1)S(1)} %copy-done, bf16[128,2048]{1,0:T(8,128)(2,1)S(1)} %collective-permute-done.14.second.q_got, ...), custom_call_target="tpu_custom_call" | custom-call | bytes 7500000 | tf_op jit(solution)/shard_map/pallas_call | solution.py:292
  51.7 1.7 %collective-permute-done.21.answer = bf16[136,1024]{1,0:T(8,128)(2,1)S(1)} collective-permute-done((bf16[136,1024]{1,0:T(8,128)(2,1)S(1)}, bf16[136,1024]{1,0:T(8,128)(2,1)S(1)}, u32[]{:S(2)}, u32[]{:S(2)}) %collective-permute-start.21) | collective-permute-done | bytes 278560 | tf_op jit(solution)/shard_map/ppermute | solution.py:313
  53.8 1.7 %collective-permute-start.22 = (bf16[128,1024]{1,0:T(8,128)(2,1)S(1)}, bf16[128,1024]{1,0:T(8,128)(2,1)S(1)}, u32[]{:S(2)}, u32[]{:S(2)}) collective-permute-start(bf16[128,1024]{1,0:T(8,128)(2,1)S(1)} %get-tuple-element.75), channel_id=1, source_target_pairs={{0,4},{4,0},{1,5},{5,1},{2,6},{6,2},{3,7},{7,3},{8,12},{12,8},{9,1... | collective-permute-start | bytes 786440 | tf_op jit(solution)/shard_map/ppermute | solution.py:307
  (57 shorter events, 12.6 us)
Async XLA Ops:
  0.6 5.7 %copy-start = (bf16[128,2048]{1,0:T(8,128)(2,1)S(1)}, bf16[128,2048]{1,0:T(8,128)(2,1)}, u32[]{:S(2)}) copy-start(bf16[128,2048]{1,0:T(8,128)(2,1)} %k_own.1) | copy-start | bytes 1572868
  0.7 4.1 %collective-permute-start = (bf16[128,2048]{1,0:T(8,128)(2,1)}, bf16[128,2048]{1,0:T(8,128)(2,1)S(1)}, u32[]{:S(2)}, u32[]{:S(2)}) collective-permute-start(bf16[128,2048]{1,0:T(8,128)(2,1)} %key.1), channel_id=1, source_target_pairs={{0,4},{4,0},{1,5},{5,1},{2,6},{6,2},{3,7},{7,3},{8,12},{12,8},{9,1... | collective-permute-start | bytes 1572872 | tf_op jit(solution)/shard_map/ppermute | solution.py:307
  1.4 3.3 %collective-permute-start.1 = (bf16[128,2048]{1,0:T(8,128)(2,1)}, bf16[128,2048]{1,0:T(8,128)(2,1)S(1)}, u32[]{:S(2)}, u32[]{:S(2)}) collective-permute-start(bf16[128,2048]{1,0:T(8,128)(2,1)} %value.1), channel_id=1, source_target_pairs={{0,4},{4,0},{1,5},{5,1},{2,6},{6,2},{3,7},{7,3},{8,12},{12,8},{9,1... | collective-permute-start | bytes 1572872 | tf_op jit(solution)/shard_map/ppermute | solution.py:307
  1.5 3.2 %collective-permute-start.2 = (s32[1,128]{1,0:T(1,128)}, s32[1,128]{1,0:T(1,128)S(1)}, u32[]{:S(2)}, u32[]{:S(2)}) collective-permute-start(s32[1,128]{1,0:T(1,128)} %bitcast.1), channel_id=1, source_target_pairs={{0,4},{4,0},{1,5},{5,1},{2,6},{6,2},{3,7},{7,3},{8,12},{12,8},{9,1... | collective-permute-start | bytes 1544 | tf_op jit(solution)/shard_map/ppermute | solution.py:307
  5.7 2.3 %collective-permute-start.3 = (bf16[128,2048]{1,0:T(8,128)(2,1)S(1)}, bf16[128,2048]{1,0:T(8,128)(2,1)S(1)}, u32[]{:S(2)}, u32[]{:S(2)}) collective-permute-start(bf16[128,2048]{1,0:T(8,128)(2,1)S(1)} %copy-done.4), channel_id=1, source_target_pairs={{0,4},{4,0},{1,5},{5,1},{2,6},{6,2},{3,7},{7,3},{8,12},{12,8},{9,1... | collective-permute-start | bytes 1572872 | tf_op jit(solution)/shard_map/ppermute | solution.py:307
  5.8 2.5 %collective-permute-start.4 = (bf16[128,2048]{1,0:T(8,128)(2,1)S(1)}, bf16[128,2048]{1,0:T(8,128)(2,1)S(1)}, u32[]{:S(2)}, u32[]{:S(2)}) collective-permute-start(bf16[128,2048]{1,0:T(8,128)(2,1)S(1)} %copy-done.5), channel_id=1, source_target_pairs={{0,4},{4,0},{1,5},{5,1},{2,6},{6,2},{3,7},{7,3},{8,12},{12,8},{9,1... | collective-permute-start | bytes 1572872 | tf_op jit(solution)/shard_map/ppermute | solution.py:307
  6.2 3.6 %collective-permute-start.14 = (bf16[128,2048]{1,0:T(8,128)(2,1)S(1)}, bf16[128,2048]{1,0:T(8,128)(2,1)S(1)}, u32[]{:S(2)}, u32[]{:S(2)}) collective-permute-start(bf16[128,2048]{1,0:T(8,128)(2,1)S(1)} %copy-done.1), channel_id=1, source_target_pairs={{0,4},{4,0},{1,5},{5,1},{2,6},{6,2},{3,7},{7,3},{8,12},{12,8},{9,1... | collective-permute-start | bytes 1572872 | tf_op jit(solution)/shard_map/ppermute | solution.py:307
  6.4 3.5 %collective-permute-start.15 = (bf16[128,2048]{1,0:T(8,128)(2,1)S(1)}, bf16[128,2048]{1,0:T(8,128)(2,1)S(1)}, u32[]{:S(2)}, u32[]{:S(2)}) collective-permute-start(bf16[128,2048]{1,0:T(8,128)(2,1)S(1)} %copy-done), channel_id=1, source_target_pairs={{0,4},{4,0},{1,5},{5,1},{2,6},{6,2},{3,7},{7,3},{8,12},{12,8},{9,1... | collective-permute-start | bytes 1572872 | tf_op jit(solution)/shard_map/ppermute | solution.py:307
  6.7 8.1 %collective-permute-start.5 = (bf16[136,1024]{1,0:T(8,128)(2,1)S(1)}, bf16[136,1024]{1,0:T(8,128)(2,1)S(1)}, u32[]{:S(2)}, u32[]{:S(2)}) collective-permute-start(bf16[136,1024]{1,0:T(8,128)(2,1)S(1)} %get-tuple-element.42), channel_id=1, source_target_pairs={{0,8},{8,16},{16,24},{24,0},{1,9},{9,17},{17,25},{25,1},{2,10},{10... | collective-permute-start | bytes 835592 | tf_op jit(solution)/shard_map/ppermute | solution.py:314
  9.6 1.2 %collective-permute-start.6 = (f32[1,256]{1,0:T(1,128)S(1)}, f32[1,256]{1,0:T(1,128)S(1)}, u32[]{:S(2)}, u32[]{:S(2)}) collective-permute-start(f32[1,256]{1,0:T(1,128)S(1)} %get-tuple-element.48), channel_id=1, source_target_pairs={{0,4},{4,0},{1,5},{5,1},{2,6},{6,2},{3,7},{7,3},{8,12},{12,8},{9,1... | collective-permute-start | bytes 3080 | tf_op jit(solution)/shard_map/ppermute | solution.py:307
  10.8 14.9 %collective-permute-start.18 = (bf16[128,2048]{1,0:T(8,128)(2,1)S(1)}, bf16[128,2048]{1,0:T(8,128)(2,1)S(1)}, u32[]{:S(2)}, u32[]{:S(2)}) collective-permute-start(bf16[128,2048]{1,0:T(8,128)(2,1)S(1)} %shard_map.101), channel_id=1, source_target_pairs={{0,8},{8,16},{16,24},{24,28},{12,4},{20,12},{28,20},{4,0},{1,9},{9... | collective-permute-start | bytes 1572872 | tf_op jit(solution)/shard_map/ppermute | solution.py:321
  14.8 10.8 %collective-permute-start.9 = (bf16[136,1024]{1,0:T(8,128)(2,1)S(1)}, bf16[136,1024]{1,0:T(8,128)(2,1)S(1)}, u32[]{:S(2)}, u32[]{:S(2)}) collective-permute-start(bf16[136,1024]{1,0:T(8,128)(2,1)S(1)} %collective-permute-done.5.t_near), channel_id=1, source_target_pairs={{0,8},{8,16},{16,24},{1,9},{9,17},{17,25},{2,10},{10,18},{18,26},{... | collective-permute-start | bytes 835592 | tf_op jit(solution)/shard_map/ppermute | solution.py:313
  18.0 12.8 %collective-permute-start.16 = (bf16[128,2048]{1,0:T(8,128)(2,1)S(1)}, bf16[128,2048]{1,0:T(8,128)(2,1)S(1)}, u32[]{:S(2)}, u32[]{:S(2)}) collective-permute-start(bf16[128,2048]{1,0:T(8,128)(2,1)S(1)} %copy-done), channel_id=1, source_target_pairs={{0,8},{8,16},{16,24},{24,28},{12,4},{20,12},{28,20},{4,0},{1,9},{9... | collective-permute-start | bytes 1572872 | tf_op jit(solution)/shard_map/ppermute | solution.py:321
  18.4 2.7 %collective-permute-start.7 = (f32[1,256]{1,0:T(1,128)S(1)}, f32[1,256]{1,0:T(1,128)S(1)}, u32[]{:S(2)}, u32[]{:S(2)}) collective-permute-start(f32[1,256]{1,0:T(1,128)S(1)} %add.12.s0), channel_id=1, source_target_pairs={{0,1},{1,0},{2,3},{3,2},{4,5},{5,4},{6,7},{7,6},{8,9},{9,8},{10,11... | collective-permute-start | bytes 3080 | tf_op jit(solution)/shard_map/ppermute | solution.py:328
  21.2 2.7 %collective-permute-start.8 = (f32[1,256]{1,0:T(1,128)S(1)}, f32[1,256]{1,0:T(1,128)S(1)}, u32[]{:S(2)}, u32[]{:S(2)}) collective-permute-start(f32[1,256]{1,0:T(1,128)S(1)} %add.13), channel_id=1, source_target_pairs={{0,2},{1,3},{2,0},{3,1},{4,6},{5,7},{6,4},{7,5},{8,10},{9,11},{10,... | collective-permute-start | bytes 3080 | tf_op jit(solution)/shard_map/ppermute | solution.py:329
  25.7 14.8 %collective-permute-start.19 = (bf16[128,2048]{1,0:T(8,128)(2,1)S(1)}, bf16[128,2048]{1,0:T(8,128)(2,1)S(1)}, u32[]{:S(2)}, u32[]{:S(2)}) collective-permute-start(bf16[128,2048]{1,0:T(8,128)(2,1)S(1)} %collective-permute-done.18.near_last.own), channel_id=1, source_target_pairs={{0,4},{4,0},{1,5},{5,1},{2,6},{6,2},{3,7},{7,3},{8,12},{12,8},{9,1... | collective-permute-start | bytes 1572872 | tf_op jit(solution)/shard_map/ppermute | solution.py:307
  28.2 15.4 %collective-permute-start.20 = (bf16[256,1024]{1,0:T(8,128)(2,1)S(1)}, bf16[256,1024]{1,0:T(8,128)(2,1)S(1)}, u32[]{:S(2)}, u32[]{:S(2)}) collective-permute-start(bf16[256,1024]{1,0:T(8,128)(2,1)S(1)} %shard_map.104), channel_id=1, source_target_pairs={{0,8},{8,16},{16,24},{1,9},{9,17},{17,25},{2,10},{10,18},{18,26},{... | collective-permute-start | bytes 1572872 | tf_op jit(solution)/shard_map/ppermute | solution.py:313
  30.8 17.4 %collective-permute-start.17 = (bf16[128,2048]{1,0:T(8,128)(2,1)S(1)}, bf16[128,2048]{1,0:T(8,128)(2,1)S(1)}, u32[]{:S(2)}, u32[]{:S(2)}) collective-permute-start(bf16[128,2048]{1,0:T(8,128)(2,1)S(1)} %collective-permute-done.16.near_first), channel_id=1, source_target_pairs={{0,4},{4,0},{1,5},{5,1},{2,6},{6,2},{3,7},{7,3},{8,12},{12,8},{9,1... | collective-permute-start | bytes 1572872 | tf_op jit(solution)/shard_map/ppermute | solution.py:307
  33.5 1.2 %collective-permute-start.10 = (f32[1,256]{1,0:T(1,128)S(1)}, f32[1,256]{1,0:T(1,128)S(1)}, u32[]{:S(2)}, u32[]{:S(2)}) collective-permute-start(f32[1,256]{1,0:T(1,128)S(1)} %get-tuple-element.52), channel_id=1, source_target_pairs={{0,4},{4,0},{1,5},{5,1},{2,6},{6,2},{3,7},{7,3},{8,12},{12,8},{9,1... | collective-permute-start | bytes 3080 | tf_op jit(solution)/shard_map/ppermute | solution.py:307
  34.8 2.7 %collective-permute-start.11 = (f32[1,256]{1,0:T(1,128)S(1)}, f32[1,256]{1,0:T(1,128)S(1)}, u32[]{:S(2)}, u32[]{:S(2)}) collective-permute-start(f32[1,256]{1,0:T(1,128)S(1)} %add.14.s0), channel_id=1, source_target_pairs={{0,1},{1,0},{2,3},{3,2},{4,5},{5,4},{6,7},{7,6},{8,9},{9,8},{10,11... | collective-permute-start | bytes 3080 | tf_op jit(solution)/shard_map/ppermute | solution.py:328
  37.5 2.7 %collective-permute-start.12 = (f32[1,256]{1,0:T(1,128)S(1)}, f32[1,256]{1,0:T(1,128)S(1)}, u32[]{:S(2)}, u32[]{:S(2)}) collective-permute-start(f32[1,256]{1,0:T(1,128)S(1)} %add.15), channel_id=1, source_target_pairs={{0,2},{1,3},{2,0},{3,1},{4,6},{5,7},{6,4},{7,5},{8,10},{9,11},{10,... | collective-permute-start | bytes 3080 | tf_op jit(solution)/shard_map/ppermute | solution.py:329
  44.1 9.3 %collective-permute-start.21 = (bf16[136,1024]{1,0:T(8,128)(2,1)S(1)}, bf16[136,1024]{1,0:T(8,128)(2,1)S(1)}, u32[]{:S(2)}, u32[]{:S(2)}) collective-permute-start(bf16[136,1024]{1,0:T(8,128)(2,1)S(1)} %shard_map.105), channel_id=1, source_target_pairs={{0,8},{8,16},{16,24},{1,9},{9,17},{17,25},{2,10},{10,18},{18,26},{... | collective-permute-start | bytes 835592 | tf_op jit(solution)/shard_map/ppermute | solution.py:313
  47.1 8.4 %collective-permute-start.13 = (bf16[128,1024]{1,0:T(8,128)(2,1)S(1)}, bf16[128,1024]{1,0:T(8,128)(2,1)S(1)}, u32[]{:S(2)}, u32[]{:S(2)}) collective-permute-start(bf16[128,1024]{1,0:T(8,128)(2,1)S(1)} %get-tuple-element.54), channel_id=1, source_target_pairs={{0,4},{4,0},{1,5},{5,1},{2,6},{6,2},{3,7},{7,3},{8,12},{12,8},{9,1... | collective-permute-start | bytes 786440 | tf_op jit(solution)/shard_map/ppermute | solution.py:307
  53.8 2.9 %collective-permute-start.22 = (bf16[128,1024]{1,0:T(8,128)(2,1)S(1)}, bf16[128,1024]{1,0:T(8,128)(2,1)S(1)}, u32[]{:S(2)}, u32[]{:S(2)}) collective-permute-start(bf16[128,1024]{1,0:T(8,128)(2,1)S(1)} %get-tuple-element.75), channel_id=1, source_target_pairs={{0,4},{4,0},{1,5},{5,1},{2,6},{6,2},{3,7},{7,3},{8,12},{12,8},{9,1... | collective-permute-start | bytes 786440 | tf_op jit(solution)/shard_map/ppermute | solution.py:307
  (7 other events, 13.9 us)
